TPU v7x, 128 devices: a whole 4x4x4 slice. The times are simulated.
128 devices in a mesh: frame: 16 (over x, z), head: 8 (over y, core).
Axes of the slice: x: 4, y: 4, z: 4, core: 2. Of those that a mesh axis runs over, the one named last changes fastest.
Arguments:
- queries: bfloat16 [10240, 5120], P('frame', 'head'), may hold values from -30 to 30
- key_rows: bfloat16 [10240, 5120], P('frame', 'head'), may hold values from -3 to 3
- value_rows: bfloat16 [10240, 5120], P('frame', 'head'), may hold values from -6 to 6
- out_weight: bfloat16 [5120, 5120], P('head'), may hold values from -2.390625 to 2.390625
- band_start: int32 [16, 16], replicated, may hold values from 0 to 4
- band_width: int32 [16], replicated, may hold values from 1 to 5, as said below
Outputs:
- attn_out: bfloat16 [10240, 5120], P('frame', 'head')
Inputs may be any that keep to these rules, and one draw needn't show every extreme that they name: band_width[0] is 5, band_width[1] is 2, every other entry lies in 1 to 2.
All inputs are finite; a program needn't handle non-finite values.
Results may differ from a plain program's by a relative error of at most 0.022.
Values may be sent and summed in bfloat16 or wider, within the bound.
No kernel may reach another device: no remote copies, remote signals or barrier semaphores. Data moves between devices by JAX's collectives and lax.ppermute only.
A program may use at most 128 MiB of HBM per device.

v0:
```python
import math

import jax
import jax.numpy as jnp
from jax import lax
from jax.sharding import PartitionSpec as P

HD = 128
BLOCK = 128


neg_large = -1e30


def lookup(small_table, index_array, length):
    onehot = index_array[:, None] == jnp.arange(length, dtype=jnp.int32)[None, :]
    return jnp.sum(jnp.where(onehot, small_table[None, :], 0), axis=1)


def absorb(running, query_heads, key_part, value_part, allowed):
    maxima, totals, weighted = running
    head_count = query_heads.shape[1]
    head_size = query_heads.shape[2]
    key_heads = key_part.reshape(key_part.shape[0], head_count, head_size)
    value_heads = value_part.reshape(value_part.shape[0], head_count, head_size)
    scores = jnp.einsum(
        "qhd,khd->hqk", query_heads, key_heads, preferred_element_type=jnp.float32
    ) * head_size ** (-0.5)
    scores = jnp.where(allowed[None, None, :], scores, neg_large)
    new_max = jnp.maximum(maxima, jnp.max(scores, axis=2))
    factor = jnp.exp(maxima - new_max)
    weights_now = jnp.where(allowed[None, None, :], jnp.exp(scores - new_max[:, :, None]), 0.0)
    totals = totals * factor + jnp.sum(weights_now, axis=2)
    mixed = jnp.einsum(
        "hqk,khd->hqd",
        weights_now.astype(jnp.bfloat16),
        value_heads,
        preferred_element_type=jnp.float32,
    )
    weighted = weighted * factor[:, :, None] + mixed
    return (new_max, totals, weighted)


def absorb_blocks(running, query_heads, key_part, value_part, allowed):
    length = key_part.shape[0]
    step_rows = math.gcd(length, 1280)
    turn_count = length // step_rows
    columns = key_part.shape[1]

    def advance(current, pieces):
        return (absorb(current, query_heads, pieces[0], pieces[1], pieces[2]), None)

    final_state, unused = lax.scan(
        advance,
        running,
        (
            key_part.reshape(turn_count, step_rows, columns),
            value_part.reshape(turn_count, step_rows, columns),
            allowed.reshape(turn_count, step_rows),
        ),
    )
    return final_state


def frame_mask(key_index, own_frame, band_start, band_width, frame_len, frames):
    key_frame = key_index // frame_len
    key_block = key_index % frame_len // BLOCK
    blocks = frame_len // BLOCK
    distance = jnp.abs(own_frame - key_frame)
    start_row = lax.dynamic_index_in_dim(band_start, own_frame, 0, keepdims=False)
    first_block = lookup(start_row, key_frame, frames)
    band_len = lookup(band_width, distance, frames)
    return (key_frame == own_frame) | (jnp.mod(key_block - first_block, blocks) < band_len)


def shards(queries, key_rows, value_rows, out_weight, band_start, band_width):
    frame_len, columns = queries.shape
    head_size = HD
    head_count = columns // head_size
    frames = lax.axis_size("frame")
    own_frame = lax.axis_index("frame")
    query_heads = queries.reshape(frame_len, head_count, head_size)
    running = (
        jnp.full((head_count, frame_len), neg_large, jnp.float32),
        jnp.zeros((head_count, frame_len), jnp.float32),
        jnp.zeros((head_count, frame_len, head_size), jnp.float32),
    )
    key_part = lax.all_gather(key_rows, "frame", axis=0, tiled=True)
    value_part = lax.all_gather(value_rows, "frame", axis=0, tiled=True)
    key_index = jnp.arange(key_part.shape[0], dtype=jnp.int32)
    allowed = frame_mask(key_index, own_frame, band_start, band_width, frame_len, frames)
    running = absorb_blocks(running, query_heads, key_part, value_part, allowed)
    maxima, totals, weighted = running
    attended = (weighted / totals[:, :, None]).astype(jnp.bfloat16)
    attended = attended.transpose(1, 0, 2).reshape(frame_len, columns)
    partial_value = jnp.dot(attended, out_weight, preferred_element_type=jnp.float32).astype(
        jnp.bfloat16
    )
    partial_value = lax.optimization_barrier(partial_value).astype(jnp.float32)
    return lax.psum_scatter(
        partial_value.astype(jnp.bfloat16), "head", scatter_dimension=1, tiled=True
    )


def solution(mesh):
    return jax.shard_map(
        shards,
        mesh=mesh,
        in_specs=(
            P("frame", "head"),
            P("frame", "head"),
            P("frame", "head"),
            P("head", None),
            P(),
            P(),
        ),
        out_specs=P("frame", "head"),
        check_vma=False,
    )
```

profile of v0, /device:TPU:32, one launch (start us, length us, event | category | flops | bytes accessed | tf_op | source)
XLA Modules:
  0.0 514.2 jit_solution(980484011006143013)
XLA Ops:
  12.8 91.3 %all-gather.3.cloned.1.call-done = bf16[10240,640]{1,0:T(8,128)(2,1)} async-done(((bf16[640,640]{1,0:T(8,128)(2,1)}), bf16[10240,640]{1,0:T(8,128)(2,1)}) %all-gather.3.cloned.1.call-update) | async-done | bytes 13107216 | tf_op jit(solution)/shard_map/all_gather | solution.py:88
  104.0 94.5 %all-gather.5.cloned.1.call-done = bf16[10240,640]{1,0:T(8,128)(2,1)} async-done(((bf16[640,640]{1,0:T(8,128)(2,1)}), bf16[10240,640]{1,0:T(8,128)(2,1)}) %all-gather.5.cloned.1.call-update) | async-done | bytes 13107216 | tf_op jit(solution)/shard_map/all_gather | solution.py:89
  198.5 242.0 %while.15 = (s32[]{:T(128)}, f32[5,640]{1,0:T(8,128)S(1)}, f32[5,640]{1,0:T(8,128)S(1)}, f32[5,640,128]{2,1,0:T(8,128)}, pred[8,1280]{1,0:T(8,128)(4,1)S(1)}, /*...) while((s32[]{:T(128)}, f32[5,640]{1,0:T(8,128)S(1)}, ...), condition=%wide.region_5.6_spmd.clone, body=%wide.region_2.5_spmd.clone.sunk | while | flops 2135260800 | bytes 141932992 | solution.py:53
  206.9 4.4 bitcast_reduce_fusion.2
  211.4 3.5 fusion.47
  217.4 11.0 %fusion.49 = f32[5,640,128]{2,1,0:T(8,128)} fusion(f32[5,640,128]{2,1,0:T(8,128)} %get-tuple-element.205, bf16[1280,5,128]{0,2,1:T(8,128)(2,1)S(1)} %bitcast.48, f32[5,1280,640]{2,1,0:T(8,128)} %copy-done.2, f32[5,640]{1,0:T(8,128)S(1)} %select_maximum_fusion.2, pred[1280]{0:T(1024)(128)(4,1)S(1)} %dynamic-slice_reduce_fusion.2, ...), kind=kOutput, calls=%fused_computation.13.clone.1 | convolution fusion | flops 1062092800 | bytes 21326080 | tf_op jit(solution)/shard_map/while/body/eval_jaxpr/hqk,khd->hqd/dot_general | solution.py:34
  236.8 4.4 bitcast_reduce_fusion.2
  241.3 3.5 fusion.47
  247.3 11.4 %fusion.49 = f32[5,640,128]{2,1,0:T(8,128)} fusion(f32[5,640,128]{2,1,0:T(8,128)} %get-tuple-element.205, bf16[1280,5,128]{0,2,1:T(8,128)(2,1)S(1)} %bitcast.48, f32[5,1280,640]{2,1,0:T(8,128)} %copy-done.2, f32[5,640]{1,0:T(8,128)S(1)} %select_maximum_fusion.2, pred[1280]{0:T(1024)(128)(4,1)S(1)} %dynamic-slice_reduce_fusion.2, ...), kind=kOutput, calls=%fused_computation.13.clone.1 | convolution fusion | flops 1062092800 | bytes 21326080 | tf_op jit(solution)/shard_map/while/body/eval_jaxpr/hqk,khd->hqd/dot_general | solution.py:34
  267.1 4.4 bitcast_reduce_fusion.2
  277.6 11.4 %fusion.49 = f32[5,640,128]{2,1,0:T(8,128)} fusion(f32[5,640,128]{2,1,0:T(8,128)} %get-tuple-element.205, bf16[1280,5,128]{0,2,1:T(8,128)(2,1)S(1)} %bitcast.48, f32[5,1280,640]{2,1,0:T(8,128)} %copy-done.2, f32[5,640]{1,0:T(8,128)S(1)} %select_maximum_fusion.2, pred[1280]{0:T(1024)(128)(4,1)S(1)} %dynamic-slice_reduce_fusion.2, ...), kind=kOutput, calls=%fused_computation.13.clone.1 | convolution fusion | flops 1062092800 | bytes 21326080 | tf_op jit(solution)/shard_map/while/body/eval_jaxpr/hqk,khd->hqd/dot_general | solution.py:34
  297.4 4.4 bitcast_reduce_fusion.2
  307.9 11.4 %fusion.49 = f32[5,640,128]{2,1,0:T(8,128)} fusion(f32[5,640,128]{2,1,0:T(8,128)} %get-tuple-element.205, bf16[1280,5,128]{0,2,1:T(8,128)(2,1)S(1)} %bitcast.48, f32[5,1280,640]{2,1,0:T(8,128)} %copy-done.2, f32[5,640]{1,0:T(8,128)S(1)} %select_maximum_fusion.2, pred[1280]{0:T(1024)(128)(4,1)S(1)} %dynamic-slice_reduce_fusion.2, ...), kind=kOutput, calls=%fused_computation.13.clone.1 | convolution fusion | flops 1062092800 | bytes 21326080 | tf_op jit(solution)/shard_map/while/body/eval_jaxpr/hqk,khd->hqd/dot_general | solution.py:34
  327.7 4.4 bitcast_reduce_fusion.2
  338.2 11.4 %fusion.49 = f32[5,640,128]{2,1,0:T(8,128)} fusion(f32[5,640,128]{2,1,0:T(8,128)} %get-tuple-element.205, bf16[1280,5,128]{0,2,1:T(8,128)(2,1)S(1)} %bitcast.48, f32[5,1280,640]{2,1,0:T(8,128)} %copy-done.2, f32[5,640]{1,0:T(8,128)S(1)} %select_maximum_fusion.2, pred[1280]{0:T(1024)(128)(4,1)S(1)} %dynamic-slice_reduce_fusion.2, ...), kind=kOutput, calls=%fused_computation.13.clone.1 | convolution fusion | flops 1062092800 | bytes 21326080 | tf_op jit(solution)/shard_map/while/body/eval_jaxpr/hqk,khd->hqd/dot_general | solution.py:34
  358.0 4.4 bitcast_reduce_fusion.2
  368.5 11.4 %fusion.49 = f32[5,640,128]{2,1,0:T(8,128)} fusion(f32[5,640,128]{2,1,0:T(8,128)} %get-tuple-element.205, bf16[1280,5,128]{0,2,1:T(8,128)(2,1)S(1)} %bitcast.48, f32[5,1280,640]{2,1,0:T(8,128)} %copy-done.2, f32[5,640]{1,0:T(8,128)S(1)} %select_maximum_fusion.2, pred[1280]{0:T(1024)(128)(4,1)S(1)} %dynamic-slice_reduce_fusion.2, ...), kind=kOutput, calls=%fused_computation.13.clone.1 | convolution fusion | flops 1062092800 | bytes 21326080 | tf_op jit(solution)/shard_map/while/body/eval_jaxpr/hqk,khd->hqd/dot_general | solution.py:34
  388.3 4.4 bitcast_reduce_fusion.2
  398.8 11.4 %fusion.49 = f32[5,640,128]{2,1,0:T(8,128)} fusion(f32[5,640,128]{2,1,0:T(8,128)} %get-tuple-element.205, bf16[1280,5,128]{0,2,1:T(8,128)(2,1)S(1)} %bitcast.48, f32[5,1280,640]{2,1,0:T(8,128)} %copy-done.2, f32[5,640]{1,0:T(8,128)S(1)} %select_maximum_fusion.2, pred[1280]{0:T(1024)(128)(4,1)S(1)} %dynamic-slice_reduce_fusion.2, ...), kind=kOutput, calls=%fused_computation.13.clone.1 | convolution fusion | flops 1062092800 | bytes 21326080 | tf_op jit(solution)/shard_map/while/body/eval_jaxpr/hqk,khd->hqd/dot_general | solution.py:34
  418.6 4.4 bitcast_reduce_fusion.2
  429.1 11.4 %fusion.49 = f32[5,640,128]{2,1,0:T(8,128)} fusion(f32[5,640,128]{2,1,0:T(8,128)} %get-tuple-element.205, bf16[1280,5,128]{0,2,1:T(8,128)(2,1)S(1)} %bitcast.48, f32[5,1280,640]{2,1,0:T(8,128)} %copy-done.2, f32[5,640]{1,0:T(8,128)S(1)} %select_maximum_fusion.2, pred[1280]{0:T(1024)(128)(4,1)S(1)} %dynamic-slice_reduce_fusion.2, ...), kind=kOutput, calls=%fused_computation.13.clone.1 | convolution fusion | flops 1062092800 | bytes 21326080 | tf_op jit(solution)/shard_map/while/body/eval_jaxpr/hqk,khd->hqd/dot_general | solution.py:34
  442.8 9.5 %convolution_convert_fusion = bf16[640,5120]{1,0:T(8,128)(2,1)} fusion(bf16[640,640]{0,1:T(8,128)(2,1)S(1)} %bitcast.54, bf16[640,5120]{1,0:T(8,128)(2,1)} %param.11), kind=kOutput, calls=%fused_computation.22 | convolution fusion | flops 4197580800 | bytes 13926400 | tf_op jit(solution)/shard_map/dot_general | solution.py:96
  452.2 9.5 %copy.41 = bf16[640,5120]{0,1:T(8,128)(2,1)} copy(bf16[640,5120]{1,0:T(8,128)(2,1)} %convolution_convert_fusion) | data formatting | bytes 13107200
  461.8 43.7 %reduce-scatter.4.cloned.1.call-done = bf16[640,640]{1,0:T(8,128)(2,1)} async-done(((bf16[5120,640]{1,0:T(8,128)(2,1)}), bf16[640,640]{1,0:T(8,128)(2,1)}) %reduce-scatter.4.cloned.1.call-update) | async-done | bytes 819216
  (120 shorter events, 118.4 us)
Async XLA Ops:
  6.5 2.5 copy-start
  6.5 97.5 %all-gather.3.cloned.1.call-start = ((), (), s32[]{:S(2)}) async-start(), calls=%async_computation.1 | async-start | bytes 13926400 | tf_op jit(solution)/shard_map/all_gather | solution.py:88
  7.3 191.3 %all-gather.5.cloned.1.call-start = ((), (), s32[]{:S(2)}) async-start(), calls=%async_computation.2 | async-start | bytes 13926400 | tf_op jit(solution)/shard_map/all_gather | solution.py:89
  8.0 497.5 %reduce-scatter.4.cloned.1.call-start = ((), (), s32[]{:S(2)}) async-start(), calls=%async_computation.3 | async-start | bytes 7372800
  211.4 6.0 %copy-start.2 = (f32[5,1280,640]{2,1,0:T(8,128)}, f32[5,1280,640]{2,1,0:T(8,128)S(1)}, u32[]{:S(2)}) copy-start(f32[5,1280,640]{2,1,0:T(8,128)S(1)} %get-tuple-element.188) | copy-start | bytes 49152004 | tf_op jit(solution)/shard_map/while
  211.4 6.0 %copy-start.3 = (bf16[1,1280,640]{1,2,0:T(8,128)(2,1)S(1)}, bf16[1,1280,640]{1,2,0:T(8,128)(2,1)}, u32[]{:S(2)}) copy-start(bf16[1,1280,640]{1,2,0:T(8,128)(2,1)} %copy.48) | copy-start | bytes 4915204 | tf_op jit(solution)/shard_map/while
  241.2 6.0 %copy-start.2 = (f32[5,1280,640]{2,1,0:T(8,128)}, f32[5,1280,640]{2,1,0:T(8,128)S(1)}, u32[]{:S(2)}) copy-start(f32[5,1280,640]{2,1,0:T(8,128)S(1)} %get-tuple-element.188) | copy-start | bytes 49152004 | tf_op jit(solution)/shard_map/while
  241.3 6.0 %copy-start.3 = (bf16[1,1280,640]{1,2,0:T(8,128)(2,1)S(1)}, bf16[1,1280,640]{1,2,0:T(8,128)(2,1)}, u32[]{:S(2)}) copy-start(bf16[1,1280,640]{1,2,0:T(8,128)(2,1)} %copy.48) | copy-start | bytes 4915204 | tf_op jit(solution)/shard_map/while
  271.5 6.0 %copy-start.2 = (f32[5,1280,640]{2,1,0:T(8,128)}, f32[5,1280,640]{2,1,0:T(8,128)S(1)}, u32[]{:S(2)}) copy-start(f32[5,1280,640]{2,1,0:T(8,128)S(1)} %get-tuple-element.188) | copy-start | bytes 49152004 | tf_op jit(solution)/shard_map/while
  271.6 6.0 %copy-start.3 = (bf16[1,1280,640]{1,2,0:T(8,128)(2,1)S(1)}, bf16[1,1280,640]{1,2,0:T(8,128)(2,1)}, u32[]{:S(2)}) copy-start(bf16[1,1280,640]{1,2,0:T(8,128)(2,1)} %copy.48) | copy-start | bytes 4915204 | tf_op jit(solution)/shard_map/while
  301.8 6.0 %copy-start.2 = (f32[5,1280,640]{2,1,0:T(8,128)}, f32[5,1280,640]{2,1,0:T(8,128)S(1)}, u32[]{:S(2)}) copy-start(f32[5,1280,640]{2,1,0:T(8,128)S(1)} %get-tuple-element.188) | copy-start | bytes 49152004 | tf_op jit(solution)/shard_map/while
  301.9 6.0 %copy-start.3 = (bf16[1,1280,640]{1,2,0:T(8,128)(2,1)S(1)}, bf16[1,1280,640]{1,2,0:T(8,128)(2,1)}, u32[]{:S(2)}) copy-start(bf16[1,1280,640]{1,2,0:T(8,128)(2,1)} %copy.48) | copy-start | bytes 4915204 | tf_op jit(solution)/shard_map/while
  332.1 6.0 %copy-start.2 = (f32[5,1280,640]{2,1,0:T(8,128)}, f32[5,1280,640]{2,1,0:T(8,128)S(1)}, u32[]{:S(2)}) copy-start(f32[5,1280,640]{2,1,0:T(8,128)S(1)} %get-tuple-element.188) | copy-start | bytes 49152004 | tf_op jit(solution)/shard_map/while
  332.2 6.0 %copy-start.3 = (bf16[1,1280,640]{1,2,0:T(8,128)(2,1)S(1)}, bf16[1,1280,640]{1,2,0:T(8,128)(2,1)}, u32[]{:S(2)}) copy-start(bf16[1,1280,640]{1,2,0:T(8,128)(2,1)} %copy.48) | copy-start | bytes 4915204 | tf_op jit(solution)/shard_map/while
  362.4 6.0 %copy-start.2 = (f32[5,1280,640]{2,1,0:T(8,128)}, f32[5,1280,640]{2,1,0:T(8,128)S(1)}, u32[]{:S(2)}) copy-start(f32[5,1280,640]{2,1,0:T(8,128)S(1)} %get-tuple-element.188) | copy-start | bytes 49152004 | tf_op jit(solution)/shard_map/while
  362.5 6.0 %copy-start.3 = (bf16[1,1280,640]{1,2,0:T(8,128)(2,1)S(1)}, bf16[1,1280,640]{1,2,0:T(8,128)(2,1)}, u32[]{:S(2)}) copy-start(bf16[1,1280,640]{1,2,0:T(8,128)(2,1)} %copy.48) | copy-start | bytes 4915204 | tf_op jit(solution)/shard_map/while
  392.7 6.0 %copy-start.2 = (f32[5,1280,640]{2,1,0:T(8,128)}, f32[5,1280,640]{2,1,0:T(8,128)S(1)}, u32[]{:S(2)}) copy-start(f32[5,1280,640]{2,1,0:T(8,128)S(1)} %get-tuple-element.188) | copy-start | bytes 49152004 | tf_op jit(solution)/shard_map/while
  392.8 6.0 %copy-start.3 = (bf16[1,1280,640]{1,2,0:T(8,128)(2,1)S(1)}, bf16[1,1280,640]{1,2,0:T(8,128)(2,1)}, u32[]{:S(2)}) copy-start(bf16[1,1280,640]{1,2,0:T(8,128)(2,1)} %copy.48) | copy-start | bytes 4915204 | tf_op jit(solution)/shard_map/while
  423.0 6.0 %copy-start.2 = (f32[5,1280,640]{2,1,0:T(8,128)}, f32[5,1280,640]{2,1,0:T(8,128)S(1)}, u32[]{:S(2)}) copy-start(f32[5,1280,640]{2,1,0:T(8,128)S(1)} %get-tuple-element.188) | copy-start | bytes 49152004 | tf_op jit(solution)/shard_map/while
  423.0 6.0 %copy-start.3 = (bf16[1,1280,640]{1,2,0:T(8,128)(2,1)S(1)}, bf16[1,1280,640]{1,2,0:T(8,128)(2,1)}, u32[]{:S(2)}) copy-start(bf16[1,1280,640]{1,2,0:T(8,128)(2,1)} %copy.48) | copy-start | bytes 4915204 | tf_op jit(solution)/shard_map/while
  452.2 55.4 %copy-start.1 = (s32[16,16]{1,0:T(8,128)S(1)}, s32[16,16]{1,0:T(8,128)}, u32[]{:S(2)}) copy-start(s32[16,16]{1,0:T(8,128)} %param.12) | copy-start | bytes 3076
Sparse Core Ops, SparseCore 0:
  9.5 94.4 all-gather.2
  106.2 92.2 all-gather.4
  461.9 43.5 reduce-scatter.3
where the time goes:
time: 516 us; the launch traced here: 514 us
  waiting for transfers between devices  231 us (45%)
  matrix products  136 us (26%)
  local copies, waits for them, and re-layouts  104 us (20%)
  other arithmetic  29.2 us (6%)
  between operations  13.2 us (3%)
    all_gather x1, waiting for transfers between devices, shards(): value_part = lax.all_gather(value_rows, 'frame', axis=0, tiled=True)  94.5 us
    all_gather x1, waiting for transfers between devices, shards(): key_part = lax.all_gather(key_rows, 'frame', axis=0, tiled=True)  91.3 us
    dot_general x8, matrix products, absorb(): jnp.einsum('hqk,khd->hqd', weights_now.astype(jnp.bfloat16), value_heads,...  91.1 us
    dynamic_slice x32, local copies, waits for them, and re-layouts, absorb_blocks(): lax.scan(advance, running, (key_part.reshape(turn_count, step_rows, colum...  66.8 us
    unnamed x4, waiting for transfers between devices  45.1 us
    dot_general x8, matrix products, absorb(): jnp.einsum('qhd,khd->hqk', query_heads, key_heads, preferred_element_type...  35.6 us
    reduce_sum x8, other arithmetic, absorb(): totals = totals * factor + jnp.sum(weights_now, axis=2)  27.7 us
    while x40, local copies, waits for them, and re-layouts  20.2 us
  transfers between devices with their start and end apart: 3, of which 3 were waited for; matrix products, arithmetic and copies ran while one was open for 1% of the time, Pallas kernels for 0%

commit v1 on v0

v1 whole, which is shorter than its diff:
```python
import functools

import jax
import jax.numpy as jnp
from jax import lax
from jax.experimental import pallas as pl
from jax.experimental.pallas import tpu as pltpu
from jax.sharding import PartitionSpec as P

HD = 128
BLOCK = 128
NB = 5
FT = 640
FRAMES = 16
SIDE = 4
CHUNK = 16
ROWS = 128
LOG2_SCALE = 1.4426950408889634 / HD**0.5
NT = (((1,), (1,)), ((), ()))
NN = (((1,), (0,)), ((), ()))
BOTH = ("frame", "head")


def pairs(move):
    out = []
    for i in range(128):
        frame, head = divmod(i, 8)
        x, z, y, c = move(*divmod(frame, 4), *divmod(head, 2))
        out.append((i, (x % 4 * 4 + z % 4) * 8 + y % 4 * 2 + c))
    return out


def line_shift(v, s):
    return lax.ppermute(v, BOTH, pairs(lambda x, z, y, c: (x, z + s, y, c) if c == 0 else (x + s, z, y, c)))


def cross_shift(v, s):
    return lax.ppermute(v, BOTH, pairs(lambda x, z, y, c: (x + s, z, y, c) if c == 0 else (x, z + s, y, c)))


def y_shift(v, s):
    return lax.ppermute(v, BOTH, pairs(lambda x, z, y, c: (x, z, y + s, c)))


def core_swap(v):
    return lax.ppermute(v, BOTH, pairs(lambda x, z, y, c: (x, z, y, 1 - c)))


def attend_kernel(qid, kid, bs, bw, q_ref, g0, g1, g2, g3, o_ref, kc, vc, acc, mx):
    a = qid[pl.program_id(0)]

    def place(n):
        return pl.ds(pl.multiple_of(n * BLOCK, BLOCK), BLOCK)

    n = 0
    for d, group in enumerate((g0, g1, g2, g3)):

        def pack(s, n, d=d, group=group):
            b = kid[d * SIDE + s]
            own = a == b
            start = jnp.where(own, 0, bs[a * FRAMES + b])
            width = jnp.where(own, NB, bw[jnp.abs(a - b)])

            def one(t, n):
                at = start + t
                rows = place(jnp.where(at >= NB, at - NB, at))
                kc[place(n), :] = group[s, 0, rows, :]
                vc[place(n), 0:HD] = group[s, 1, rows, :]
                vc[place(n), HD:] = (lax.broadcasted_iota(jnp.int32, (BLOCK, HD), 1) == 0).astype(jnp.bfloat16)
                return n + 1

            return lax.fori_loop(0, width, one, n)

        n = lax.fori_loop(0, SIDE, pack, n)
    steps = (n + CHUNK - 1) // CHUNK

    def fill(j, carry):
        kc[place(j), :] = kc[0:BLOCK, :]
        vc[place(j), :] = jnp.zeros((BLOCK, 2 * HD), jnp.bfloat16)
        return carry

    lax.fori_loop(n, steps * CHUNK, fill, 0)
    acc[...] = jnp.zeros_like(acc)
    mx[...] = jnp.full_like(mx, -1e30)

    def step(j, carry):
        keys = pl.ds(pl.multiple_of(j * CHUNK * BLOCK, CHUNK * BLOCK), CHUNK * BLOCK)
        kk, vv = kc[keys, :], vc[keys, :]
        for r in range(FT // ROWS):
            rows = slice(r * ROWS, (r + 1) * ROWS)
            scores = lax.dot_general(q_ref[0, rows, :], kk, NT, preferred_element_type=jnp.float32)
            old = mx[rows, :]
            new = jnp.maximum(old, jnp.max(scores, axis=1, keepdims=True))
            mx[rows, :] = new
            top = new * LOG2_SCALE
            probs = jnp.exp2(scores * LOG2_SCALE - top[:, 0:1]).astype(jnp.bfloat16)
            factor = jnp.exp2(old * LOG2_SCALE - top)
            acc[rows, :] = acc[rows, :] * factor[:, 0:1] + lax.dot_general(
                probs, vv, NN, preferred_element_type=jnp.float32
            )
        return carry

    lax.fori_loop(0, steps, step, 0)
    o_ref[0] = (acc[:, 0:HD] / acc[:, HD : HD + 1]).astype(jnp.bfloat16)


def attend(qid, kid, bs, bw, q, groups):
    items = q.shape[0]
    most = -(-(NB + 2 * (FRAMES - 1)) // CHUNK) * CHUNK * BLOCK
    whole = pl.BlockSpec((SIDE, 2, FT, HD), lambda i, *_: (0, 0, 0, 0))
    item = pl.BlockSpec((1, FT, HD), lambda i, *_: (i, 0, 0))
    return pl.pallas_call(
        attend_kernel,
        grid_spec=pltpu.PrefetchScalarGridSpec(
            num_scalar_prefetch=4,
            grid=(items,),
            in_specs=[item] + [whole] * 4,
            out_specs=item,
            scratch_shapes=[
                pltpu.VMEM((most, HD), jnp.bfloat16),
                pltpu.VMEM((most, 2 * HD), jnp.bfloat16),
                pltpu.VMEM((FT, 2 * HD), jnp.float32),
                pltpu.VMEM((FT, HD), jnp.float32),
            ],
        ),
        out_shape=jax.ShapeDtypeStruct((items, FT, HD), jnp.bfloat16),
        compiler_params=pltpu.CompilerParams(vmem_limit_bytes=48 << 20),
        cost_estimate=pl.CostEstimate(
            flops=items * 4 * FT * HD * 28 * BLOCK, bytes_accessed=6 << 20, transcendentals=items * FT * 28 * BLOCK
        ),
        name="attend",
    )(qid, kid, bs, bw, q, *groups)


def project_kernel(order, pos, o0, o1, o2, o3, o4, w_ref, y_ref, att):
    @pl.when(pl.program_id(0) == 0)
    def _():
        for s, o in enumerate((o0, o1, o2, o3)):
            head = lax.rem(pos[0] + s, SIDE)
            att[:, pl.ds(pl.multiple_of(head * HD, HD), HD)] = o[...]
        att[:, 4 * HD :] = o4[...]

    y_ref[0] = jnp.dot(att[...], w_ref[...], preferred_element_type=jnp.float32).astype(jnp.bfloat16)


def project(order, pos, outs, weight):
    count = order.shape[0]
    width = weight.shape[1] // 8
    whole = pl.BlockSpec((FT, HD), lambda i, *_: (0, 0))
    return pl.pallas_call(
        project_kernel,
        grid_spec=pltpu.PrefetchScalarGridSpec(
            num_scalar_prefetch=2,
            grid=(count,),
            in_specs=[whole] * 5 + [pl.BlockSpec((5 * HD, width), lambda i, order, pos: (0, order[i]))],
            out_specs=pl.BlockSpec((1, FT, width), lambda i, *_: (i, 0, 0)),
            scratch_shapes=[pltpu.VMEM((FT, 5 * HD), jnp.bfloat16)],
        ),
        out_shape=jax.ShapeDtypeStruct((count, FT, width), jnp.bfloat16),
        compiler_params=pltpu.CompilerParams(vmem_limit_bytes=48 << 20),
        cost_estimate=pl.CostEstimate(
            flops=2 * count * FT * 5 * HD * width, bytes_accessed=count * 2 * FT * width * 2, transcendentals=0
        ),
        name="project",
    )(order, pos, *outs, weight)


def add(*terms):
    total = terms[0].astype(jnp.float32)
    for t in terms[1:]:
        total = total + t.astype(jnp.float32)
    return total.astype(jnp.bfloat16)


def shards(queries, key_rows, value_rows, out_weight, band_start, band_width):
    frame, head = lax.axis_index("frame"), lax.axis_index("head")
    x, z = frame // SIDE, frame % SIDE
    y, core = head // 2, head % 2
    line = jnp.where(core == 0, z, x)
    ring = jnp.arange(SIDE, dtype=jnp.int32)
    line_frames = jnp.where(core == 0, x * SIDE + (z - ring) % SIDE, (x - ring) % SIDE * SIDE + z)
    back, slot = ring[:, None], ring[None, :]
    all_frames = jnp.where(
        core == 0,
        (x - back) % SIDE * SIDE + (z - slot) % SIDE,
        (x - slot) % SIDE * SIDE + (z - back) % SIDE,
    ).reshape(-1)
    bs, bw = band_start.reshape(-1), band_width

    def columns(v, h):
        return lax.dynamic_slice_in_dim(v, h * HD, HD, 1)

    k4, v4 = key_rows[:, 4 * HD :], value_rows[:, 4 * HD :]
    got = []
    for s in range(SIDE):
        h = (line + s) % SIDE
        piece = jnp.stack([columns(queries, h), columns(key_rows, h), columns(value_rows, h), k4, v4])
        got.append(piece if s == 0 else line_shift(piece, s))
    q_main = jnp.stack([g[0] for g in got])
    main = [jnp.stack([g[1:3] for g in got])]
    last = [jnp.stack([g[3:5] for g in got])]

    main_1, main_3 = cross_shift(main[0], 1), cross_shift(main[0], 3)
    last_1, last_3 = cross_shift(last[0], 1), cross_shift(last[0], 3)
    main += [main_1, cross_shift(main_1, 1), main_3]
    last += [last_1, cross_shift(last_3, 3), last_3]

    o_main = attend(line_frames, all_frames, bs, bw, q_main, main)
    o_last = attend(frame[None], all_frames, bs, bw, queries[None, :, 4 * HD :], last)

    outs = [o_main[0]] + [line_shift(o_main[s], SIDE - s) for s in range(1, SIDE)] + [o_last[0]]

    far = (y + jnp.array([2, 1, 3, 0], jnp.int32)) % SIDE * 2
    given = core_swap(project(far + 1 - core, line[None], outs, out_weight))
    kept = project(far + core, line[None], outs, out_weight)
    two, up, down, own = [add(kept[i], given[i]) for i in range(4)]
    half = FT // 2
    from_down, from_up = y_shift(two[:half], 1), y_shift(two[half:], 3)
    up = jnp.concatenate([add(up[:half], from_down), up[half:]])
    down = jnp.concatenate([down[:half], add(down[half:], from_up)])
    return add(own, y_shift(up, 1), y_shift(down, 3))


def solution(mesh):
    return jax.shard_map(
        shards,
        mesh=mesh,
        in_specs=(
            P("frame", "head"),
            P("frame", "head"),
            P("frame", "head"),
            P("head", None),
            P(),
            P(),
        ),
        out_specs=P("frame", "head"),
        check_vma=False,
    )
```

time: 516 us -> 159 us (0.31)
  waiting for transfers between devices: 231 us -> 74.9 us
  matrix products: 136 us -> 0 us
  local copies, waits for them, and re-layouts: 104 us -> 9.93 us
  Pallas kernels: 0 us -> 43.8 us
  starting transfers between devices: 0.08 us -> 26.9 us
  other arithmetic: 29.2 us -> 2.9 us
  between operations: 13.2 us -> 0.24 us
    all_gather x2 -> x0, waiting for transfers between devices: 186 us -> none  [the longest x1 94.5 us: shards(): value_part = lax.all_gather(value_rows, 'frame', axis=0, tiled=True)]
    dot_general x17 -> x0, matrix products: 136 us -> none  [the longest x8 91.1 us: absorb(): jnp.einsum('hqk,khd->hqd', weights_now.astype(jnp.bfloat16), value_heads,...]
    ppermute x0 -> x17, waiting for transfers between devices: none -> 74.9 us  [the longest x4 30 us: y_shift(): return lax.ppermute(v, BOTH, pairs(lambda x, z, y, c: (x, z, y + s, c)))]
    dynamic_slice x32 -> x0, local copies, waits for them, and re-layouts: 66.8 us -> none  [absorb_blocks(): lax.scan(advance, running, (key_part.reshape(turn_count, step_rows, colum...]
    unnamed x4 -> x0, waiting for transfers between devices: 45.1 us -> none
    pallas_call x0 -> x4, Pallas kernels: none -> 43.8 us  [the longest x2 32.2 us: attend(): pl.pallas_call(attend_kernel, grid_spec=pltpu.PrefetchScalarGridSpec(num_...]
    reduce_sum x10 -> x0, other arithmetic: 28.8 us -> none  [the longest x8 27.7 us: absorb(): totals = totals * factor + jnp.sum(weights_now, axis=2)]
    ppermute x0 -> x17, starting transfers between devices: none -> 26.9 us  [the longest x6 11.2 us: line_shift(): lax.ppermute(v, BOTH, pairs(lambda x, z, y, c: (x, z + s, y, c) if c == 0...]
  transfers between devices with their start and end apart: 3 -> 17, of which waited for: 3 -> 9; matrix products, arithmetic and copies ran while one was open for 1% -> 2% of each run, Pallas kernels for 0% -> 24%
where the time goes in v1:
time: 159 us
  waiting for transfers between devices  74.9 us (47%)
  Pallas kernels  43.8 us (28%)
  starting transfers between devices  26.9 us (17%)
  local copies, waits for them, and re-layouts  9.93 us (6%)
  other arithmetic  2.9 us (2%)
    pallas_call x2, Pallas kernels, attend(): pl.pallas_call(attend_kernel, grid_spec=pltpu.PrefetchScalarGridSpec(num_...  32.2 us
    ppermute x4, waiting for transfers between devices, y_shift(): return lax.ppermute(v, BOTH, pairs(lambda x, z, y, c: (x, z, y + s, c)))  30 us
    ppermute x6, waiting for transfers between devices, cross_shift(): lax.ppermute(v, BOTH, pairs(lambda x, z, y, c: (x + s, z, y, c) if c == 0...  27 us
    ppermute x6, waiting for transfers between devices, line_shift(): lax.ppermute(v, BOTH, pairs(lambda x, z, y, c: (x, z + s, y, c) if c == 0...  17.8 us
    pallas_call x2, Pallas kernels, project(): pl.pallas_call(project_kernel, grid_spec=pltpu.PrefetchScalarGridSpec(num...  11.6 us
    ppermute x6, starting transfers between devices, line_shift(): lax.ppermute(v, BOTH, pairs(lambda x, z, y, c: (x, z + s, y, c) if c == 0...  11.2 us
    ppermute x6, starting transfers between devices, cross_shift(): lax.ppermute(v, BOTH, pairs(lambda x, z, y, c: (x + s, z, y, c) if c == 0...  8.45 us
    ppermute x4, starting transfers between devices, y_shift(): return lax.ppermute(v, BOTH, pairs(lambda x, z, y, c: (x, z, y + s, c)))  6.92 us
  transfers between devices with their start and end apart: 17, of which 9 were waited for; matrix products, arithmetic and copies ran while one was open for 2% of the time, Pallas kernels for 24%

profile of v1, /device:TPU:32, one launch (start us, length us, event | category | flops | bytes accessed | tf_op | source)
XLA Modules:
  0.0 158.7 jit_solution(5554970688700021240)
XLA Ops:
  0.0 2.0 %bitcast_dynamic-update-slice_fusion.8 = (bf16[5,640,128]{2,1,0:T(8,128)(2,1)}, bf16[5,640,128]{2,1,0:T(8,128)(2,1)}, bf16[5,640,128]{2,1,0:T(8,128)(2,1)}) fusion(bf16[640,640]{1,0:T(8,128)(2,1)} %param.7, s32[]{:T(128)S(6)} %select_n.139, s32[]{:T(128)S(6)} %select_n.141, s32[]{:T(128)S(6)} %select_n.143), kind=kLoop, calls=%fused_computation.43 | loop fusion | bytes 983052
  2.0 1.9 %bitcast_dynamic-update-slice_fusion.7 = (bf16[5,640,128]{2,1,0:T(8,128)(2,1)}, bf16[5,640,128]{2,1,0:T(8,128)(2,1)}, bf16[5,640,128]{2,1,0:T(8,128)(2,1)}) fusion(bf16[5,640,128]{2,1,0:T(8,128)(2,1)} %get-tuple-element.36, bf16[640,640]{1,0:T(8,128)(2,1)} %param.8, s32[]{:T(128)S(6)} %select_n.139, bf16[5,640,128]{2,1,0:T(8,128)(2,1)} %get-tuple-element.37, ...), kind=kLoop, calls=%fused_computation.42 | loop fusion | bytes 983052
  6.3 3.4 %collective-permute-start.1 = (bf16[5,640,128]{2,1,0:T(8,128)(2,1)}, bf16[5,640,128]{2,1,0:T(8,128)(2,1)S(1)}, u32[]{:S(2)}, u32[]{:S(2)}) collective-permute-start(bf16[5,640,128]{2,1,0:T(8,128)(2,1)} %get-tuple-element.25), channel_id=1, source_target_pairs={{0,16},{1,65},{2,18},{3,67},{4,20},{5,69},{6,22},{7,71},{8,24},{9,... | collective-permute-start | bytes 2457608 | tf_op jit(solution)/shard_map/ppermute | solution.py:34
  9.7 2.2 %collective-permute-start = (bf16[5,640,128]{2,1,0:T(8,128)(2,1)}, bf16[5,640,128]{2,1,0:T(8,128)(2,1)}, u32[]{:S(2)}, u32[]{:S(2)}) collective-permute-start(bf16[5,640,128]{2,1,0:T(8,128)(2,1)} %get-tuple-element.24), channel_id=1, source_target_pairs={{0,8},{1,33},{2,10},{3,35},{4,12},{5,37},{6,14},{7,39},{8,16},{9,4... | collective-permute-start | bytes 2457608 | tf_op jit(solution)/shard_map/ppermute | solution.py:34
  12.0 6.8 %collective-permute-done.2 = bf16[5,640,128]{2,1,0:T(8,128)(2,1)S(1)} collective-permute-done((bf16[5,640,128]{2,1,0:T(8,128)(2,1)}, bf16[5,640,128]{2,1,0:T(8,128)(2,1)S(1)}, u32[]{:S(2)}, u32[]{:S(2)}) %collective-permute-start.2) | collective-permute-done | bytes 819232 | tf_op jit(solution)/shard_map/ppermute | solution.py:34
  18.9 10.1 %collective-permute-done.1 = bf16[5,640,128]{2,1,0:T(8,128)(2,1)S(1)} collective-permute-done((bf16[5,640,128]{2,1,0:T(8,128)(2,1)}, bf16[5,640,128]{2,1,0:T(8,128)(2,1)S(1)}, u32[]{:S(2)}, u32[]{:S(2)}) %collective-permute-start.1) | collective-permute-done | bytes 819232 | tf_op jit(solution)/shard_map/ppermute | solution.py:34
  31.2 1.6 collective-permute-start.3
  33.0 1.8 %collective-permute-start.10 = (bf16[4,2,640,128]{3,2,1,0:T(8,128)(2,1)S(1)}, bf16[4,2,640,128]{3,2,1,0:T(8,128)(2,1)}, u32[]{:S(2)}, u32[]{:S(2)}) collective-permute-start(bf16[4,2,640,128]{3,2,1,0:T(8,128)(2,1)S(1)} %pad_maximum_fusion.1.g0), channel_id=1, source_target_pairs={{0,96},{1,25},{2,98},{3,27},{4,100},{5,29},{6,102},{7,31},{8,104},... | collective-permute-start | bytes 3932168 | tf_op jit(solution)/shard_map/ppermute | solution.py:38
  34.8 1.5 collective-permute-start.5
  36.3 13.8 %collective-permute-done.3.g1 = bf16[4,2,640,128]{3,2,1,0:T(8,128)(2,1)} collective-permute-done((bf16[4,2,640,128]{3,2,1,0:T(8,128)(2,1)S(1)}, bf16[4,2,640,128]{3,2,1,0:T(8,128)(2,1)}, u32[]{:S(2)}, u32[]{:S(2)}) %collective-permute-start.3) | collective-permute-done | bytes 1310752 | tf_op jit(solution)/shard_map/ppermute | solution.py:38
  52.1 1.7 %collective-permute-start.11 = (bf16[4,2,640,128]{3,2,1,0:T(8,128)(2,1)}, bf16[4,2,640,128]{3,2,1,0:T(8,128)(2,1)}, u32[]{:S(2)}, u32[]{:S(2)}) collective-permute-start(bf16[4,2,640,128]{3,2,1,0:T(8,128)(2,1)} %collective-permute-done.10.g3), channel_id=1, source_target_pairs={{0,96},{1,25},{2,98},{3,27},{4,100},{5,29},{6,102},{7,31},{8,104},... | collective-permute-start | bytes 3932168 | tf_op jit(solution)/shard_map/ppermute | solution.py:38
  56.1 8.7 %collective-permute-done.5.g3 = bf16[4,2,640,128]{3,2,1,0:T(8,128)(2,1)} collective-permute-done((bf16[4,2,640,128]{3,2,1,0:T(8,128)(2,1)S(1)}, bf16[4,2,640,128]{3,2,1,0:T(8,128)(2,1)}, u32[]{:S(2)}, u32[]{:S(2)}) %collective-permute-start.5) | collective-permute-done | bytes 1310752 | tf_op jit(solution)/shard_map/ppermute | solution.py:38
  64.8 4.5 %collective-permute-done.4.g2 = bf16[4,2,640,128]{3,2,1,0:T(8,128)(2,1)} collective-permute-done((bf16[4,2,640,128]{3,2,1,0:T(8,128)(2,1)}, bf16[4,2,640,128]{3,2,1,0:T(8,128)(2,1)}, u32[]{:S(2)}, u32[]{:S(2)}) %collective-permute-start.4) | collective-permute-done | bytes 1310752 | tf_op jit(solution)/shard_map/ppermute | solution.py:38
  69.3 24.2 %attend.2 = bf16[4,640,128]{2,1,0:T(8,128)(2,1)S(1)} custom-call(s32[4]{0:T(128)S(1)} %broadcast_select_fusion.qid, s32[16]{0:T(128)S(1)} %select_n.135.kid, s32[256]{0:T(256)S(1)} %reshape.132.bs, s32[16]{0:T(128)S(1)} %copy-done, bf16[4,640,128]{2,1,0:T(8,128)(2,1)S(1)} %pad_maximum_fusion.4.q_ref, bf16[4,2,640,128]{3,2,1,0:T(8,128)(2,1)S(1)} %pad_maximum_fusion.g0, ...), custom_call_target="tpu_custom_call" | custom-call | flops 4697620480 | bytes 6291456 | tf_op jit(solution)/shard_map/attend/pallas_call | solution.py:112
  93.6 3.3 %collective-permute-start.6 = (bf16[640,128]{1,0:T(8,128)(2,1)S(1)}, bf16[640,128]{1,0:T(8,128)(2,1)S(1)}, u32[]{:S(2)}, u32[]{:S(2)}) collective-permute-start(bf16[640,128]{1,0:T(8,128)(2,1)S(1)} %get-tuple-element.41), channel_id=1, source_target_pairs={{0,24},{1,97},{2,26},{3,99},{4,28},{5,101},{6,30},{7,103},{8,0},{9... | collective-permute-start | bytes 491528 | tf_op jit(solution)/shard_map/ppermute | solution.py:34
  96.9 2.4 %collective-permute-start.8 = (bf16[640,128]{1,0:T(8,128)(2,1)S(1)}, bf16[640,128]{1,0:T(8,128)(2,1)S(1)}, u32[]{:S(2)}, u32[]{:S(2)}) collective-permute-start(bf16[640,128]{1,0:T(8,128)(2,1)S(1)} %get-tuple-element.39), channel_id=1, source_target_pairs={{0,8},{1,33},{2,10},{3,35},{4,12},{5,37},{6,14},{7,39},{8,16},{9,4... | collective-permute-start | bytes 491528 | tf_op jit(solution)/shard_map/ppermute | solution.py:34
  99.2 8.0 %attend.3 = bf16[1,640,128]{2,1,0:T(8,128)(2,1)S(1)} custom-call(s32[1]{0:T(128)} %bitcast.23.qid, s32[16]{0:T(128)S(1)} %select_n.135.kid, s32[256]{0:T(256)S(1)} %reshape.132.bs, s32[16]{0:T(128)S(1)} %copy-done, bf16[1,640,128]{2,1,0:T(8,128)(2,1)S(1)} %get-tuple-element.22.q_ref, bf16[4,2,640,128]{3,2,1,0:T(8,128)(2,1)S(1)} %pad_maximum_fusion.1.g0, ...), custom_call_target="tpu_custom_call" | custom-call | flops 1174405120 | bytes 6291456 | tf_op jit(solution)/shard_map/attend/pallas_call | solution.py:112
  107.3 5.8 %project.3 = bf16[4,640,640]{2,1,0:T(8,128)(2,1)S(1)} custom-call(s32[4]{0:T(128)S(1)} %add_subtract_fusion.order, s32[1]{0:T(128)} %bitcast.pos, bf16[640,128]{1,0:T(8,128)(2,1)S(1)} %get-tuple-element.42.o0, bf16[640,128]{1,0:T(8,128)(2,1)S(1)} %collective-permute-done.6.o1, bf16[640,128]{1,0:T(8,128)(2,1)S(1)} %collective-permute-done.7.o2, ...), custom_call_target="tpu_custom_call" | custom-call | flops 2097152000 | bytes 6553600 | tf_op jit(solution)/shard_map/project/pallas_call | solution.py:150
  113.4 5.8 %project.2 = bf16[4,640,640]{2,1,0:T(8,128)(2,1)S(1)} custom-call(s32[4]{0:T(128)S(1)} %get-tuple-element.5.order, s32[1]{0:T(128)} %bitcast.pos, bf16[640,128]{1,0:T(8,128)(2,1)S(1)} %get-tuple-element.42.o0, bf16[640,128]{1,0:T(8,128)(2,1)S(1)} %collective-permute-done.6.o1, bf16[640,128]{1,0:T(8,128)(2,1)S(1)} %collective-permute-done.7.o2, ...), custom_call_target="tpu_custom_call" | custom-call | flops 2097152000 | bytes 6553600 | tf_op jit(solution)/shard_map/project/pallas_call | solution.py:150
  119.9 3.1 %collective-permute-start.15 = (bf16[320,640]{1,0:T(8,128)(2,1)S(1)}, bf16[320,640]{1,0:T(8,128)(2,1)S(1)}, u32[]{:S(2)}, u32[]{:S(2)}) collective-permute-start(bf16[320,640]{1,0:T(8,128)(2,1)S(1)} %get-tuple-element.11), channel_id=1, source_target_pairs={{0,6},{1,7},{2,0},{3,1},{4,2},{5,3},{6,4},{7,5},{8,14},{9,15},{10,... | collective-permute-start | bytes 1228808 | tf_op jit(solution)/shard_map/ppermute | solution.py:42
  123.1 9.3 %collective-permute-done.15 = bf16[320,640]{1,0:T(8,128)(2,1)S(1)} collective-permute-done((bf16[320,640]{1,0:T(8,128)(2,1)S(1)}, bf16[320,640]{1,0:T(8,128)(2,1)S(1)}, u32[]{:S(2)}, u32[]{:S(2)}) %collective-permute-start.15) | collective-permute-done | bytes 409632 | tf_op jit(solution)/shard_map/ppermute | solution.py:42
  132.6 3.8 %collective-permute-start.16 = (bf16[640,640]{1,0:T(8,128)(2,1)S(1)}, bf16[640,640]{1,0:T(8,128)(2,1)S(1)}, u32[]{:S(2)}, u32[]{:S(2)}) collective-permute-start(bf16[640,640]{1,0:T(8,128)(2,1)S(1)} %pad_maximum_fusion.3), channel_id=1, source_target_pairs={{0,6},{1,7},{2,0},{3,1},{4,2},{5,3},{6,4},{7,5},{8,14},{9,15},{10,... | collective-permute-start | bytes 2457608 | tf_op jit(solution)/shard_map/ppermute | solution.py:42
  136.6 17.1 %collective-permute-done.16 = bf16[640,640]{1,0:T(8,128)(2,1)S(1)} collective-permute-done((bf16[640,640]{1,0:T(8,128)(2,1)S(1)}, bf16[640,640]{1,0:T(8,128)(2,1)S(1)}, u32[]{:S(2)}, u32[]{:S(2)}) %collective-permute-start.16) | collective-permute-done | bytes 819232 | tf_op jit(solution)/shard_map/ppermute | solution.py:42
  153.7 3.7 %collective-permute-done.14 = bf16[640,640]{1,0:T(8,128)(2,1)S(1)} collective-permute-done((bf16[640,640]{1,0:T(8,128)(2,1)S(1)}, bf16[640,640]{1,0:T(8,128)(2,1)S(1)}, u32[]{:S(2)}, u32[]{:S(2)}) %collective-permute-start.14) | collective-permute-done | bytes 819232 | tf_op jit(solution)/shard_map/ppermute | solution.py:42
  (63 shorter events, 12.0 us)
Async XLA Ops:
  0.0 4.7 %copy-start.2 = (bf16[640,640]{1,0:T(8,128)(2,1)S(1)}, bf16[640,640]{1,0:T(8,128)(2,1)}, u32[]{:S(2)}) copy-start(bf16[640,640]{1,0:T(8,128)(2,1)} %param.8) | copy-start | bytes 2457604
  0.0 3.9 %copy-start.1 = (bf16[640,640]{1,0:T(8,128)(2,1)S(1)}, bf16[640,640]{1,0:T(8,128)(2,1)}, u32[]{:S(2)}) copy-start(bf16[640,640]{1,0:T(8,128)(2,1)} %param.9) | copy-start | bytes 2457604
  6.3 12.6 %collective-permute-start.2 = (bf16[5,640,128]{2,1,0:T(8,128)(2,1)}, bf16[5,640,128]{2,1,0:T(8,128)(2,1)S(1)}, u32[]{:S(2)}, u32[]{:S(2)}) collective-permute-start(bf16[5,640,128]{2,1,0:T(8,128)(2,1)} %get-tuple-element.26), channel_id=1, source_target_pairs={{0,24},{1,97},{2,26},{3,99},{4,28},{5,101},{6,30},{7,103},{8,0},{9... | collective-permute-start | bytes 2457608 | tf_op jit(solution)/shard_map/ppermute | solution.py:34
  6.3 22.7 %collective-permute-start.1 = (bf16[5,640,128]{2,1,0:T(8,128)(2,1)}, bf16[5,640,128]{2,1,0:T(8,128)(2,1)S(1)}, u32[]{:S(2)}, u32[]{:S(2)}) collective-permute-start(bf16[5,640,128]{2,1,0:T(8,128)(2,1)} %get-tuple-element.25), channel_id=1, source_target_pairs={{0,16},{1,65},{2,18},{3,67},{4,20},{5,69},{6,22},{7,71},{8,24},{9,... | collective-permute-start | bytes 2457608 | tf_op jit(solution)/shard_map/ppermute | solution.py:34
  9.7 20.2 %collective-permute-start = (bf16[5,640,128]{2,1,0:T(8,128)(2,1)}, bf16[5,640,128]{2,1,0:T(8,128)(2,1)}, u32[]{:S(2)}, u32[]{:S(2)}) collective-permute-start(bf16[5,640,128]{2,1,0:T(8,128)(2,1)} %get-tuple-element.24), channel_id=1, source_target_pairs={{0,8},{1,33},{2,10},{3,35},{4,12},{5,37},{6,14},{7,39},{8,16},{9,4... | collective-permute-start | bytes 2457608 | tf_op jit(solution)/shard_map/ppermute | solution.py:34
  29.0 2.0 %copy-start.3 = (bf16[5,640,128]{2,1,0:T(8,128)(2,1)}, bf16[5,640,128]{2,1,0:T(8,128)(2,1)S(1)}, u32[]{:S(2)}) copy-start(bf16[5,640,128]{2,1,0:T(8,128)(2,1)S(1)} %collective-permute-done.1) | copy-start | bytes 2457604
  31.2 19.0 %collective-permute-start.3 = (bf16[4,2,640,128]{3,2,1,0:T(8,128)(2,1)S(1)}, bf16[4,2,640,128]{3,2,1,0:T(8,128)(2,1)}, u32[]{:S(2)}, u32[]{:S(2)}) collective-permute-start(bf16[4,2,640,128]{3,2,1,0:T(8,128)(2,1)S(1)} %pad_maximum_fusion.g0), channel_id=1, source_target_pairs={{0,32},{1,9},{2,34},{3,11},{4,36},{5,13},{6,38},{7,15},{8,40},{9,1... | collective-permute-start | bytes 3932168 | tf_op jit(solution)/shard_map/ppermute | solution.py:38
  32.7 17.7 %copy-start.5 = (s32[4]{0:T(128)S(1)}, s32[4]{0:T(128)}, u32[]{:S(2)}) copy-start(s32[4]{0:T(128)} %constant.125.clone) | copy-start | bytes 52
  32.8 21.2 %copy-start.4 = (s32[16,16]{1,0:T(8,128)S(1)}, s32[16,16]{1,0:T(8,128)}, u32[]{:S(2)}) copy-start(s32[16,16]{1,0:T(8,128)} %param.11) | copy-start | bytes 3076
  33.0 36.4 %copy-start = (s32[16]{0:T(128)S(1)}, s32[16]{0:T(128)}, u32[]{:S(2)}) copy-start(s32[16]{0:T(128)} %bw.3) | copy-start | bytes 196
  33.0 19.1 %collective-permute-start.10 = (bf16[4,2,640,128]{3,2,1,0:T(8,128)(2,1)S(1)}, bf16[4,2,640,128]{3,2,1,0:T(8,128)(2,1)}, u32[]{:S(2)}, u32[]{:S(2)}) collective-permute-start(bf16[4,2,640,128]{3,2,1,0:T(8,128)(2,1)S(1)} %pad_maximum_fusion.1.g0), channel_id=1, source_target_pairs={{0,96},{1,25},{2,98},{3,27},{4,100},{5,29},{6,102},{7,31},{8,104},... | collective-permute-start | bytes 3932168 | tf_op jit(solution)/shard_map/ppermute | solution.py:38
  34.8 30.0 %collective-permute-start.5 = (bf16[4,2,640,128]{3,2,1,0:T(8,128)(2,1)S(1)}, bf16[4,2,640,128]{3,2,1,0:T(8,128)(2,1)}, u32[]{:S(2)}, u32[]{:S(2)}) collective-permute-start(bf16[4,2,640,128]{3,2,1,0:T(8,128)(2,1)S(1)} %pad_maximum_fusion.g0), channel_id=1, source_target_pairs={{0,96},{1,25},{2,98},{3,27},{4,100},{5,29},{6,102},{7,31},{8,104},... | collective-permute-start | bytes 3932168 | tf_op jit(solution)/shard_map/ppermute | solution.py:38
  50.2 19.1 %collective-permute-start.4 = (bf16[4,2,640,128]{3,2,1,0:T(8,128)(2,1)}, bf16[4,2,640,128]{3,2,1,0:T(8,128)(2,1)}, u32[]{:S(2)}, u32[]{:S(2)}) collective-permute-start(bf16[4,2,640,128]{3,2,1,0:T(8,128)(2,1)} %collective-permute-done.3.g1), channel_id=1, source_target_pairs={{0,32},{1,9},{2,34},{3,11},{4,36},{5,13},{6,38},{7,15},{8,40},{9,1... | collective-permute-start | bytes 3932168 | tf_op jit(solution)/shard_map/ppermute | solution.py:38
  50.6 48.6 %collective-permute-start.9 = (bf16[4,2,640,128]{3,2,1,0:T(8,128)(2,1)S(1)}, bf16[4,2,640,128]{3,2,1,0:T(8,128)(2,1)}, u32[]{:S(2)}, u32[]{:S(2)}) collective-permute-start(bf16[4,2,640,128]{3,2,1,0:T(8,128)(2,1)S(1)} %pad_maximum_fusion.1.g0), channel_id=1, source_target_pairs={{0,32},{1,9},{2,34},{3,11},{4,36},{5,13},{6,38},{7,15},{8,40},{9,1... | collective-permute-start | bytes 3932168 | tf_op jit(solution)/shard_map/ppermute | solution.py:38
  52.1 47.1 %collective-permute-start.11 = (bf16[4,2,640,128]{3,2,1,0:T(8,128)(2,1)}, bf16[4,2,640,128]{3,2,1,0:T(8,128)(2,1)}, u32[]{:S(2)}, u32[]{:S(2)}) collective-permute-start(bf16[4,2,640,128]{3,2,1,0:T(8,128)(2,1)} %collective-permute-done.10.g3), channel_id=1, source_target_pairs={{0,96},{1,25},{2,98},{3,27},{4,100},{5,29},{6,102},{7,31},{8,104},... | collective-permute-start | bytes 3932168 | tf_op jit(solution)/shard_map/ppermute | solution.py:38
  54.0 2.0 %slice-start = ((bf16[5,640,128]{2,1,0:T(8,128)(2,1)}), bf16[1,640,128]{2,1,0:T(8,128)(2,1)S(1)}, s32[]{:S(2)}) async-start(bf16[5,640,128]{2,1,0:T(8,128)(2,1)} %copy-done.3), calls=%async_computation | async-start | bytes 327680 | tf_op jit(solution)/shard_map/slice | solution.py:199
  93.6 13.7 %collective-permute-start.6 = (bf16[640,128]{1,0:T(8,128)(2,1)S(1)}, bf16[640,128]{1,0:T(8,128)(2,1)S(1)}, u32[]{:S(2)}, u32[]{:S(2)}) collective-permute-start(bf16[640,128]{1,0:T(8,128)(2,1)S(1)} %get-tuple-element.41), channel_id=1, source_target_pairs={{0,24},{1,97},{2,26},{3,99},{4,28},{5,101},{6,30},{7,103},{8,0},{9... | collective-permute-start | bytes 491528 | tf_op jit(solution)/shard_map/ppermute | solution.py:34
  96.9 10.4 %collective-permute-start.7 = (bf16[640,128]{1,0:T(8,128)(2,1)S(1)}, bf16[640,128]{1,0:T(8,128)(2,1)S(1)}, u32[]{:S(2)}, u32[]{:S(2)}) collective-permute-start(bf16[640,128]{1,0:T(8,128)(2,1)S(1)} %get-tuple-element.40), channel_id=1, source_target_pairs={{0,16},{1,65},{2,18},{3,67},{4,20},{5,69},{6,22},{7,71},{8,24},{9,... | collective-permute-start | bytes 491528 | tf_op jit(solution)/shard_map/ppermute | solution.py:34
  96.9 10.4 %collective-permute-start.8 = (bf16[640,128]{1,0:T(8,128)(2,1)S(1)}, bf16[640,128]{1,0:T(8,128)(2,1)S(1)}, u32[]{:S(2)}, u32[]{:S(2)}) collective-permute-start(bf16[640,128]{1,0:T(8,128)(2,1)S(1)} %get-tuple-element.39), channel_id=1, source_target_pairs={{0,8},{1,33},{2,10},{3,35},{4,12},{5,37},{6,14},{7,39},{8,16},{9,4... | collective-permute-start | bytes 491528 | tf_op jit(solution)/shard_map/ppermute | solution.py:34
  113.1 6.1 %collective-permute-start.12 = (bf16[4,640,640]{2,1,0:T(8,128)(2,1)S(1)}, bf16[4,640,640]{2,1,0:T(8,128)(2,1)S(1)}, u32[]{:S(2)}, u32[]{:S(2)}) collective-permute-start(bf16[4,640,640]{2,1,0:T(8,128)(2,1)S(1)} %project.3), channel_id=1, source_target_pairs={{0,1},{1,0},{2,3},{3,2},{4,5},{5,4},{6,7},{7,6},{8,9},{9,8},{10,11... | collective-permute-start | bytes 9830408 | tf_op jit(solution)/shard_map/ppermute | solution.py:46
  119.9 12.4 %collective-permute-start.15 = (bf16[320,640]{1,0:T(8,128)(2,1)S(1)}, bf16[320,640]{1,0:T(8,128)(2,1)S(1)}, u32[]{:S(2)}, u32[]{:S(2)}) collective-permute-start(bf16[320,640]{1,0:T(8,128)(2,1)S(1)} %get-tuple-element.11), channel_id=1, source_target_pairs={{0,6},{1,7},{2,0},{3,1},{4,2},{5,3},{6,4},{7,5},{8,14},{9,15},{10,... | collective-permute-start | bytes 1228808 | tf_op jit(solution)/shard_map/ppermute | solution.py:42
  123.0 13.3 %collective-permute-start.13 = (bf16[320,640]{1,0:T(8,128)(2,1)S(1)}, bf16[320,640]{1,0:T(8,128)(2,1)S(1)}, u32[]{:S(2)}, u32[]{:S(2)}) collective-permute-start(bf16[320,640]{1,0:T(8,128)(2,1)S(1)} %get-tuple-element.10), channel_id=1, source_target_pairs={{0,2},{1,3},{2,4},{3,5},{4,6},{5,7},{6,0},{7,1},{8,10},{9,11},{10,... | collective-permute-start | bytes 1228808 | tf_op jit(solution)/shard_map/ppermute | solution.py:42
  132.6 21.1 %collective-permute-start.16 = (bf16[640,640]{1,0:T(8,128)(2,1)S(1)}, bf16[640,640]{1,0:T(8,128)(2,1)S(1)}, u32[]{:S(2)}, u32[]{:S(2)}) collective-permute-start(bf16[640,640]{1,0:T(8,128)(2,1)S(1)} %pad_maximum_fusion.3), channel_id=1, source_target_pairs={{0,6},{1,7},{2,0},{3,1},{4,2},{5,3},{6,4},{7,5},{8,14},{9,15},{10,... | collective-permute-start | bytes 2457608 | tf_op jit(solution)/shard_map/ppermute | solution.py:42
  136.5 20.8 %collective-permute-start.14 = (bf16[640,640]{1,0:T(8,128)(2,1)S(1)}, bf16[640,640]{1,0:T(8,128)(2,1)S(1)}, u32[]{:S(2)}, u32[]{:S(2)}) collective-permute-start(bf16[640,640]{1,0:T(8,128)(2,1)S(1)} %pad_maximum_fusion.2), channel_id=1, source_target_pairs={{0,2},{1,3},{2,4},{3,5},{4,6},{5,7},{6,0},{7,1},{8,10},{9,11},{10,... | collective-permute-start | bytes 2457608 | tf_op jit(solution)/shard_map/ppermute | solution.py:42

commit v2 on v1

v2 whole, which is shorter than its diff:
```python
import functools

import jax
import jax.numpy as jnp
from jax import lax
from jax.experimental import pallas as pl
from jax.experimental.pallas import tpu as pltpu
from jax.sharding import PartitionSpec as P

HD = 128
BLOCK = 128
NB = 5
FT = 640
FRAMES = 16
SIDE = 4
ROWS = 128
LOG2_SCALE = 1.4426950408889634 / HD**0.5
NT = (((1,), (1,)), ((), ()))
NN = (((1,), (0,)), ((), ()))
BOTH = ("frame", "head")


def pairs(move):
    out = []
    for i in range(128):
        frame, head = divmod(i, 8)
        x, z, y, c = move(*divmod(frame, 4), *divmod(head, 2))
        out.append((i, (x % 4 * 4 + z % 4) * 8 + y % 4 * 2 + c))
    return out


def line_shift(v, s):
    return lax.ppermute(v, BOTH, pairs(lambda x, z, y, c: (x, z + s, y, c) if c == 0 else (x + s, z, y, c)))


def cross_shift(v, s):
    return lax.ppermute(v, BOTH, pairs(lambda x, z, y, c: (x + s, z, y, c) if c == 0 else (x, z + s, y, c)))


def y_shift(v, s):
    return lax.ppermute(v, BOTH, pairs(lambda x, z, y, c: (x, z, y + s, c)))


def core_swap(v):
    return lax.ppermute(v, BOTH, pairs(lambda x, z, y, c: (x, z, y, 1 - c)))


ANY = pl.BlockSpec(memory_space=pl.ANY)
VMEM = pl.BlockSpec(memory_space=pltpu.VMEM)
LIMIT = 20 << 20


def fence_kernel(*refs):
    del refs


def fence(values, *after):
    count = len(values)
    return pl.pallas_call(
        fence_kernel,
        in_specs=[ANY] * (count + len(after)),
        out_specs=[ANY] * count,
        out_shape=[jax.ShapeDtypeStruct(v.shape, v.dtype) for v in values],
        input_output_aliases={i: i for i in range(count)},
        name="fence",
    )(*values, *after)


def pick_kernel(pos, q_ref, k_ref, v_ref, *outs):
    for s, out in enumerate(outs):
        head = lax.rem(pos[0] + s, SIDE)
        columns = pl.ds(pl.multiple_of(head * HD, HD), HD)
        out[0] = q_ref[:, columns]
        out[1] = k_ref[:, columns]
        out[2] = v_ref[:, columns]
        out[3] = k_ref[:, 4 * HD :]
        out[4] = v_ref[:, 4 * HD :]


def pick(pos, queries, keys, values):
    return pl.pallas_call(
        pick_kernel,
        in_specs=[pl.BlockSpec(memory_space=pltpu.SMEM)] + [VMEM] * 3,
        out_specs=[VMEM] * SIDE,
        out_shape=[jax.ShapeDtypeStruct((5, FT, HD), jnp.bfloat16)] * SIDE,
        compiler_params=pltpu.CompilerParams(vmem_limit_bytes=LIMIT),
        name="pick",
    )(pos, queries, keys, values)


def block_rows(n):
    return pl.ds(pl.multiple_of(n * BLOCK, BLOCK), BLOCK)


def band_kernel(qid, kid, bs, *refs):
    keys, values, outs = refs[:SIDE], refs[SIDE : 2 * SIDE], refs[-3:]
    for s in range(SIDE):
        for i, out in enumerate(outs):
            first = bs[qid[i] * FRAMES + kid[s]]
            second = jnp.where(first == NB - 1, 0, first + 1)
            for j, source in enumerate((keys[s], values[s])):
                out[s, j, 0:BLOCK, :] = source[0, block_rows(first), :]
                out[s, j, BLOCK:, :] = source[0, block_rows(second), :]


def bands(qid, kid, bs, pieces, *after):
    shape = (SIDE, 2, 2 * BLOCK, HD)
    return pl.pallas_call(
        band_kernel,
        grid_spec=pltpu.PrefetchScalarGridSpec(
            num_scalar_prefetch=3,
            grid=(1,),
            in_specs=[pl.BlockSpec((1, FT, HD), lambda i, *_, j=j: (j, 0, 0)) for j in (3, 4) for _ in pieces]
            + [ANY] * len(after),
            out_specs=[pl.BlockSpec(shape, lambda i, *_: (0, 0, 0, 0))] * 3,
        ),
        out_shape=[jax.ShapeDtypeStruct(shape, jnp.bfloat16)] * 3,
        name="bands",
    )(qid, kid, bs, *pieces, *pieces, *after)


def place(n, keys, values, row, kc, vc, valid=None, stand_in=None):
    ones = lax.broadcasted_iota(jnp.int32, (BLOCK, HD), 1) == 0
    at = slice(n * BLOCK, (n + 1) * BLOCK)
    if valid is None:
        kc[at, :] = keys[block_rows(row), :]
        vc[at, 0:HD] = values[block_rows(row), :]
        vc[at, HD:] = ones.astype(jnp.bfloat16)
    else:
        kc[at, :] = keys[block_rows(jnp.where(valid, row, stand_in)), :]
        kept = jnp.where(valid, 1.0, 0.0)
        vc[at, 0:HD] = (values[block_rows(row), :].astype(jnp.float32) * kept).astype(jnp.bfloat16)
        vc[at, HD:] = jnp.where(ones, kept, 0.0).astype(jnp.bfloat16)


def band_of(a, b, bs, bw):
    own = a == b
    first = jnp.where(own, 0, bs[a * FRAMES + b])
    second = jnp.where(first == NB - 1, 0, first + 1)
    return first, second, own | (bw[jnp.abs(a - b)] == 2)


def attend_to(q, kc, vc, state, emit):
    kk, vv = kc[...], vc[...]
    steps = FT // ROWS

    def score(r):
        return lax.dot_general(q[r * ROWS : (r + 1) * ROWS, :], kk, NT, preferred_element_type=jnp.float32)

    scores = score(0)
    for r in range(steps):
        later = score(r + 1) if r + 1 < steps else None
        rows = slice(r * ROWS, (r + 1) * ROWS)
        new = jnp.max(scores, axis=1, keepdims=True)
        if state:
            old = state[1][0, rows, 0:1]
            new = jnp.maximum(old, new)
        probs = jnp.exp2(scores * LOG2_SCALE - new * LOG2_SCALE).astype(jnp.bfloat16)
        mixed = lax.dot_general(probs, vv, NN, preferred_element_type=jnp.float32)
        weighted, totals = mixed[:, 0:HD], mixed[:, HD : HD + 1]
        if state:
            factor = jnp.exp2((old - new) * LOG2_SCALE)
            weighted = weighted + state[0][0, rows, :] * factor
            totals = totals + state[1][0, rows, 1:2] * factor
        emit(rows, weighted, totals, new)
        scores = later


def put_state(acc, stats):
    def emit(rows, weighted, totals, new):
        acc[0, rows, :] = weighted
        column = lax.broadcasted_iota(jnp.int32, (ROWS, HD), 1)
        stats[0, rows, :] = jnp.where(column == 0, new, totals)

    return emit


def put_result(out):
    def emit(rows, weighted, totals, new):
        out[0, rows, :] = (weighted / totals).astype(jnp.bfloat16)

    return emit


def line_kernel(qid, kid, bs, bw, p0, p1, p2, p3, q_last, acc, stats, q, kc, vc):
    i = pl.program_id(0)
    which = jnp.where(i == SIDE, 3, 1)
    own = jnp.where(i == SIDE, 0, i)
    for s, piece in enumerate((p0, p1, p2, p3)):
        keys, values = piece.at[which], piece.at[which + 1]
        first, second, valid = band_of(qid[i], kid[s], bs, bw)
        place(2 * s, keys, values, first, kc, vc)
        place(2 * s + 1, keys, values, second, kc, vc, valid, first)

        @pl.when(own == s)
        def _(keys=keys, values=values):
            for j in range(2, NB):
                place(2 * SIDE + j - 2, keys, values, j, kc, vc)

        @pl.when(i == s)
        def _(piece=piece):
            q[...] = piece[0]

    @pl.when(i == SIDE)
    def _():
        q[...] = q_last[...]

    attend_to(q, kc, vc, None, put_state(acc, stats))


ITEM = pl.BlockSpec((1, FT, HD), lambda i, *_: (i, 0, 0))


def cost(items, blocks):
    pairs_read = items * FT * blocks * BLOCK
    return pl.CostEstimate(flops=pairs_read * 4 * HD, bytes_accessed=8 << 20, transcendentals=pairs_read)


def packed(blocks):
    return [pltpu.VMEM((blocks * BLOCK, HD), jnp.bfloat16), pltpu.VMEM((blocks * BLOCK, 2 * HD), jnp.bfloat16)]


def state_shape(items):
    return [jax.ShapeDtypeStruct((items, FT, HD), jnp.float32)] * 2


def attend_line(qid, kid, bs, bw, pieces, queries):
    blocks = 2 * SIDE + NB - 2
    items = SIDE + 1
    return pl.pallas_call(
        line_kernel,
        grid_spec=pltpu.PrefetchScalarGridSpec(
            num_scalar_prefetch=4,
            grid=(items,),
            in_specs=[pl.BlockSpec((5, FT, HD), lambda i, *_: (0, 0, 0))] * SIDE
            + [pl.BlockSpec((FT, HD), lambda i, *_: (0, SIDE))],
            out_specs=[ITEM, ITEM],
            scratch_shapes=[pltpu.VMEM((FT, HD), jnp.bfloat16)] + packed(blocks),
        ),
        out_shape=state_shape(items),
        compiler_params=pltpu.CompilerParams(vmem_limit_bytes=LIMIT),
        cost_estimate=cost(items, blocks),
        name="attend_line",
    )(qid, kid, bs, bw, *pieces, queries)


def groups_kernel(count, finished, qid, kid, bs, bw, *refs):
    q_refs, groups, refs = refs[:SIDE], refs[SIDE : SIDE + count], refs[SIDE + count :]
    state, results, (q, kc, vc) = refs[:2], refs[2:-3], refs[-3:]
    i = pl.program_id(0)
    for s, q_ref in enumerate(q_refs):

        @pl.when(i == s)
        def _(q_ref=q_ref):
            q[...] = q_ref[0]

    for d in range(count // 2):
        for s in range(SIDE):
            n = d * SIDE + s
            keys, values = groups[2 * d].at[s], groups[2 * d + 1].at[s]
            first, second, valid = band_of(qid[i], kid[n], bs, bw)
            place(2 * n, keys, values, first, kc, vc)
            place(2 * n + 1, keys, values, second, kc, vc, valid, first)
    attend_to(q, kc, vc, state, put_result(*results) if finished else put_state(*results))


def attend_groups(qid, kid, bs, bw, pieces, groups, state, finished=False):
    blocks = SIDE * len(groups)
    whole = pl.BlockSpec((SIDE, FT, HD), lambda i, *_: (0, 0, 0))
    return pl.pallas_call(
        functools.partial(groups_kernel, len(groups), finished),
        grid_spec=pltpu.PrefetchScalarGridSpec(
            num_scalar_prefetch=4,
            grid=(SIDE,),
            in_specs=[pl.BlockSpec((1, FT, HD), lambda i, *_: (0, 0, 0))] * SIDE + [whole] * len(groups) + [ITEM] * 2,
            out_specs=ITEM if finished else [ITEM] * 2,
            scratch_shapes=[pltpu.VMEM((FT, HD), jnp.bfloat16)] + packed(blocks),
        ),
        out_shape=jax.ShapeDtypeStruct((SIDE, FT, HD), jnp.bfloat16) if finished else state_shape(SIDE),
        compiler_params=pltpu.CompilerParams(vmem_limit_bytes=LIMIT),
        cost_estimate=cost(SIDE, blocks),
        name="attend_groups",
    )(qid, kid, bs, bw, *pieces, *groups, *state)


def bands_attend_kernel(qid, kid, bs, bw, q, g1, g2, g3, acc, stats, after, out, kc, vc):
    del after
    for d, group in enumerate((g1, g2, g3)):
        for s in range(SIDE):
            n = d * SIDE + s
            valid = band_of(qid[0], kid[n], bs, bw)[2]
            place(2 * n, group.at[s, 0], group.at[s, 1], 0, kc, vc)
            place(2 * n + 1, group.at[s, 0], group.at[s, 1], 1, kc, vc, valid, 0)
    attend_to(q, kc, vc, (acc, stats), put_result(out))


def attend_bands(qid, kid, bs, bw, queries, groups, state, after):
    blocks = 2 * SIDE * len(groups)
    last = pl.BlockSpec((1, FT, HD), lambda i, *_: (SIDE, 0, 0))
    return pl.pallas_call(
        bands_attend_kernel,
        grid_spec=pltpu.PrefetchScalarGridSpec(
            num_scalar_prefetch=4,
            grid=(1,),
            in_specs=[pl.BlockSpec((FT, HD), lambda i, *_: (0, SIDE))]
            + [pl.BlockSpec(g.shape, lambda i, *_: (0, 0, 0, 0)) for g in groups]
            + [last, last, ANY],
            out_specs=ITEM,
            scratch_shapes=packed(blocks),
        ),
        out_shape=jax.ShapeDtypeStruct((1, FT, HD), jnp.bfloat16),
        compiler_params=pltpu.CompilerParams(vmem_limit_bytes=LIMIT),
        cost_estimate=cost(1, blocks),
        name="attend_bands",
    )(qid, kid, bs, bw, queries, *groups, *state, after)


def project_kernel(order, pos, o0, o1, o2, o3, o4, w_ref, *refs):
    y_ref, att = refs[-2:]
    for s, o in enumerate((o0, o1, o2, o3)):
        head = lax.rem(pos[0] + s, SIDE)
        att[:, pl.ds(pl.multiple_of(head * HD, HD), HD)] = o[...]
    att[:, 4 * HD :] = o4[...]
    width = y_ref.shape[2]
    for i in range(y_ref.shape[0]):
        weight = w_ref[:, pl.ds(pl.multiple_of(order[i] * width, width), width)]
        y_ref[i] = jnp.dot(att[...], weight, preferred_element_type=jnp.float32).astype(jnp.bfloat16)


def project(order, pos, outs, weight, *after):
    count = order.shape[0]
    width = weight.shape[1] // 8
    smem = pl.BlockSpec(memory_space=pltpu.SMEM)
    return pl.pallas_call(
        project_kernel,
        in_specs=[smem] * 2 + [VMEM] * 6 + [ANY] * len(after),
        out_specs=VMEM,
        scratch_shapes=[pltpu.VMEM((FT, 5 * HD), jnp.bfloat16)],
        out_shape=jax.ShapeDtypeStruct((count, FT, width), jnp.bfloat16),
        compiler_params=pltpu.CompilerParams(vmem_limit_bytes=LIMIT),
        cost_estimate=pl.CostEstimate(
            flops=2 * count * FT * 5 * HD * width, bytes_accessed=count * FT * width * 2, transcendentals=0
        ),
        name="project",
    )(order, pos, *outs, weight, *after)


def add(*terms):
    total = terms[0].astype(jnp.float32)
    for t in terms[1:]:
        total = total + t.astype(jnp.float32)
    return total.astype(jnp.bfloat16)


def shards(queries, key_rows, value_rows, out_weight, band_start, band_width):
    frame, head = lax.axis_index("frame"), lax.axis_index("head")
    x, z = frame // SIDE, frame % SIDE
    y, core = head // 2, head % 2
    line = jnp.where(core == 0, z, x)
    ring = jnp.arange(SIDE, dtype=jnp.int32)

    def frames_at(cross, along):
        return jnp.where(
            core == 0,
            (x - cross) % SIDE * SIDE + (z - along) % SIDE,
            (x - along) % SIDE * SIDE + (z - cross) % SIDE,
        )

    f0, f1, f2, f3 = [frames_at(d, ring) for d in range(SIDE)]
    bs, bw = band_start.reshape(-1), band_width

    pieces = pick(line[None], queries, key_rows, value_rows)
    pieces = [pieces[0]] + [line_shift(pieces[s], s) for s in range(1, SIDE)]
    k_0, v_0 = jnp.stack([p[1] for p in pieces]), jnp.stack([p[2] for p in pieces])

    k_1, v_3 = cross_shift(k_0, 1), cross_shift(v_0, 3)
    v_1, k_3 = cross_shift(v_0, 1), cross_shift(k_0, 3)
    state = attend_line(f0, f0, bs, bw, pieces, queries)
    k_1, v_3 = fence((k_1, v_3), state[1])
    k_2, v_2 = cross_shift(k_1, 1), cross_shift(v_3, 3)

    sent = bands(frames_at(-ring[1:], 0), f0, bs, pieces, v_1, k_3)
    last_1, last_2, last_3 = [cross_shift(sent[s - 1], s) for s in range(1, SIDE)]

    main = attend_groups(
        f0, jnp.concatenate([f1, f3]), bs, bw, pieces, [k_1, v_1, k_3, v_3], state
    )
    o_main = attend_groups(f0, f2, bs, bw, pieces, [k_2, v_2], main, True)
    outs = [o_main[0]] + [line_shift(o_main[s], SIDE - s) for s in range(1, SIDE)]
    o_last = attend_bands(
        frame[None], jnp.concatenate([f1, f2, f3]), bs, bw, queries, [last_1, last_2, last_3], state, o_main
    )
    outs.append(o_last[0])

    def summed(ahead, *after):
        target = (y + jnp.array(ahead, jnp.int32)) % SIDE * 2
        away = project(target + 1 - core, line[None], outs, out_weight, *after)
        given = core_swap(away)
        kept = project(target + core, line[None], outs, out_weight, away)
        return [add(kept[i], given[i]) for i in range(len(ahead))]

    half = FT // 2
    (two,) = summed([2])
    from_down, from_up = y_shift(two[:half], 1), y_shift(two[half:], 3)
    up, down = summed([1, 3], two)
    plain_up, plain_down = y_shift(up[half:], 1), y_shift(down[:half], 3)
    (own,) = summed([0], up)
    more_up, more_down = y_shift(add(up[:half], from_down), 1), y_shift(add(down[half:], from_up), 3)
    return jnp.concatenate([add(own[:half], more_up, plain_down), add(own[half:], plain_up, more_down)])


def solution(mesh):
    return jax.shard_map(
        shards,
        mesh=mesh,
        in_specs=(
            P("frame", "head"),
            P("frame", "head"),
            P("frame", "head"),
            P("head", None),
            P(),
            P(),
        ),
        out_specs=P("frame", "head"),
        check_vma=False,
    )
```

time: 159 us -> 139 us (0.87)
  the two profiles are of different devices: /device:TPU:32 before, /device:TPU:0 now
where the time goes in v2:
time: 139 us; the launch traced here: 138 us
  Pallas kernels  46.7 us (34%)
  waiting for transfers between devices  46.2 us (33%)
  starting transfers between devices  29.4 us (21%)
  local copies, waits for them, and re-layouts  10.2 us (7%)
  other arithmetic  5.23 us (4%)
    ppermute x6, waiting for transfers between devices, line_shift(): lax.ppermute(v, BOTH, pairs(lambda x, z, y, c: (x, z + s, y, c) if c == 0...  24.5 us
    pallas_call x2, Pallas kernels, attend_groups(): pl.pallas_call(functools.partial(groups_kernel, len(groups), finished), g...  20.5 us
    ppermute x6, waiting for transfers between devices, y_shift(): return lax.ppermute(v, BOTH, pairs(lambda x, z, y, c: (x, z, y + s, c)))  20.4 us
    ppermute x9, starting transfers between devices, cross_shift(): lax.ppermute(v, BOTH, pairs(lambda x, z, y, c: (x + s, z, y, c) if c == 0...  13 us
    unnamed x56, local copies, waits for them, and re-layouts  9.86 us
    pallas_call x1, Pallas kernels, attend_line(): pl.pallas_call(line_kernel, grid_spec=pltpu.PrefetchScalarGridSpec(num_sc...  9.85 us
    ppermute x6, starting transfers between devices, y_shift(): return lax.ppermute(v, BOTH, pairs(lambda x, z, y, c: (x, z, y + s, c)))  8.49 us
    pallas_call x6, Pallas kernels, project(): pl.pallas_call(project_kernel, in_specs=[smem] * 2 + [VMEM] * 6 + [ANY] *...  8.47 us
  transfers between devices with their start and end apart: 24, of which 11 were waited for; matrix products, arithmetic and copies ran while one was open for 2% of the time, Pallas kernels for 31%

profile of v2, /device:TPU:0, one launch (start us, length us, event | category | flops | bytes accessed | tf_op | source)
XLA Modules:
  0.0 138.3 jit_solution(5939391182731733909)
XLA Ops:
  4.0 4.2 %collective-permute-start.2 = (bf16[5,640,128]{2,1,0:T(8,128)(2,1)S(1)}, bf16[5,640,128]{2,1,0:T(8,128)(2,1)S(1)}, u32[]{:S(2)}, u32[]{:S(2)}) collective-permute-start(bf16[5,640,128]{2,1,0:T(8,128)(2,1)S(1)} %get-tuple-element.21), channel_id=1, source_target_pairs={{0,24},{1,97},{2,26},{3,99},{4,28},{5,101},{6,30},{7,103},{8,0},{9... | collective-permute-start | bytes 2457608 | tf_op jit(solution)/shard_map/ppermute | solution.py:33
  9.5 17.4 %collective-permute-done.2.p3.refs_3_.refs_7_ = bf16[5,640,128]{2,1,0:T(8,128)(2,1)S(1)} collective-permute-done((bf16[5,640,128]{2,1,0:T(8,128)(2,1)S(1)}, bf16[5,640,128]{2,1,0:T(8,128)(2,1)S(1)}, u32[]{:S(2)}, u32[]{:S(2)}) %collective-permute-start.2) | collective-permute-done | bytes 819232 | tf_op jit(solution)/shard_map/ppermute | solution.py:33
  26.9 3.6 %collective-permute-done.p1.refs_1_.refs_5_ = bf16[5,640,128]{2,1,0:T(8,128)(2,1)S(1)} collective-permute-done((bf16[5,640,128]{2,1,0:T(8,128)(2,1)S(1)}, bf16[5,640,128]{2,1,0:T(8,128)(2,1)S(1)}, u32[]{:S(2)}, u32[]{:S(2)}) %collective-permute-start) | collective-permute-done | bytes 819232 | tf_op jit(solution)/shard_map/ppermute | solution.py:33
  34.0 1.7 %collective-permute-start.4 = (bf16[4,640,128]{2,1,0:T(8,128)(2,1)}, bf16[4,640,128]{2,1,0:T(8,128)(2,1)}, u32[]{:S(2)}, u32[]{:S(2)}) collective-permute-start(bf16[4,640,128]{2,1,0:T(8,128)(2,1)} %pad_maximum_fusion.2), channel_id=1, source_target_pairs={{0,96},{1,25},{2,98},{3,27},{4,100},{5,29},{6,102},{7,31},{8,104},... | collective-permute-start | bytes 1966088 | tf_op jit(solution)/shard_map/ppermute | solution.py:37
  36.3 3.0 %collective-permute-start.8 = (bf16[4,640,128]{2,1,0:T(8,128)(2,1)}, bf16[4,640,128]{2,1,0:T(8,128)(2,1)}, u32[]{:S(2)}, u32[]{:S(2)}) collective-permute-start(bf16[4,640,128]{2,1,0:T(8,128)(2,1)} %pad_maximum_fusion.1), channel_id=1, source_target_pairs={{0,96},{1,25},{2,98},{3,27},{4,100},{5,29},{6,102},{7,31},{8,104},... | collective-permute-start | bytes 1966088 | tf_op jit(solution)/shard_map/ppermute | solution.py:37
  40.4 9.8 %attend_line.1 = (f32[5,640,128]{2,1,0:T(8,128)S(1)}, f32[5,640,128]{2,1,0:T(8,128)S(1)}) custom-call(s32[4]{0:T(128)S(1)} %broadcast_select_fusion.4.qid.kid, s32[4]{0:T(128)S(1)} %broadcast_select_fusion.4.qid.kid, s32[256]{0:T(256)S(1)} %reshape.39.bs, s32[16]{0:T(128)S(1)} %copy-done.23, bf16[5,640,128]{2,1,0:T(8,128)(2,1)S(1)} %get-tuple-element.18.p0.refs_0_.refs_4_, ...), custom_call_target="tpu_custom_call" | custom-call | flops 2306867200 | bytes 8388608 | tf_op jit(solution)/shard_map/attend_line/pallas_call | solution.py:230
  52.7 3.2 %collective-permute-start.6 = (bf16[4,640,128]{2,1,0:T(8,128)(2,1)}, bf16[4,640,128]{2,1,0:T(8,128)(2,1)}, u32[]{:S(2)}, u32[]{:S(2)}) collective-permute-start(bf16[4,640,128]{2,1,0:T(8,128)(2,1)} %get-tuple-element.24.refs_7_), channel_id=1, source_target_pairs={{0,96},{1,25},{2,98},{3,27},{4,100},{5,29},{6,102},{7,31},{8,104},... | collective-permute-start | bytes 1966088 | tf_op jit(solution)/shard_map/ppermute | solution.py:37
  56.7 3.6 %bands.1 = (bf16[4,2,256,128]{3,2,1,0:T(8,128)(2,1)}, bf16[4,2,256,128]{3,2,1,0:T(8,128)(2,1)}, bf16[4,2,256,128]{3,2,1,0:T(8,128)(2,1)}) custom-call(s32[3]{0:T(128)} %broadcast_select_fusion.qid, s32[4]{0:T(128)} %copy-done.21, s32[256]{0:T(256)} %copy-done.19, bf16[5,640,128]{2,1,0:T(8,128)(2,1)} %copy-done, bf16[5,640,128]{2,1,0:T(8,128)(2,1)} %copy-done.6, ...), custom_call_target="tpu_custom_call" | custom-call | tf_op jit(solution)/shard_map/bands/pallas_call | solution.py:108
  61.8 1.8 %collective-permute-start.14 = (bf16[4,2,256,128]{3,2,1,0:T(8,128)(2,1)}, bf16[4,2,256,128]{3,2,1,0:T(8,128)(2,1)S(1)}, u32[]{:S(2)}, u32[]{:S(2)}) collective-permute-start(bf16[4,2,256,128]{3,2,1,0:T(8,128)(2,1)} %get-tuple-element.30), channel_id=1, source_target_pairs={{0,96},{1,25},{2,98},{3,27},{4,100},{5,29},{6,102},{7,31},{8,104},... | collective-permute-start | bytes 1572872 | tf_op jit(solution)/shard_map/ppermute | solution.py:37
  66.4 11.6 %attend_groups.2 = (f32[4,640,128]{2,1,0:T(8,128)S(1)}, f32[4,640,128]{2,1,0:T(8,128)S(1)}) custom-call(s32[4]{0:T(128)S(1)} %copy-done.22, s32[8]{0:T(128)S(1)} %pad_add_fusion.kid, s32[256]{0:T(256)S(1)} %copy-done.20, s32[16]{0:T(128)S(1)} %copy-done.23, bf16[5,640,128]{2,1,0:T(8,128)(2,1)S(1)} %copy-done.1, bf16[5,640,128]{2,1,0:T(8,128)(2,1)S(1)} %copy-done.7, ...), custom_call_target="tpu_custom_call" | custom-call | flops 2684354560 | bytes 8388608 | tf_op jit(solution)/shard_map/attend_groups/pallas_call | solution.py:270
  78.1 8.9 %attend_groups.3.after = bf16[4,640,128]{2,1,0:T(8,128)(2,1)S(1)} custom-call(s32[4]{0:T(128)S(1)} %copy-done.22, s32[4]{0:T(128)S(1)} %broadcast_select_fusion.3.kid, s32[256]{0:T(256)S(1)} %copy-done.20, s32[16]{0:T(128)S(1)} %copy-done.23, bf16[5,640,128]{2,1,0:T(8,128)(2,1)S(1)} %copy-done.1, bf16[5,640,128]{2,1,0:T(8,128)(2,1)S(1)} %copy-done.7, ...), custom_call_target="tpu_custom_call" | custom-call | flops 1342177280 | bytes 8388608 | tf_op jit(solution)/shard_map/attend_groups/pallas_call | solution.py:270
  89.3 3.8 %attend_bands.1 = bf16[1,640,128]{2,1,0:T(8,128)(2,1)S(1)} custom-call(s32[1]{0:T(128)} %bitcast.7.qid, s32[12]{0:T(128)S(1)} %pad_add_fusion.1.kid, s32[256]{0:T(256)S(1)} %copy-done.20, s32[16]{0:T(128)S(1)} %copy-done.23, bf16[640,640]{1,0:T(8,128)(2,1)S(1)} %copy-done.13, bf16[4,2,256,128]{3,2,1,0:T(8,128)(2,1)S(1)} %collective-permute-done.12.g1, ...), custom_call_target="tpu_custom_call" | custom-call | flops 1006632960 | bytes 8388608 | tf_op jit(solution)/shard_map/attend_bands/pallas_call | solution.py:300
  93.1 1.9 %collective-permute-done.10.o2 = bf16[640,128]{1,0:T(8,128)(2,1)S(1)} collective-permute-done((bf16[640,128]{1,0:T(8,128)(2,1)S(1)}, bf16[640,128]{1,0:T(8,128)(2,1)S(1)}, u32[]{:S(2)}, u32[]{:S(2)}) %collective-permute-start.10) | collective-permute-done | bytes 163872 | tf_op jit(solution)/shard_map/ppermute | solution.py:33
  95.0 1.7 %collective-permute-done.11.o3 = bf16[640,128]{1,0:T(8,128)(2,1)S(1)} collective-permute-done((bf16[640,128]{1,0:T(8,128)(2,1)S(1)}, bf16[640,128]{1,0:T(8,128)(2,1)S(1)}, u32[]{:S(2)}, u32[]{:S(2)}) %collective-permute-start.11) | collective-permute-done | bytes 163872 | tf_op jit(solution)/shard_map/ppermute | solution.py:33
  100.3 2.2 %project.8.refs_0_ = bf16[2,640,640]{2,1,0:T(8,128)(2,1)S(1)} custom-call(s32[2]{0:T(128)S(1)} %add_subtract_fusion.order, s32[1]{0:T(128)} %bitcast.2.pos, bf16[640,128]{1,0:T(8,128)(2,1)S(1)} %get-tuple-element.50.o0, bf16[640,128]{1,0:T(8,128)(2,1)S(1)} %collective-permute-done.9.o1, bf16[640,128]{1,0:T(8,128)(2,1)S(1)} %collective-permute-done.10.o2, ...), custom_call_target="tpu_custom_call" | custom-call | flops 1048576000 | bytes 1638400 | tf_op jit(solution)/shard_map/project/pallas_call | solution.py:334
  104.4 1.7 %collective-permute-start.22 = (bf16[320,640]{1,0:T(8,128)(2,1)S(1)}, bf16[320,640]{1,0:T(8,128)(2,1)S(1)}, u32[]{:S(2)}, u32[]{:S(2)}) collective-permute-start(bf16[320,640]{1,0:T(8,128)(2,1)S(1)} %get-tuple-element.38), channel_id=1, source_target_pairs={{0,6},{1,7},{2,0},{3,1},{4,2},{5,3},{6,4},{7,5},{8,14},{9,15},{10,... | collective-permute-start | bytes 1228808 | tf_op jit(solution)/shard_map/ppermute | solution.py:41
  106.1 2.2 %project.9 = bf16[2,640,640]{2,1,0:T(8,128)(2,1)S(1)} custom-call(s32[2]{0:T(128)S(1)} %get-tuple-element.31.order, s32[1]{0:T(128)} %bitcast.2.pos, bf16[640,128]{1,0:T(8,128)(2,1)S(1)} %get-tuple-element.50.o0, bf16[640,128]{1,0:T(8,128)(2,1)S(1)} %collective-permute-done.9.o1, bf16[640,128]{1,0:T(8,128)(2,1)S(1)} %collective-permute-done.10.o2, ...), custom_call_target="tpu_custom_call" | custom-call | flops 1048576000 | bytes 1638400 | tf_op jit(solution)/shard_map/project/pallas_call | solution.py:334
  108.8 1.9 %collective-permute-start.20 = (bf16[320,640]{1,0:T(8,128)(2,1)S(1)}, bf16[320,640]{1,0:T(8,128)(2,1)S(1)}, u32[]{:S(2)}, u32[]{:S(2)}) collective-permute-start(bf16[320,640]{1,0:T(8,128)(2,1)S(1)} %slice_bitcast_fusion.4), channel_id=1, source_target_pairs={{0,6},{1,7},{2,0},{3,1},{4,2},{5,3},{6,4},{7,5},{8,14},{9,15},{10,... | collective-permute-start | bytes 1228808 | tf_op jit(solution)/shard_map/ppermute | solution.py:41
  111.8 4.1 %collective-permute-done.18 = bf16[320,640]{1,0:T(8,128)(2,1)S(1)} collective-permute-done((bf16[320,640]{1,0:T(8,128)(2,1)S(1)}, bf16[320,640]{1,0:T(8,128)(2,1)S(1)}, u32[]{:S(2)}, u32[]{:S(2)}) %collective-permute-start.18) | collective-permute-done | bytes 409632 | tf_op jit(solution)/shard_map/ppermute | solution.py:41
  116.9 2.9 %collective-permute-start.23 = (bf16[320,640]{1,0:T(8,128)(2,1)S(1)}, bf16[320,640]{1,0:T(8,128)(2,1)S(1)}, u32[]{:S(2)}, u32[]{:S(2)}) collective-permute-start(bf16[320,640]{1,0:T(8,128)(2,1)S(1)} %fusion), channel_id=1, source_target_pairs={{0,6},{1,7},{2,0},{3,1},{4,2},{5,3},{6,4},{7,5},{8,14},{9,15},{10,... | collective-permute-start | bytes 1228808 | tf_op jit(solution)/shard_map/ppermute | solution.py:41
  121.0 4.5 %collective-permute-done.20 = bf16[320,640]{1,0:T(8,128)(2,1)S(1)} collective-permute-done((bf16[320,640]{1,0:T(8,128)(2,1)S(1)}, bf16[320,640]{1,0:T(8,128)(2,1)S(1)}, u32[]{:S(2)}, u32[]{:S(2)}) %collective-permute-start.20) | collective-permute-done | bytes 409632 | tf_op jit(solution)/shard_map/ppermute | solution.py:41
  125.5 4.1 %collective-permute-done.19 = bf16[320,640]{1,0:T(8,128)(2,1)S(1)} collective-permute-done((bf16[320,640]{1,0:T(8,128)(2,1)S(1)}, bf16[320,640]{1,0:T(8,128)(2,1)S(1)}, u32[]{:S(2)}, u32[]{:S(2)}) %collective-permute-start.19) | collective-permute-done | bytes 409632 | tf_op jit(solution)/shard_map/ppermute | solution.py:41
  129.6 3.8 %collective-permute-done.23 = bf16[320,640]{1,0:T(8,128)(2,1)S(1)} collective-permute-done((bf16[320,640]{1,0:T(8,128)(2,1)S(1)}, bf16[320,640]{1,0:T(8,128)(2,1)S(1)}, u32[]{:S(2)}, u32[]{:S(2)}) %collective-permute-start.23) | collective-permute-done | bytes 409632 | tf_op jit(solution)/shard_map/ppermute | solution.py:41
  133.4 3.6 %collective-permute-done.21 = bf16[320,640]{1,0:T(8,128)(2,1)S(1)} collective-permute-done((bf16[320,640]{1,0:T(8,128)(2,1)S(1)}, bf16[320,640]{1,0:T(8,128)(2,1)S(1)}, u32[]{:S(2)}, u32[]{:S(2)}) %collective-permute-start.21) | collective-permute-done | bytes 409632 | tf_op jit(solution)/shard_map/ppermute | solution.py:41
  (121 shorter events, 30.8 us)
Async XLA Ops:
  4.0 22.8 %collective-permute-start.2 = (bf16[5,640,128]{2,1,0:T(8,128)(2,1)S(1)}, bf16[5,640,128]{2,1,0:T(8,128)(2,1)S(1)}, u32[]{:S(2)}, u32[]{:S(2)}) collective-permute-start(bf16[5,640,128]{2,1,0:T(8,128)(2,1)S(1)} %get-tuple-element.21), channel_id=1, source_target_pairs={{0,24},{1,97},{2,26},{3,99},{4,28},{5,101},{6,30},{7,103},{8,0},{9... | collective-permute-start | bytes 2457608 | tf_op jit(solution)/shard_map/ppermute | solution.py:33
  8.2 18.7 %collective-permute-start.1 = (bf16[5,640,128]{2,1,0:T(8,128)(2,1)S(1)}, bf16[5,640,128]{2,1,0:T(8,128)(2,1)S(1)}, u32[]{:S(2)}, u32[]{:S(2)}) collective-permute-start(bf16[5,640,128]{2,1,0:T(8,128)(2,1)S(1)} %get-tuple-element.20), channel_id=1, source_target_pairs={{0,16},{1,65},{2,18},{3,67},{4,20},{5,69},{6,22},{7,71},{8,24},{9,... | collective-permute-start | bytes 2457608 | tf_op jit(solution)/shard_map/ppermute | solution.py:33
  8.2 22.3 %collective-permute-start = (bf16[5,640,128]{2,1,0:T(8,128)(2,1)S(1)}, bf16[5,640,128]{2,1,0:T(8,128)(2,1)S(1)}, u32[]{:S(2)}, u32[]{:S(2)}) collective-permute-start(bf16[5,640,128]{2,1,0:T(8,128)(2,1)S(1)} %get-tuple-element.19), channel_id=1, source_target_pairs={{0,8},{1,33},{2,10},{3,35},{4,12},{5,37},{6,14},{7,39},{8,16},{9,4... | collective-permute-start | bytes 2457608 | tf_op jit(solution)/shard_map/ppermute | solution.py:33
  31.6 21.0 %collective-permute-start.3 = (bf16[4,640,128]{2,1,0:T(8,128)(2,1)}, bf16[4,640,128]{2,1,0:T(8,128)(2,1)}, u32[]{:S(2)}, u32[]{:S(2)}) collective-permute-start(bf16[4,640,128]{2,1,0:T(8,128)(2,1)} %pad_maximum_fusion.1), channel_id=1, source_target_pairs={{0,32},{1,9},{2,34},{3,11},{4,36},{5,13},{6,38},{7,15},{8,40},{9,1... | collective-permute-start | bytes 1966088 | tf_op jit(solution)/shard_map/ppermute | solution.py:37
  34.0 18.6 %collective-permute-start.4 = (bf16[4,640,128]{2,1,0:T(8,128)(2,1)}, bf16[4,640,128]{2,1,0:T(8,128)(2,1)}, u32[]{:S(2)}, u32[]{:S(2)}) collective-permute-start(bf16[4,640,128]{2,1,0:T(8,128)(2,1)} %pad_maximum_fusion.2), channel_id=1, source_target_pairs={{0,96},{1,25},{2,98},{3,27},{4,100},{5,29},{6,102},{7,31},{8,104},... | collective-permute-start | bytes 1966088 | tf_op jit(solution)/shard_map/ppermute | solution.py:37
  36.0 20.7 %collective-permute-start.7 = (bf16[4,640,128]{2,1,0:T(8,128)(2,1)}, bf16[4,640,128]{2,1,0:T(8,128)(2,1)}, u32[]{:S(2)}, u32[]{:S(2)}) collective-permute-start(bf16[4,640,128]{2,1,0:T(8,128)(2,1)} %pad_maximum_fusion.2), channel_id=1, source_target_pairs={{0,32},{1,9},{2,34},{3,11},{4,36},{5,13},{6,38},{7,15},{8,40},{9,1... | collective-permute-start | bytes 1966088 | tf_op jit(solution)/shard_map/ppermute | solution.py:37
  36.3 20.4 %collective-permute-start.8 = (bf16[4,640,128]{2,1,0:T(8,128)(2,1)}, bf16[4,640,128]{2,1,0:T(8,128)(2,1)}, u32[]{:S(2)}, u32[]{:S(2)}) collective-permute-start(bf16[4,640,128]{2,1,0:T(8,128)(2,1)} %pad_maximum_fusion.1), channel_id=1, source_target_pairs={{0,96},{1,25},{2,98},{3,27},{4,100},{5,29},{6,102},{7,31},{8,104},... | collective-permute-start | bytes 1966088 | tf_op jit(solution)/shard_map/ppermute | solution.py:37
  52.7 25.4 %collective-permute-start.5 = (bf16[4,640,128]{2,1,0:T(8,128)(2,1)}, bf16[4,640,128]{2,1,0:T(8,128)(2,1)}, u32[]{:S(2)}, u32[]{:S(2)}) collective-permute-start(bf16[4,640,128]{2,1,0:T(8,128)(2,1)} %get-tuple-element.23.refs_4_), channel_id=1, source_target_pairs={{0,32},{1,9},{2,34},{3,11},{4,36},{5,13},{6,38},{7,15},{8,40},{9,1... | collective-permute-start | bytes 1966088 | tf_op jit(solution)/shard_map/ppermute | solution.py:37
  52.7 25.4 %collective-permute-start.6 = (bf16[4,640,128]{2,1,0:T(8,128)(2,1)}, bf16[4,640,128]{2,1,0:T(8,128)(2,1)}, u32[]{:S(2)}, u32[]{:S(2)}) collective-permute-start(bf16[4,640,128]{2,1,0:T(8,128)(2,1)} %get-tuple-element.24.refs_7_), channel_id=1, source_target_pairs={{0,96},{1,25},{2,98},{3,27},{4,100},{5,29},{6,102},{7,31},{8,104},... | collective-permute-start | bytes 1966088 | tf_op jit(solution)/shard_map/ppermute | solution.py:37
  60.3 27.7 %collective-permute-start.12 = (bf16[4,2,256,128]{3,2,1,0:T(8,128)(2,1)}, bf16[4,2,256,128]{3,2,1,0:T(8,128)(2,1)S(1)}, u32[]{:S(2)}, u32[]{:S(2)}) collective-permute-start(bf16[4,2,256,128]{3,2,1,0:T(8,128)(2,1)} %get-tuple-element.28), channel_id=1, source_target_pairs={{0,32},{1,9},{2,34},{3,11},{4,36},{5,13},{6,38},{7,15},{8,40},{9,1... | collective-permute-start | bytes 1572872 | tf_op jit(solution)/shard_map/ppermute | solution.py:37
  60.3 28.9 %collective-permute-start.13 = (bf16[4,2,256,128]{3,2,1,0:T(8,128)(2,1)}, bf16[4,2,256,128]{3,2,1,0:T(8,128)(2,1)S(1)}, u32[]{:S(2)}, u32[]{:S(2)}) collective-permute-start(bf16[4,2,256,128]{3,2,1,0:T(8,128)(2,1)} %get-tuple-element.29), channel_id=1, source_target_pairs={{0,64},{1,17},{2,66},{3,19},{4,68},{5,21},{6,70},{7,23},{8,72},{9,... | collective-permute-start | bytes 1572872 | tf_op jit(solution)/shard_map/ppermute | solution.py:37
  61.8 27.5 %collective-permute-start.14 = (bf16[4,2,256,128]{3,2,1,0:T(8,128)(2,1)}, bf16[4,2,256,128]{3,2,1,0:T(8,128)(2,1)S(1)}, u32[]{:S(2)}, u32[]{:S(2)}) collective-permute-start(bf16[4,2,256,128]{3,2,1,0:T(8,128)(2,1)} %get-tuple-element.30), channel_id=1, source_target_pairs={{0,96},{1,25},{2,98},{3,27},{4,100},{5,29},{6,102},{7,31},{8,104},... | collective-permute-start | bytes 1572872 | tf_op jit(solution)/shard_map/ppermute | solution.py:37
  87.1 6.0 %collective-permute-start.9 = (bf16[640,128]{1,0:T(8,128)(2,1)S(1)}, bf16[640,128]{1,0:T(8,128)(2,1)S(1)}, u32[]{:S(2)}, u32[]{:S(2)}) collective-permute-start(bf16[640,128]{1,0:T(8,128)(2,1)S(1)} %get-tuple-element.49), channel_id=1, source_target_pairs={{0,24},{1,97},{2,26},{3,99},{4,28},{5,101},{6,30},{7,103},{8,0},{9... | collective-permute-start | bytes 491528 | tf_op jit(solution)/shard_map/ppermute | solution.py:33
  88.0 6.9 %collective-permute-start.10 = (bf16[640,128]{1,0:T(8,128)(2,1)S(1)}, bf16[640,128]{1,0:T(8,128)(2,1)S(1)}, u32[]{:S(2)}, u32[]{:S(2)}) collective-permute-start(bf16[640,128]{1,0:T(8,128)(2,1)S(1)} %get-tuple-element.48), channel_id=1, source_target_pairs={{0,16},{1,65},{2,18},{3,67},{4,20},{5,69},{6,22},{7,71},{8,24},{9,... | collective-permute-start | bytes 491528 | tf_op jit(solution)/shard_map/ppermute | solution.py:33
  88.0 8.6 %collective-permute-start.11 = (bf16[640,128]{1,0:T(8,128)(2,1)S(1)}, bf16[640,128]{1,0:T(8,128)(2,1)S(1)}, u32[]{:S(2)}, u32[]{:S(2)}) collective-permute-start(bf16[640,128]{1,0:T(8,128)(2,1)S(1)} %get-tuple-element.47), channel_id=1, source_target_pairs={{0,8},{1,33},{2,10},{3,35},{4,12},{5,37},{6,14},{7,39},{8,16},{9,4... | collective-permute-start | bytes 491528 | tf_op jit(solution)/shard_map/ppermute | solution.py:33
  97.6 2.4 %collective-permute-start.15 = (bf16[1,640,640]{2,1,0:T(8,128)(2,1)S(1)}, bf16[1,640,640]{2,1,0:T(8,128)(2,1)S(1)}, u32[]{:S(2)}, u32[]{:S(2)}) collective-permute-start(bf16[1,640,640]{2,1,0:T(8,128)(2,1)S(1)} %project.6.refs_0_), channel_id=1, source_target_pairs={{0,1},{1,0},{2,3},{3,2},{4,5},{5,4},{6,7},{7,6},{8,9},{9,8},{10,11... | collective-permute-start | bytes 2457608 | tf_op jit(solution)/shard_map/ppermute | solution.py:45
  102.5 5.9 %collective-permute-start.16 = (bf16[2,640,640]{2,1,0:T(8,128)(2,1)S(1)}, bf16[2,640,640]{2,1,0:T(8,128)(2,1)S(1)}, u32[]{:S(2)}, u32[]{:S(2)}) collective-permute-start(bf16[2,640,640]{2,1,0:T(8,128)(2,1)S(1)} %project.8.refs_0_), channel_id=1, source_target_pairs={{0,1},{1,0},{2,3},{3,2},{4,5},{5,4},{6,7},{7,6},{8,9},{9,8},{10,11... | collective-permute-start | bytes 4915208 | tf_op jit(solution)/shard_map/ppermute | solution.py:45
  102.8 13.1 %collective-permute-start.18 = (bf16[320,640]{1,0:T(8,128)(2,1)S(1)}, bf16[320,640]{1,0:T(8,128)(2,1)S(1)}, u32[]{:S(2)}, u32[]{:S(2)}) collective-permute-start(bf16[320,640]{1,0:T(8,128)(2,1)S(1)} %get-tuple-element.37), channel_id=1, source_target_pairs={{0,2},{1,3},{2,4},{3,5},{4,6},{5,7},{6,0},{7,1},{8,10},{9,11},{10,... | collective-permute-start | bytes 1228808 | tf_op jit(solution)/shard_map/ppermute | solution.py:41
  104.4 12.3 %collective-permute-start.22 = (bf16[320,640]{1,0:T(8,128)(2,1)S(1)}, bf16[320,640]{1,0:T(8,128)(2,1)S(1)}, u32[]{:S(2)}, u32[]{:S(2)}) collective-permute-start(bf16[320,640]{1,0:T(8,128)(2,1)S(1)} %get-tuple-element.38), channel_id=1, source_target_pairs={{0,6},{1,7},{2,0},{3,1},{4,2},{5,3},{6,4},{7,5},{8,14},{9,15},{10,... | collective-permute-start | bytes 1228808 | tf_op jit(solution)/shard_map/ppermute | solution.py:41
  108.8 16.7 %collective-permute-start.20 = (bf16[320,640]{1,0:T(8,128)(2,1)S(1)}, bf16[320,640]{1,0:T(8,128)(2,1)S(1)}, u32[]{:S(2)}, u32[]{:S(2)}) collective-permute-start(bf16[320,640]{1,0:T(8,128)(2,1)S(1)} %slice_bitcast_fusion.4), channel_id=1, source_target_pairs={{0,6},{1,7},{2,0},{3,1},{4,2},{5,3},{6,4},{7,5},{8,14},{9,15},{10,... | collective-permute-start | bytes 1228808 | tf_op jit(solution)/shard_map/ppermute | solution.py:41
  111.7 9.1 %collective-permute-start.17 = (bf16[1,640,640]{2,1,0:T(8,128)(2,1)S(1)}, bf16[1,640,640]{2,1,0:T(8,128)(2,1)S(1)}, u32[]{:S(2)}, u32[]{:S(2)}) collective-permute-start(bf16[1,640,640]{2,1,0:T(8,128)(2,1)S(1)} %project.10.refs_0_), channel_id=1, source_target_pairs={{0,1},{1,0},{2,3},{3,2},{4,5},{5,4},{6,7},{7,6},{8,9},{9,8},{10,11... | collective-permute-start | bytes 2457608 | tf_op jit(solution)/shard_map/ppermute | solution.py:45
  116.0 13.7 %collective-permute-start.19 = (bf16[320,640]{1,0:T(8,128)(2,1)S(1)}, bf16[320,640]{1,0:T(8,128)(2,1)S(1)}, u32[]{:S(2)}, u32[]{:S(2)}) collective-permute-start(bf16[320,640]{1,0:T(8,128)(2,1)S(1)} %fusion.3), channel_id=1, source_target_pairs={{0,2},{1,3},{2,4},{3,5},{4,6},{5,7},{6,0},{7,1},{8,10},{9,11},{10,... | collective-permute-start | bytes 1228808 | tf_op jit(solution)/shard_map/ppermute | solution.py:41
  116.9 16.6 %collective-permute-start.23 = (bf16[320,640]{1,0:T(8,128)(2,1)S(1)}, bf16[320,640]{1,0:T(8,128)(2,1)S(1)}, u32[]{:S(2)}, u32[]{:S(2)}) collective-permute-start(bf16[320,640]{1,0:T(8,128)(2,1)S(1)} %fusion), channel_id=1, source_target_pairs={{0,6},{1,7},{2,0},{3,1},{4,2},{5,3},{6,4},{7,5},{8,14},{9,15},{10,... | collective-permute-start | bytes 1228808 | tf_op jit(solution)/shard_map/ppermute | solution.py:41
  119.8 17.2 %collective-permute-start.21 = (bf16[320,640]{1,0:T(8,128)(2,1)S(1)}, bf16[320,640]{1,0:T(8,128)(2,1)S(1)}, u32[]{:S(2)}, u32[]{:S(2)}) collective-permute-start(bf16[320,640]{1,0:T(8,128)(2,1)S(1)} %slice_bitcast_fusion.2), channel_id=1, source_target_pairs={{0,2},{1,3},{2,4},{3,5},{4,6},{5,7},{6,0},{7,1},{8,10},{9,11},{10,... | collective-permute-start | bytes 1228808 | tf_op jit(solution)/shard_map/ppermute | solution.py:41
  (28 other events, 244.3 us)

commit v3 on v2

v3 whole, which is shorter than its diff:
```python
import functools

import jax
import jax.numpy as jnp
from jax import lax
from jax.experimental import pallas as pl
from jax.experimental.pallas import tpu as pltpu
from jax.sharding import PartitionSpec as P

HD = 128
BLOCK = 128
NB = 5
FT = 640
FRAMES = 16
SIDE = 4
ROWS = 128
LOG2_SCALE = 1.4426950408889634 / HD**0.5
NT = (((1,), (1,)), ((), ()))
NN = (((1,), (0,)), ((), ()))
BOTH = ("frame", "head")


def pairs(move):
    out = []
    for i in range(128):
        frame, head = divmod(i, 8)
        x, z, y, c = move(*divmod(frame, 4), *divmod(head, 2))
        out.append((i, (x % 4 * 4 + z % 4) * 8 + y % 4 * 2 + c))
    return out


def line_shift(v, s):
    return lax.ppermute(v, BOTH, pairs(lambda x, z, y, c: (x, z + s, y, c) if c == 0 else (x + s, z, y, c)))


def cross_shift(v, s):
    return lax.ppermute(v, BOTH, pairs(lambda x, z, y, c: (x + s, z, y, c) if c == 0 else (x, z + s, y, c)))


def y_shift(v, s):
    return lax.ppermute(v, BOTH, pairs(lambda x, z, y, c: (x, z, y + s, c)))


def core_swap(v):
    return lax.ppermute(v, BOTH, pairs(lambda x, z, y, c: (x, z, y, 1 - c)))


ANY = pl.BlockSpec(memory_space=pl.ANY)
VMEM = pl.BlockSpec(memory_space=pltpu.VMEM)
LIMIT = 20 << 20


def in_hbm(*arrays):
    return [pltpu.with_memory_space_constraint(v, pltpu.HBM) for v in arrays]


def pick_kernel(pos, q_any, k_any, v_any, *refs):
    outs, (q, k, v, sems) = refs[:SIDE], refs[SIDE:]
    rows = FT // 5
    copies = []
    for i in range(5):
        part = pl.ds(i * rows, rows)
        for j, (source, target) in enumerate(((q_any, q), (k_any, k), (v_any, v))):
            copies.append(pltpu.make_async_copy(source.at[part, :], target.at[part, :], sems.at[3 * i + j]))
    for copy in copies:
        copy.start()
    for i in range(5):
        for copy in copies[3 * i : 3 * i + 3]:
            copy.wait()
        part = slice(i * rows, (i + 1) * rows)
        for s, out in enumerate(outs):
            head = lax.rem(pos[0] + s, SIDE)
            columns = pl.ds(pl.multiple_of(head * HD, HD), HD)
            out[0, part, :] = q[part, columns]
            out[1, part, :] = k[part, columns]
            out[2, part, :] = v[part, columns]
            out[3, part, :] = k[part, 4 * HD :]
            out[4, part, :] = v[part, 4 * HD :]


def pick(pos, queries, keys, values):
    return pl.pallas_call(
        pick_kernel,
        in_specs=[pl.BlockSpec(memory_space=pltpu.SMEM)] + [ANY] * 3,
        out_specs=[VMEM] * SIDE,
        out_shape=[pltpu.VMEM((5, FT, HD), jnp.bfloat16)] * SIDE,
        scratch_shapes=[pltpu.VMEM((FT, 5 * HD), jnp.bfloat16)] * 3 + [pltpu.SemaphoreType.DMA((15,))],
        compiler_params=pltpu.CompilerParams(vmem_limit_bytes=LIMIT),
        name="pick",
    )(pos, *in_hbm(queries, keys, values))


def stack_kernel(*refs):
    pieces, (q, kv, k_last, v_last, sems) = refs[:SIDE], refs[SIDE:]
    copies = []
    for s, piece in enumerate(pieces):
        targets = (q.at[s], kv.at[s], kv.at[SIDE + s], k_last.at[s], v_last.at[s])
        for j, target in enumerate(targets):
            copies.append(pltpu.make_async_copy(piece.at[j], target, sems.at[s, j]))
    for copy in copies:
        copy.start()
    for copy in copies:
        copy.wait()


def stack(pieces):
    shape = (SIDE, FT, HD)
    both = (2 * SIDE, FT, HD)
    return pl.pallas_call(
        stack_kernel,
        in_specs=[VMEM] * SIDE,
        out_specs=[ANY] * 4,
        out_shape=[pltpu.HBM(s, jnp.bfloat16) for s in (shape, both, shape, shape)],
        scratch_shapes=[pltpu.SemaphoreType.DMA((SIDE, 5))],
        compiler_params=pltpu.CompilerParams(vmem_limit_bytes=LIMIT),
        name="stack",
    )(*pieces)


def block_rows(n):
    return pl.ds(pl.multiple_of(n * BLOCK, BLOCK), BLOCK)


def place(n, keys, values, row, kc, vc, valid=None, stand_in=None):
    ones = lax.broadcasted_iota(jnp.int32, (BLOCK, HD), 1) == 0
    at = slice(n * BLOCK, (n + 1) * BLOCK)
    if valid is None:
        kc[at, :] = keys[block_rows(row), :]
        vc[at, 0:HD] = values[block_rows(row), :]
        vc[at, HD:] = ones.astype(jnp.bfloat16)
    else:
        kc[at, :] = keys[block_rows(jnp.where(valid, row, stand_in)), :]
        taken = values[block_rows(row), :]
        vc[at, 0:HD] = jnp.where(valid, taken, jnp.zeros_like(taken))
        vc[at, HD:] = jnp.where(ones & valid, 1.0, 0.0).astype(jnp.bfloat16)


def band_of(a, b, bs, bw):
    own = a == b
    first = jnp.where(own, 0, bs[a * FRAMES + b])
    second = jnp.where(first == NB - 1, 0, first + 1)
    return first, second, own | (bw[jnp.abs(a - b)] == 2)


def attend_to(q, kc, vc, state, emit):
    kk, vv = kc[...], vc[...]
    steps = FT // ROWS

    def score(r):
        return lax.dot_general(q[r * ROWS : (r + 1) * ROWS, :], kk, NT, preferred_element_type=jnp.float32)

    scores = score(0)
    for r in range(steps):
        later = score(r + 1) if r + 1 < steps else None
        rows = slice(r * ROWS, (r + 1) * ROWS)
        top = jnp.max(scores, axis=1, keepdims=True) * LOG2_SCALE
        if state:
            level = jnp.broadcast_to(state[1][0, r : r + 1, :], (ROWS, HD)).T[:, 0:1]
            top = jnp.maximum(top, level)
        probs = jnp.exp2(scores * LOG2_SCALE - top).astype(jnp.bfloat16)
        mixed = lax.dot_general(probs, vv, NN, preferred_element_type=jnp.float32)
        weighted, totals = mixed[:, 0:HD], mixed[:, HD : HD + 1]
        if state:
            share = jnp.exp2(level - top)
            weighted = weighted + state[0][0, rows, :].astype(jnp.float32) * share
            totals = totals + share
        emit(r, (weighted / totals).astype(jnp.bfloat16), top, totals)
        scores = later


def put_state(out, levels):
    def emit(r, result, top, totals):
        out[0, r * ROWS : (r + 1) * ROWS, :] = result
        level = top + jnp.log2(totals)
        levels[0, r : r + 1, :] = jnp.broadcast_to(level, (ROWS, HD)).T[0:1, :]

    return emit


def put_result(out):
    def emit(r, result, top, totals):
        out[0, r * ROWS : (r + 1) * ROWS, :] = result

    return emit


def line_kernel(qid, kid, bs, bw, q, kv, out, levels, kc, vc):
    i = pl.program_id(0)
    for s in range(SIDE):
        first, second, valid = band_of(qid[i], kid[s], bs, bw)
        place(2 * s, kv.at[s], kv.at[SIDE + s], first, kc, vc)
        place(2 * s + 1, kv.at[s], kv.at[SIDE + s], second, kc, vc, valid, first)
    for j in range(2, NB):
        place(2 * SIDE + j - 2, kv.at[i], kv.at[SIDE + i], j, kc, vc)
    attend_to(q.at[0], kc, vc, None, put_state(out, levels))


def last_line_kernel(qid, kid, bs, bw, q, keys, values, after, out, levels, s1, s2, s3, kc, vc):
    del after
    for s in range(SIDE):
        for i, sent in enumerate((s1, s2, s3)):
            first, second, unused = band_of(qid[i + 1], kid[s], bs, bw)
            for j, source in enumerate((keys, values)):
                sent[s, j, 0:BLOCK, :] = source[s, block_rows(first), :]
                sent[s, j, BLOCK:, :] = source[s, block_rows(second), :]
    for j in range(NB):
        place(j, keys.at[0], values.at[0], j, kc, vc)
    for s in range(1, SIDE):
        first, second, valid = band_of(qid[0], kid[s], bs, bw)
        n = NB + 2 * (s - 1)
        place(n, keys.at[s], values.at[s], first, kc, vc)
        place(n + 1, keys.at[s], values.at[s], second, kc, vc, valid, first)
    attend_to(q, kc, vc, None, put_state(out, levels))


ITEM = pl.BlockSpec((1, FT, HD), lambda i, *_: (i, 0, 0))
LEVEL = pl.BlockSpec((1, 8, HD), lambda i, *_: (i, 0, 0))


def cost(items, blocks):
    pairs_read = items * FT * blocks * BLOCK
    return pl.CostEstimate(flops=pairs_read * 4 * HD, bytes_accessed=8 << 20, transcendentals=pairs_read)


def packed(blocks):
    return [pltpu.VMEM((blocks * BLOCK, HD), jnp.bfloat16), pltpu.VMEM((blocks * BLOCK, 2 * HD), jnp.bfloat16)]


def state_shape(items):
    return [pltpu.HBM((items, FT, HD), jnp.bfloat16), pltpu.HBM((items, 8, HD), jnp.float32)]


def attend_line(qid, kid, bs, bw, q, kv):
    blocks = 2 * SIDE + NB - 2
    return pl.pallas_call(
        line_kernel,
        grid_spec=pltpu.PrefetchScalarGridSpec(
            num_scalar_prefetch=4,
            grid=(SIDE,),
            in_specs=[ITEM, pl.BlockSpec(kv.shape, lambda i, *_: (0, 0, 0))],
            out_specs=[ITEM, LEVEL],
            scratch_shapes=packed(blocks),
        ),
        out_shape=state_shape(SIDE),
        compiler_params=pltpu.CompilerParams(vmem_limit_bytes=LIMIT),
        cost_estimate=cost(SIDE, blocks),
        name="attend_line",
    )(qid, kid, bs, bw, *in_hbm(q, kv))


def attend_last_line(qid, kid, bs, bw, queries, keys, values, after):
    blocks = 2 * SIDE + NB - 2
    whole = pl.BlockSpec((SIDE, FT, HD), lambda i, *_: (0, 0, 0))
    sent = (SIDE, 2, 2 * BLOCK, HD)
    return pl.pallas_call(
        last_line_kernel,
        grid_spec=pltpu.PrefetchScalarGridSpec(
            num_scalar_prefetch=4,
            grid=(1,),
            in_specs=[pl.BlockSpec((FT, HD), lambda i, *_: (0, SIDE)), whole, whole, ANY],
            out_specs=[ITEM, LEVEL] + [pl.BlockSpec(sent, lambda i, *_: (0, 0, 0, 0))] * 3,
            scratch_shapes=packed(blocks),
        ),
        out_shape=state_shape(1) + [pltpu.HBM(sent, jnp.bfloat16)] * 3,
        compiler_params=pltpu.CompilerParams(vmem_limit_bytes=LIMIT),
        cost_estimate=cost(1, blocks),
        name="attend_last_line",
    )(qid, kid, bs, bw, *in_hbm(queries, keys, values, after))


def groups_kernel(count, finished, qid, kid, bs, bw, q, *refs):
    groups, (before, levels), results, (kc, vc) = refs[:count], refs[count : count + 2], refs[count + 2 : -2], refs[-2:]
    i = pl.program_id(0)
    for d, group in enumerate(groups):
        for s in range(SIDE):
            n = d * SIDE + s
            keys, values = group.at[s], group.at[SIDE + s]
            first, second, valid = band_of(qid[i], kid[n], bs, bw)
            place(2 * n, keys, values, first, kc, vc)
            place(2 * n + 1, keys, values, second, kc, vc, valid, first)
    if finished:
        out, token = results
        token[...] = jnp.zeros(token.shape, token.dtype)
        emit = put_result(out)
    else:
        emit = put_state(*results)
    attend_to(q.at[0], kc, vc, (before, levels), emit)


def attend_groups(qid, kid, bs, bw, q, groups, state, finished):
    blocks = 2 * SIDE * len(groups)
    if finished:
        out_specs = [ITEM, pl.BlockSpec((8, HD), lambda i, *_: (0, 0))]
        out_shape = [jax.ShapeDtypeStruct((SIDE, FT, HD), jnp.bfloat16), pltpu.HBM((8, HD), jnp.float32)]
    else:
        out_specs, out_shape = [ITEM, LEVEL], state_shape(SIDE)
    return pl.pallas_call(
        functools.partial(groups_kernel, len(groups), finished),
        grid_spec=pltpu.PrefetchScalarGridSpec(
            num_scalar_prefetch=4,
            grid=(SIDE,),
            in_specs=[ITEM] + [pl.BlockSpec(g.shape, lambda i, *_: (0, 0, 0)) for g in groups] + [ITEM, LEVEL],
            out_specs=out_specs,
            scratch_shapes=packed(blocks),
        ),
        out_shape=out_shape,
        compiler_params=pltpu.CompilerParams(vmem_limit_bytes=LIMIT),
        cost_estimate=cost(SIDE, blocks),
        name="attend_groups",
    )(qid, kid, bs, bw, *in_hbm(q), *groups, *in_hbm(*state))


def bands_attend_kernel(qid, kid, bs, bw, q, g1, g2, g3, before, levels, after, out, kc, vc):
    del after
    for d, group in enumerate((g1, g2, g3)):
        for s in range(SIDE):
            n = d * SIDE + s
            valid = band_of(qid[0], kid[n], bs, bw)[2]
            place(2 * n, group.at[s, 0], group.at[s, 1], 0, kc, vc)
            place(2 * n + 1, group.at[s, 0], group.at[s, 1], 1, kc, vc, valid, 0)
    attend_to(q, kc, vc, (before, levels), put_result(out))


def attend_bands(qid, kid, bs, bw, queries, groups, state, after):
    blocks = 2 * SIDE * len(groups)
    return pl.pallas_call(
        bands_attend_kernel,
        grid_spec=pltpu.PrefetchScalarGridSpec(
            num_scalar_prefetch=4,
            grid=(1,),
            in_specs=[pl.BlockSpec((FT, HD), lambda i, *_: (0, SIDE))]
            + [pl.BlockSpec(g.shape, lambda i, *_: (0, 0, 0, 0)) for g in groups]
            + [ITEM, LEVEL, ANY],
            out_specs=ITEM,
            scratch_shapes=packed(blocks),
        ),
        out_shape=jax.ShapeDtypeStruct((1, FT, HD), jnp.bfloat16),
        compiler_params=pltpu.CompilerParams(vmem_limit_bytes=LIMIT),
        cost_estimate=cost(1, blocks),
        name="attend_bands",
    )(qid, kid, bs, bw, *in_hbm(queries), *groups, *in_hbm(*state, after))


def project_kernel(order, pos, o0, o1, o2, o3, o4, w_ref, *refs):
    y_ref, att = refs[-2:]

    @pl.when(pl.program_id(0) == 0)
    def _():
        for s, o in enumerate((o0, o1, o2, o3)):
            head = lax.rem(pos[0] + s, SIDE)
            att[:, pl.ds(pl.multiple_of(head * HD, HD), HD)] = o[...]
        att[:, 4 * HD :] = o4[...]

    y_ref[0] = jnp.dot(att[...], w_ref[...], preferred_element_type=jnp.float32).astype(jnp.bfloat16)


def project(order, pos, outs, weight, *after):
    count = order.shape[0]
    width = weight.shape[1] // 8
    whole = pl.BlockSpec((FT, HD), lambda i, *_: (0, 0))
    return pl.pallas_call(
        project_kernel,
        grid_spec=pltpu.PrefetchScalarGridSpec(
            num_scalar_prefetch=2,
            grid=(count,),
            in_specs=[whole] * 5
            + [pl.BlockSpec((5 * HD, width), lambda i, order, pos: (0, order[i]))]
            + [ANY] * len(after),
            out_specs=pl.BlockSpec((1, FT, width), lambda i, *_: (i, 0, 0)),
            scratch_shapes=[pltpu.VMEM((FT, 5 * HD), jnp.bfloat16)],
        ),
        out_shape=jax.ShapeDtypeStruct((count, FT, width), jnp.bfloat16),
        compiler_params=pltpu.CompilerParams(vmem_limit_bytes=LIMIT),
        cost_estimate=pl.CostEstimate(
            flops=2 * count * FT * 5 * HD * width, bytes_accessed=count * FT * width * 2, transcendentals=0
        ),
        name="project",
    )(order, pos, *outs, *in_hbm(weight), *after)


def add(*terms):
    total = terms[0].astype(jnp.float32)
    for t in terms[1:]:
        total = total + t.astype(jnp.float32)
    return total.astype(jnp.bfloat16)


def finish_kernel(own, more_up, plain_up, more_down, plain_down, out):
    half = FT // 2
    wide = lambda v: v.astype(jnp.float32)
    out[0:half, :] = (wide(own[0:half, :]) + wide(more_up[...]) + wide(plain_down[...])).astype(jnp.bfloat16)
    out[half:, :] = (wide(own[half:, :]) + wide(more_down[...]) + wide(plain_up[...])).astype(jnp.bfloat16)


def finish(*args):
    return pl.pallas_call(
        finish_kernel,
        in_specs=[VMEM] * 5,
        out_specs=pl.BlockSpec(args[0].shape, lambda: (0, 0)),
        out_shape=jax.ShapeDtypeStruct(args[0].shape, jnp.bfloat16),
        compiler_params=pltpu.CompilerParams(vmem_limit_bytes=LIMIT),
        name="finish",
    )(*args)


def shards(queries, key_rows, value_rows, out_weight, band_start, band_width):
    frame, head = lax.axis_index("frame"), lax.axis_index("head")
    x, z = frame // SIDE, frame % SIDE
    y, core = head // 2, head % 2
    line = jnp.where(core == 0, z, x)
    ring = jnp.arange(SIDE, dtype=jnp.int32)

    def frames_at(cross, along):
        return jnp.where(
            core == 0,
            (x - cross) % SIDE * SIDE + (z - along) % SIDE,
            (x - along) % SIDE * SIDE + (z - cross) % SIDE,
        )

    f0, f1, f2, f3 = [frames_at(d, ring) for d in range(SIDE)]
    bs, bw = band_start.reshape(-1), band_width

    pieces = pick(line[None], queries, key_rows, value_rows)
    pieces = [pieces[0]] + [line_shift(pieces[s], s) for s in range(1, SIDE)]
    q, kv, k_last, v_last = stack(pieces)

    groups = [cross_shift(kv, s) for s in range(1, SIDE)]
    state = attend_line(f0, f0, bs, bw, q, kv)

    here_and_across = frames_at(-ring, 0)
    *last_state, s_1, s_2, s_3 = attend_last_line(here_and_across, f0, bs, bw, queries, k_last, v_last, state[0])
    last = [cross_shift(sent, s) for s, sent in ((1, s_1), (2, s_2), (3, s_3))]

    state = attend_groups(f0, f1, bs, bw, q, groups[:1], state, False)
    o_main, token = attend_groups(f0, jnp.concatenate([f2, f3]), bs, bw, q, groups[1:], state, True)
    outs = [o_main[0]] + [line_shift(o_main[s], SIDE - s) for s in range(1, SIDE)]
    o_last = attend_bands(frame[None], jnp.concatenate([f1, f2, f3]), bs, bw, queries, last, last_state, token)
    outs.append(o_last[0])

    def summed(ahead, *after):
        target = (y + jnp.array(ahead, jnp.int32)) % SIDE * 2
        away = project(target + 1 - core, line[None], outs, out_weight, *after)
        given = core_swap(away)
        kept = project(target + core, line[None], outs, out_weight, away)
        return [add(kept[i], given[i]) for i in range(len(ahead))]

    half = FT // 2
    (two,) = summed([2])
    from_down, from_up = y_shift(two[:half], 1), y_shift(two[half:], 3)
    up, down = summed([1, 3], two)
    plain_up, plain_down = y_shift(up[half:], 1), y_shift(down[:half], 3)
    (own,) = summed([0], up)
    more_up, more_down = y_shift(add(up[:half], from_down), 1), y_shift(add(down[half:], from_up), 3)
    return finish(own, more_up, plain_up, more_down, plain_down)


def solution(mesh):
    return jax.shard_map(
        shards,
        mesh=mesh,
        in_specs=(
            P("frame", "head"),
            P("frame", "head"),
            P("frame", "head"),
            P("head", None),
            P(),
            P(),
        ),
        out_specs=P("frame", "head"),
        check_vma=False,
    )
```

time: 139 us -> 135 us (0.971)
  the two profiles are of different devices: /device:TPU:0 before, /device:TPU:32 now
where the time goes in v3:
time: 135 us; the launch traced here: 132 us
  Pallas kernels  60.4 us (45%)
  waiting for transfers between devices  43 us (32%)
  starting transfers between devices  27.2 us (20%)
    pallas_call x2, Pallas kernels, attend_groups(): pl.pallas_call(functools.partial(groups_kernel, len(groups), finished), g...  19.7 us
    ppermute x6, waiting for transfers between devices, line_shift(): lax.ppermute(v, BOTH, pairs(lambda x, z, y, c: (x, z + s, y, c) if c == 0...  19.3 us
    ppermute x6, waiting for transfers between devices, y_shift(): return lax.ppermute(v, BOTH, pairs(lambda x, z, y, c: (x, z, y + s, c)))  19.1 us
    pallas_call x6, Pallas kernels, project(): pl.pallas_call(project_kernel, grid_spec=pltpu.PrefetchScalarGridSpec(num...  16 us
    pallas_call x1, Pallas kernels, attend_line(): pl.pallas_call(line_kernel, grid_spec=pltpu.PrefetchScalarGridSpec(num_sc...  10.2 us
    ppermute x6, starting transfers between devices, line_shift(): lax.ppermute(v, BOTH, pairs(lambda x, z, y, c: (x, z + s, y, c) if c == 0...  9.87 us
    ppermute x6, starting transfers between devices, cross_shift(): lax.ppermute(v, BOTH, pairs(lambda x, z, y, c: (x + s, z, y, c) if c == 0...  9.47 us
    ppermute x6, starting transfers between devices, y_shift(): return lax.ppermute(v, BOTH, pairs(lambda x, z, y, c: (x, z, y + s, c)))  7.19 us
  transfers between devices with their start and end apart: 21, of which 9 were waited for; matrix products, arithmetic and copies ran while one was open for 1% of the time, Pallas kernels for 37%

profile of v3, /device:TPU:32, one launch (start us, length us, event | category | flops | bytes accessed | tf_op | source)
XLA Modules:
  0.0 132.4 jit_solution(4023115280032491359)
XLA Ops:
  0.0 2.0 %pick.1 = (bf16[5,640,128]{2,1,0:T(8,128)(2,1)S(1)}, bf16[5,640,128]{2,1,0:T(8,128)(2,1)S(1)}, bf16[5,640,128]{2,1,0:T(8,128)(2,1)S(1)}, bf16[5,640,128]{2,1,0:T(8,128)(2,1)S(1)}) custom-call(s32[1]{0:T(128)} %bitcast.2.pos, bf16[640,640]{1,0:T(8,128)(2,1)} %q.3, bf16[640,640]{1,0:T(8,128)(2,1)} %k_any.1, bf16[640,640]{1,0:T(8,128)(2,1)} %v_any.1), custom_call_target="tpu_custom_call" | custom-call | tf_op jit(solution)/shard_map/pick/pallas_call | solution.py:82
  2.0 2.0 %collective-permute-start = (bf16[5,640,128]{2,1,0:T(8,128)(2,1)S(1)}, bf16[5,640,128]{2,1,0:T(8,128)(2,1)S(1)}, u32[]{:S(2)}, u32[]{:S(2)}) collective-permute-start(bf16[5,640,128]{2,1,0:T(8,128)(2,1)S(1)} %get-tuple-element.25), channel_id=1, source_target_pairs={{0,8},{1,33},{2,10},{3,35},{4,12},{5,37},{6,14},{7,39},{8,16},{9,4... | collective-permute-start | bytes 2457608 | tf_op jit(solution)/shard_map/ppermute | solution.py:33
  5.1 2.5 %collective-permute-start.2 = (bf16[5,640,128]{2,1,0:T(8,128)(2,1)S(1)}, bf16[5,640,128]{2,1,0:T(8,128)(2,1)S(1)}, u32[]{:S(2)}, u32[]{:S(2)}) collective-permute-start(bf16[5,640,128]{2,1,0:T(8,128)(2,1)S(1)} %get-tuple-element.27), channel_id=1, source_target_pairs={{0,24},{1,97},{2,26},{3,99},{4,28},{5,101},{6,30},{7,103},{8,0},{9... | collective-permute-start | bytes 2457608 | tf_op jit(solution)/shard_map/ppermute | solution.py:33
  7.6 15.0 %collective-permute-done.refs_1_ = bf16[5,640,128]{2,1,0:T(8,128)(2,1)S(1)} collective-permute-done((bf16[5,640,128]{2,1,0:T(8,128)(2,1)S(1)}, bf16[5,640,128]{2,1,0:T(8,128)(2,1)S(1)}, u32[]{:S(2)}, u32[]{:S(2)}) %collective-permute-start) | collective-permute-done | bytes 819232 | tf_op jit(solution)/shard_map/ppermute | solution.py:33
  22.6 3.6 %collective-permute-done.2.refs_3_ = bf16[5,640,128]{2,1,0:T(8,128)(2,1)S(1)} collective-permute-done((bf16[5,640,128]{2,1,0:T(8,128)(2,1)S(1)}, bf16[5,640,128]{2,1,0:T(8,128)(2,1)S(1)}, u32[]{:S(2)}, u32[]{:S(2)}) %collective-permute-start.2) | collective-permute-done | bytes 819232 | tf_op jit(solution)/shard_map/ppermute | solution.py:33
  33.5 10.2 %attend_line.1 = (bf16[4,640,128]{2,1,0:T(8,128)(2,1)}, f32[4,8,128]{2,1,0:T(8,128)}) custom-call(s32[4]{0:T(128)S(1)} %broadcast_select_fusion.4.qid.kid, s32[4]{0:T(128)S(1)} %broadcast_select_fusion.4.qid.kid, s32[256]{0:T(256)S(1)} %reshape.33.bs, s32[16]{0:T(128)S(1)} %copy-done, bf16[4,640,128]{2,1,0:T(8,128)(2,1)} %get-tuple-element.28.q, ...), custom_call_target="tpu_custom_call" | custom-call | flops 1845493760 | bytes 8388608 | tf_op jit(solution)/shard_map/attend_line/pallas_call | solution.py:235
  43.6 4.9 %attend_last_line.1 = (bf16[1,640,128]{2,1,0:T(8,128)(2,1)}, f32[1,8,128]{2,1,0:T(8,128)}, bf16[4,2,256,128]{3,2,1,0:T(8,128)(2,1)}, bf16[4,2,256,128]{3,2,1,0:T(8,128)(2,1)}, bf16[4,2,256,128]{3,2,1,0:T(8,128)(2,1)}) custom-call(s32[4]{0:T(128)S(1)} %broadcast_select_fusion.qid, s32[4]{0:T(128)S(1)} %broadcast_select_fusion.4.qid.kid, s32[256]{0:T(256)S(1)} %reshape.33.bs, ...), custom_call_target="tpu_custom_call" | custom-call | flops 461373440 | bytes 8388608 | tf_op jit(solution)/shard_map/attend_last_line/pallas_call | solution.py:255
  49.2 2.0 %collective-permute-start.10 = (bf16[4,2,256,128]{3,2,1,0:T(8,128)(2,1)}, bf16[4,2,256,128]{3,2,1,0:T(8,128)(2,1)S(1)}, u32[]{:S(2)}, u32[]{:S(2)}) collective-permute-start(bf16[4,2,256,128]{3,2,1,0:T(8,128)(2,1)} %get-tuple-element.38), channel_id=1, source_target_pairs={{0,64},{1,17},{2,66},{3,19},{4,68},{5,21},{6,70},{7,23},{8,72},{9,... | collective-permute-start | bytes 1572872 | tf_op jit(solution)/shard_map/ppermute | solution.py:37
  53.0 9.1 %attend_groups.2 = (bf16[4,640,128]{2,1,0:T(8,128)(2,1)}, f32[4,8,128]{2,1,0:T(8,128)}) custom-call(s32[4]{0:T(128)S(1)} %broadcast_select_fusion.4.qid.kid, s32[4]{0:T(128)S(1)} %get-tuple-element.53.kid, s32[256]{0:T(256)S(1)} %reshape.33.bs, s32[16]{0:T(128)S(1)} %copy-done, bf16[4,640,128]{2,1,0:T(8,128)(2,1)} %get-tuple-element.28.q, ...), custom_call_target="tpu_custom_call" | custom-call | flops 1342177280 | bytes 8388608 | tf_op jit(solution)/shard_map/attend_groups/pallas_call | solution.py:297
  62.1 4.5 %collective-permute-done.4.refs_1_ = bf16[8,640,128]{2,1,0:T(8,128)(2,1)S(1)} collective-permute-done((bf16[8,640,128]{2,1,0:T(8,128)(2,1)}, bf16[8,640,128]{2,1,0:T(8,128)(2,1)S(1)}, u32[]{:S(2)}, u32[]{:S(2)}) %collective-permute-start.4) | collective-permute-done | bytes 1310752 | tf_op jit(solution)/shard_map/ppermute | solution.py:37
  66.5 10.6 %attend_groups.3 = (bf16[4,640,128]{2,1,0:T(8,128)(2,1)S(1)}, f32[8,128]{1,0:T(8,128)}) custom-call(s32[4]{0:T(128)S(1)} %broadcast_select_fusion.4.qid.kid, s32[8]{0:T(128)S(1)} %pad_add_fusion.kid, s32[256]{0:T(256)S(1)} %reshape.33.bs, s32[16]{0:T(128)S(1)} %copy-done, bf16[4,640,128]{2,1,0:T(8,128)(2,1)} %get-tuple-element.28.q, ...), custom_call_target="tpu_custom_call" | custom-call | flops 2684354560 | bytes 8388608 | tf_op jit(solution)/shard_map/attend_groups/pallas_call | solution.py:297
  81.4 4.6 %attend_bands.1 = bf16[1,640,128]{2,1,0:T(8,128)(2,1)S(1)} custom-call(s32[1]{0:T(128)} %bitcast.7.qid, s32[12]{0:T(128)S(1)} %pad_add_fusion.1.kid, s32[256]{0:T(256)S(1)} %reshape.33.bs, s32[16]{0:T(128)S(1)} %copy-done, bf16[640,640]{1,0:T(8,128)(2,1)} %q.3, bf16[4,2,256,128]{3,2,1,0:T(8,128)(2,1)S(1)} %collective-permute-done.9.g1, ...), custom_call_target="tpu_custom_call" | custom-call | flops 1006632960 | bytes 8388608 | tf_op jit(solution)/shard_map/attend_bands/pallas_call | solution.py:326
  86.8 2.2 %project.6.refs_0_ = bf16[1,640,640]{2,1,0:T(8,128)(2,1)S(1)} custom-call(s32[1]{0:T(128)S(6)} %sub.85.order, s32[1]{0:T(128)} %bitcast.2.pos, bf16[640,128]{1,0:T(8,128)(2,1)S(1)} %get-tuple-element.52.o0, bf16[640,128]{1,0:T(8,128)(2,1)S(1)} %collective-permute-done.6.o1, bf16[640,128]{1,0:T(8,128)(2,1)S(1)} %collective-permute-done.7.o2, ...), custom_call_target="tpu_custom_call" | custom-call | flops 524288000 | bytes 819200 | tf_op jit(solution)/shard_map/project/pallas_call | solution.py:361
  89.1 2.1 %project.7 = bf16[1,640,640]{2,1,0:T(8,128)(2,1)S(1)} custom-call(s32[1]{0:T(128)S(6)} %add.252.order, s32[1]{0:T(128)} %bitcast.2.pos, bf16[640,128]{1,0:T(8,128)(2,1)S(1)} %get-tuple-element.52.o0, bf16[640,128]{1,0:T(8,128)(2,1)S(1)} %collective-permute-done.6.o1, bf16[640,128]{1,0:T(8,128)(2,1)S(1)} %collective-permute-done.7.o2, ...), custom_call_target="tpu_custom_call" | custom-call | flops 524288000 | bytes 819200 | tf_op jit(solution)/shard_map/project/pallas_call | solution.py:361
  91.6 3.7 %project.8.refs_0_ = bf16[2,640,640]{2,1,0:T(8,128)(2,1)S(1)} custom-call(s32[2]{0:T(128)S(1)} %add_subtract_fusion.order, s32[1]{0:T(128)} %bitcast.2.pos, bf16[640,128]{1,0:T(8,128)(2,1)S(1)} %get-tuple-element.52.o0, bf16[640,128]{1,0:T(8,128)(2,1)S(1)} %collective-permute-done.6.o1, bf16[640,128]{1,0:T(8,128)(2,1)S(1)} %collective-permute-done.7.o2, ...), custom_call_target="tpu_custom_call" | custom-call | flops 1048576000 | bytes 1638400 | tf_op jit(solution)/shard_map/project/pallas_call | solution.py:361
  95.8 3.1 %collective-permute-start.18 = (bf16[320,640]{1,0:T(8,128)(2,1)S(1)}, bf16[320,640]{1,0:T(8,128)(2,1)S(1)}, u32[]{:S(2)}, u32[]{:S(2)}) collective-permute-start(bf16[320,640]{1,0:T(8,128)(2,1)S(1)} %get-tuple-element.47), channel_id=1, source_target_pairs={{0,6},{1,7},{2,0},{3,1},{4,2},{5,3},{6,4},{7,5},{8,14},{9,15},{10,... | collective-permute-start | bytes 1228808 | tf_op jit(solution)/shard_map/ppermute | solution.py:41
  98.9 3.7 %project.9 = bf16[2,640,640]{2,1,0:T(8,128)(2,1)S(1)} custom-call(s32[2]{0:T(128)S(1)} %get-tuple-element.43.order, s32[1]{0:T(128)} %bitcast.2.pos, bf16[640,128]{1,0:T(8,128)(2,1)S(1)} %get-tuple-element.52.o0, bf16[640,128]{1,0:T(8,128)(2,1)S(1)} %collective-permute-done.6.o1, bf16[640,128]{1,0:T(8,128)(2,1)S(1)} %collective-permute-done.7.o2, ...), custom_call_target="tpu_custom_call" | custom-call | flops 1048576000 | bytes 1638400 | tf_op jit(solution)/shard_map/project/pallas_call | solution.py:361
  103.7 2.1 %project.10.refs_0_ = bf16[1,640,640]{2,1,0:T(8,128)(2,1)S(1)} custom-call(s32[1]{0:T(128)S(6)} %sub.83.order, s32[1]{0:T(128)} %bitcast.2.pos, bf16[640,128]{1,0:T(8,128)(2,1)S(1)} %get-tuple-element.52.o0, bf16[640,128]{1,0:T(8,128)(2,1)S(1)} %collective-permute-done.6.o1, bf16[640,128]{1,0:T(8,128)(2,1)S(1)} %collective-permute-done.7.o2, ...), custom_call_target="tpu_custom_call" | custom-call | flops 524288000 | bytes 819200 | tf_op jit(solution)/shard_map/project/pallas_call | solution.py:361
  106.0 6.5 %collective-permute-done.15 = bf16[320,640]{1,0:T(8,128)(2,1)S(1)} collective-permute-done((bf16[320,640]{1,0:T(8,128)(2,1)S(1)}, bf16[320,640]{1,0:T(8,128)(2,1)S(1)}, u32[]{:S(2)}, u32[]{:S(2)}) %collective-permute-start.15) | collective-permute-done | bytes 409632 | tf_op jit(solution)/shard_map/ppermute | solution.py:41
  112.7 3.3 %collective-permute-start.20 = (bf16[320,640]{1,0:T(8,128)(2,1)S(1)}, bf16[320,640]{1,0:T(8,128)(2,1)S(1)}, u32[]{:S(2)}, u32[]{:S(2)}) collective-permute-start(bf16[320,640]{1,0:T(8,128)(2,1)S(1)} %slice_bitcast_fusion), channel_id=1, source_target_pairs={{0,6},{1,7},{2,0},{3,1},{4,2},{5,3},{6,4},{7,5},{8,14},{9,15},{10,... | collective-permute-start | bytes 1228808 | tf_op jit(solution)/shard_map/ppermute | solution.py:41
  116.2 2.1 %project.11 = bf16[1,640,640]{2,1,0:T(8,128)(2,1)S(1)} custom-call(s32[1]{0:T(128)S(6)} %add.211.order, s32[1]{0:T(128)} %bitcast.2.pos, bf16[640,128]{1,0:T(8,128)(2,1)S(1)} %get-tuple-element.52.o0, bf16[640,128]{1,0:T(8,128)(2,1)S(1)} %collective-permute-done.6.o1, bf16[640,128]{1,0:T(8,128)(2,1)S(1)} %collective-permute-done.7.o2, ...), custom_call_target="tpu_custom_call" | custom-call | flops 524288000 | bytes 819200 | tf_op jit(solution)/shard_map/project/pallas_call | solution.py:361
  118.5 2.7 %collective-permute-done.17.plain_up = bf16[320,640]{1,0:T(8,128)(2,1)S(1)} collective-permute-done((bf16[320,640]{1,0:T(8,128)(2,1)S(1)}, bf16[320,640]{1,0:T(8,128)(2,1)S(1)}, u32[]{:S(2)}, u32[]{:S(2)}) %collective-permute-start.17) | collective-permute-done | bytes 409632 | tf_op jit(solution)/shard_map/ppermute | solution.py:41
  121.2 7.7 %collective-permute-done.16.more_up = bf16[320,640]{1,0:T(8,128)(2,1)S(1)} collective-permute-done((bf16[320,640]{1,0:T(8,128)(2,1)S(1)}, bf16[320,640]{1,0:T(8,128)(2,1)S(1)}, u32[]{:S(2)}, u32[]{:S(2)}) %collective-permute-start.16) | collective-permute-done | bytes 409632 | tf_op jit(solution)/shard_map/ppermute | solution.py:41
  128.9 2.3 %collective-permute-done.19.more_down = bf16[320,640]{1,0:T(8,128)(2,1)S(1)} collective-permute-done((bf16[320,640]{1,0:T(8,128)(2,1)S(1)}, bf16[320,640]{1,0:T(8,128)(2,1)S(1)}, u32[]{:S(2)}, u32[]{:S(2)}) %collective-permute-start.19) | collective-permute-done | bytes 409632 | tf_op jit(solution)/shard_map/ppermute | solution.py:41
  (56 shorter events, 19.8 us)
Async XLA Ops:
  2.0 20.7 %collective-permute-start = (bf16[5,640,128]{2,1,0:T(8,128)(2,1)S(1)}, bf16[5,640,128]{2,1,0:T(8,128)(2,1)S(1)}, u32[]{:S(2)}, u32[]{:S(2)}) collective-permute-start(bf16[5,640,128]{2,1,0:T(8,128)(2,1)S(1)} %get-tuple-element.25), channel_id=1, source_target_pairs={{0,8},{1,33},{2,10},{3,35},{4,12},{5,37},{6,14},{7,39},{8,16},{9,4... | collective-permute-start | bytes 2457608 | tf_op jit(solution)/shard_map/ppermute | solution.py:33
  3.9 18.7 %collective-permute-start.1 = (bf16[5,640,128]{2,1,0:T(8,128)(2,1)S(1)}, bf16[5,640,128]{2,1,0:T(8,128)(2,1)S(1)}, u32[]{:S(2)}, u32[]{:S(2)}) collective-permute-start(bf16[5,640,128]{2,1,0:T(8,128)(2,1)S(1)} %get-tuple-element.26), channel_id=1, source_target_pairs={{0,16},{1,65},{2,18},{3,67},{4,20},{5,69},{6,22},{7,71},{8,24},{9,... | collective-permute-start | bytes 2457608 | tf_op jit(solution)/shard_map/ppermute | solution.py:33
  5.1 21.1 %collective-permute-start.2 = (bf16[5,640,128]{2,1,0:T(8,128)(2,1)S(1)}, bf16[5,640,128]{2,1,0:T(8,128)(2,1)S(1)}, u32[]{:S(2)}, u32[]{:S(2)}) collective-permute-start(bf16[5,640,128]{2,1,0:T(8,128)(2,1)S(1)} %get-tuple-element.27), channel_id=1, source_target_pairs={{0,24},{1,97},{2,26},{3,99},{4,28},{5,101},{6,30},{7,103},{8,0},{9... | collective-permute-start | bytes 2457608 | tf_op jit(solution)/shard_map/ppermute | solution.py:33
  26.2 7.0 %copy-start.1 = (s32[16,16]{1,0:T(8,128)S(1)}, s32[16,16]{1,0:T(8,128)}, u32[]{:S(2)}) copy-start(s32[16,16]{1,0:T(8,128)} %param.13) | copy-start | bytes 3076
  26.2 7.2 %copy-start = (s32[16]{0:T(128)S(1)}, s32[16]{0:T(128)}, u32[]{:S(2)}) copy-start(s32[16]{0:T(128)} %bw.9) | copy-start | bytes 196
  28.1 23.1 %collective-permute-start.5 = (bf16[8,640,128]{2,1,0:T(8,128)(2,1)}, bf16[8,640,128]{2,1,0:T(8,128)(2,1)}, u32[]{:S(2)}, u32[]{:S(2)}) collective-permute-start(bf16[8,640,128]{2,1,0:T(8,128)(2,1)} %get-tuple-element.29.kv), channel_id=1, source_target_pairs={{0,32},{1,9},{2,34},{3,11},{4,36},{5,13},{6,38},{7,15},{8,40},{9,1... | collective-permute-start | bytes 3932168 | tf_op jit(solution)/shard_map/ppermute | solution.py:37
  29.7 36.9 %collective-permute-start.4 = (bf16[8,640,128]{2,1,0:T(8,128)(2,1)}, bf16[8,640,128]{2,1,0:T(8,128)(2,1)S(1)}, u32[]{:S(2)}, u32[]{:S(2)}) collective-permute-start(bf16[8,640,128]{2,1,0:T(8,128)(2,1)} %get-tuple-element.29.kv), channel_id=1, source_target_pairs={{0,96},{1,25},{2,98},{3,27},{4,100},{5,29},{6,102},{7,31},{8,104},... | collective-permute-start | bytes 3932168 | tf_op jit(solution)/shard_map/ppermute | solution.py:37
  31.4 35.1 %collective-permute-start.3 = (bf16[8,640,128]{2,1,0:T(8,128)(2,1)}, bf16[8,640,128]{2,1,0:T(8,128)(2,1)S(1)}, u32[]{:S(2)}, u32[]{:S(2)}) collective-permute-start(bf16[8,640,128]{2,1,0:T(8,128)(2,1)} %get-tuple-element.29.kv), channel_id=1, source_target_pairs={{0,64},{1,17},{2,66},{3,19},{4,68},{5,21},{6,70},{7,23},{8,72},{9,... | collective-permute-start | bytes 3932168 | tf_op jit(solution)/shard_map/ppermute | solution.py:37
  48.6 31.2 %collective-permute-start.9 = (bf16[4,2,256,128]{3,2,1,0:T(8,128)(2,1)}, bf16[4,2,256,128]{3,2,1,0:T(8,128)(2,1)S(1)}, u32[]{:S(2)}, u32[]{:S(2)}) collective-permute-start(bf16[4,2,256,128]{3,2,1,0:T(8,128)(2,1)} %get-tuple-element.37), channel_id=1, source_target_pairs={{0,32},{1,9},{2,34},{3,11},{4,36},{5,13},{6,38},{7,15},{8,40},{9,1... | collective-permute-start | bytes 1572872 | tf_op jit(solution)/shard_map/ppermute | solution.py:37
  49.2 32.3 %collective-permute-start.10 = (bf16[4,2,256,128]{3,2,1,0:T(8,128)(2,1)}, bf16[4,2,256,128]{3,2,1,0:T(8,128)(2,1)S(1)}, u32[]{:S(2)}, u32[]{:S(2)}) collective-permute-start(bf16[4,2,256,128]{3,2,1,0:T(8,128)(2,1)} %get-tuple-element.38), channel_id=1, source_target_pairs={{0,64},{1,17},{2,66},{3,19},{4,68},{5,21},{6,70},{7,23},{8,72},{9,... | collective-permute-start | bytes 1572872 | tf_op jit(solution)/shard_map/ppermute | solution.py:37
  51.2 30.2 %collective-permute-start.11 = (bf16[4,2,256,128]{3,2,1,0:T(8,128)(2,1)}, bf16[4,2,256,128]{3,2,1,0:T(8,128)(2,1)S(1)}, u32[]{:S(2)}, u32[]{:S(2)}) collective-permute-start(bf16[4,2,256,128]{3,2,1,0:T(8,128)(2,1)} %get-tuple-element.39), channel_id=1, source_target_pairs={{0,96},{1,25},{2,98},{3,27},{4,100},{5,29},{6,102},{7,31},{8,104},... | collective-permute-start | bytes 1572872 | tf_op jit(solution)/shard_map/ppermute | solution.py:37
  77.2 8.9 %collective-permute-start.8 = (bf16[640,128]{1,0:T(8,128)(2,1)S(1)}, bf16[640,128]{1,0:T(8,128)(2,1)S(1)}, u32[]{:S(2)}, u32[]{:S(2)}) collective-permute-start(bf16[640,128]{1,0:T(8,128)(2,1)S(1)} %get-tuple-element.49), channel_id=1, source_target_pairs={{0,8},{1,33},{2,10},{3,35},{4,12},{5,37},{6,14},{7,39},{8,16},{9,4... | collective-permute-start | bytes 491528 | tf_op jit(solution)/shard_map/ppermute | solution.py:33
  78.2 7.8 %collective-permute-start.7 = (bf16[640,128]{1,0:T(8,128)(2,1)S(1)}, bf16[640,128]{1,0:T(8,128)(2,1)S(1)}, u32[]{:S(2)}, u32[]{:S(2)}) collective-permute-start(bf16[640,128]{1,0:T(8,128)(2,1)S(1)} %get-tuple-element.50), channel_id=1, source_target_pairs={{0,16},{1,65},{2,18},{3,67},{4,20},{5,69},{6,22},{7,71},{8,24},{9,... | collective-permute-start | bytes 491528 | tf_op jit(solution)/shard_map/ppermute | solution.py:33
  79.8 7.0 %collective-permute-start.6 = (bf16[640,128]{1,0:T(8,128)(2,1)S(1)}, bf16[640,128]{1,0:T(8,128)(2,1)S(1)}, u32[]{:S(2)}, u32[]{:S(2)}) collective-permute-start(bf16[640,128]{1,0:T(8,128)(2,1)S(1)} %get-tuple-element.51), channel_id=1, source_target_pairs={{0,24},{1,97},{2,26},{3,99},{4,28},{5,101},{6,30},{7,103},{8,0},{9... | collective-permute-start | bytes 491528 | tf_op jit(solution)/shard_map/ppermute | solution.py:33
  86.8 2.3 %copy-start.2 = (s32[2]{0:T(128)S(1)}, s32[2]{0:T(128)}, u32[]{:S(2)}) copy-start(s32[2]{0:T(128)} %constant.183.clone) | copy-start | bytes 28
  88.9 2.4 %collective-permute-start.12 = (bf16[1,640,640]{2,1,0:T(8,128)(2,1)S(1)}, bf16[1,640,640]{2,1,0:T(8,128)(2,1)S(1)}, u32[]{:S(2)}, u32[]{:S(2)}) collective-permute-start(bf16[1,640,640]{2,1,0:T(8,128)(2,1)S(1)} %project.6.refs_0_), channel_id=1, source_target_pairs={{0,1},{1,0},{2,3},{3,2},{4,5},{5,4},{6,7},{7,6},{8,9},{9,8},{10,11... | collective-permute-start | bytes 2457608 | tf_op jit(solution)/shard_map/ppermute | solution.py:45
  95.3 7.3 %collective-permute-start.13 = (bf16[2,640,640]{2,1,0:T(8,128)(2,1)S(1)}, bf16[2,640,640]{2,1,0:T(8,128)(2,1)S(1)}, u32[]{:S(2)}, u32[]{:S(2)}) collective-permute-start(bf16[2,640,640]{2,1,0:T(8,128)(2,1)S(1)} %project.8.refs_0_), channel_id=1, source_target_pairs={{0,1},{1,0},{2,3},{3,2},{4,5},{5,4},{6,7},{7,6},{8,9},{9,8},{10,11... | collective-permute-start | bytes 4915208 | tf_op jit(solution)/shard_map/ppermute | solution.py:45
  95.8 20.2 %collective-permute-start.18 = (bf16[320,640]{1,0:T(8,128)(2,1)S(1)}, bf16[320,640]{1,0:T(8,128)(2,1)S(1)}, u32[]{:S(2)}, u32[]{:S(2)}) collective-permute-start(bf16[320,640]{1,0:T(8,128)(2,1)S(1)} %get-tuple-element.47), channel_id=1, source_target_pairs={{0,6},{1,7},{2,0},{3,1},{4,2},{5,3},{6,4},{7,5},{8,14},{9,15},{10,... | collective-permute-start | bytes 1228808 | tf_op jit(solution)/shard_map/ppermute | solution.py:41
  98.9 13.6 %collective-permute-start.15 = (bf16[320,640]{1,0:T(8,128)(2,1)S(1)}, bf16[320,640]{1,0:T(8,128)(2,1)S(1)}, u32[]{:S(2)}, u32[]{:S(2)}) collective-permute-start(bf16[320,640]{1,0:T(8,128)(2,1)S(1)} %get-tuple-element.48), channel_id=1, source_target_pairs={{0,2},{1,3},{2,4},{3,5},{4,6},{5,7},{6,0},{7,1},{8,10},{9,11},{10,... | collective-permute-start | bytes 1228808 | tf_op jit(solution)/shard_map/ppermute | solution.py:41
  103.1 18.1 %collective-permute-start.17 = (bf16[320,640]{1,0:T(8,128)(2,1)S(1)}, bf16[320,640]{1,0:T(8,128)(2,1)S(1)}, u32[]{:S(2)}, u32[]{:S(2)}) collective-permute-start(bf16[320,640]{1,0:T(8,128)(2,1)S(1)} %slice_bitcast_fusion.3), channel_id=1, source_target_pairs={{0,2},{1,3},{2,4},{3,5},{4,6},{5,7},{6,0},{7,1},{8,10},{9,11},{10,... | collective-permute-start | bytes 1228808 | tf_op jit(solution)/shard_map/ppermute | solution.py:41
  105.9 12.4 %collective-permute-start.14 = (bf16[1,640,640]{2,1,0:T(8,128)(2,1)S(1)}, bf16[1,640,640]{2,1,0:T(8,128)(2,1)S(1)}, u32[]{:S(2)}, u32[]{:S(2)}) collective-permute-start(bf16[1,640,640]{2,1,0:T(8,128)(2,1)S(1)} %project.10.refs_0_), channel_id=1, source_target_pairs={{0,1},{1,0},{2,3},{3,2},{4,5},{5,4},{6,7},{7,6},{8,9},{9,8},{10,11... | collective-permute-start | bytes 2457608 | tf_op jit(solution)/shard_map/ppermute | solution.py:45
  112.5 16.3 %collective-permute-start.16 = (bf16[320,640]{1,0:T(8,128)(2,1)S(1)}, bf16[320,640]{1,0:T(8,128)(2,1)S(1)}, u32[]{:S(2)}, u32[]{:S(2)}) collective-permute-start(bf16[320,640]{1,0:T(8,128)(2,1)S(1)} %fusion.2), channel_id=1, source_target_pairs={{0,2},{1,3},{2,4},{3,5},{4,6},{5,7},{6,0},{7,1},{8,10},{9,11},{10,... | collective-permute-start | bytes 1228808 | tf_op jit(solution)/shard_map/ppermute | solution.py:41
  112.7 16.2 %collective-permute-start.20 = (bf16[320,640]{1,0:T(8,128)(2,1)S(1)}, bf16[320,640]{1,0:T(8,128)(2,1)S(1)}, u32[]{:S(2)}, u32[]{:S(2)}) collective-permute-start(bf16[320,640]{1,0:T(8,128)(2,1)S(1)} %slice_bitcast_fusion), channel_id=1, source_target_pairs={{0,6},{1,7},{2,0},{3,1},{4,2},{5,3},{6,4},{7,5},{8,14},{9,15},{10,... | collective-permute-start | bytes 1228808 | tf_op jit(solution)/shard_map/ppermute | solution.py:41
  116.1 15.2 %collective-permute-start.19 = (bf16[320,640]{1,0:T(8,128)(2,1)S(1)}, bf16[320,640]{1,0:T(8,128)(2,1)S(1)}, u32[]{:S(2)}, u32[]{:S(2)}) collective-permute-start(bf16[320,640]{1,0:T(8,128)(2,1)S(1)} %fusion.1), channel_id=1, source_target_pairs={{0,6},{1,7},{2,0},{3,1},{4,2},{5,3},{6,4},{7,5},{8,14},{9,15},{10,... | collective-permute-start | bytes 1228808 | tf_op jit(solution)/shard_map/ppermute | solution.py:41

commit v4 on v3

--- a/solution.py
+++ b/solution.py
@@ -184,7 +184,8 @@
     return emit
 
 
-def line_kernel(qid, kid, bs, bw, q, kv, out, levels, kc, vc):
+def line_kernel(qid, kid, bs, bw, q, kv, after, out, levels, kc, vc):
+    del after
     i = pl.program_id(0)
     for s in range(SIDE):
         first, second, valid = band_of(qid[i], kid[s], bs, bw)
@@ -230,14 +231,14 @@
     return [pltpu.HBM((items, FT, HD), jnp.bfloat16), pltpu.HBM((items, 8, HD), jnp.float32)]
 
 
-def attend_line(qid, kid, bs, bw, q, kv):
+def attend_line(qid, kid, bs, bw, q, kv, after):
     blocks = 2 * SIDE + NB - 2
     return pl.pallas_call(
         line_kernel,
         grid_spec=pltpu.PrefetchScalarGridSpec(
             num_scalar_prefetch=4,
             grid=(SIDE,),
-            in_specs=[ITEM, pl.BlockSpec(kv.shape, lambda i, *_: (0, 0, 0))],
+            in_specs=[ITEM, pl.BlockSpec(kv.shape, lambda i, *_: (0, 0, 0)), ANY],
             out_specs=[ITEM, LEVEL],
             scratch_shapes=packed(blocks),
         ),
@@ -245,7 +246,7 @@
         compiler_params=pltpu.CompilerParams(vmem_limit_bytes=LIMIT),
         cost_estimate=cost(SIDE, blocks),
         name="attend_line",
-    )(qid, kid, bs, bw, *in_hbm(q, kv))
+    )(qid, kid, bs, bw, *in_hbm(q, kv, after))
 
 
 def attend_last_line(qid, kid, bs, bw, queries, keys, values, after):
@@ -341,41 +342,54 @@
     )(qid, kid, bs, bw, *in_hbm(queries), *groups, *in_hbm(*state, after))
 
 
-def project_kernel(order, pos, o0, o1, o2, o3, o4, w_ref, *refs):
-    y_ref, att = refs[-2:]
-
-    @pl.when(pl.program_id(0) == 0)
-    def _():
-        for s, o in enumerate((o0, o1, o2, o3)):
-            head = lax.rem(pos[0] + s, SIDE)
-            att[:, pl.ds(pl.multiple_of(head * HD, HD), HD)] = o[...]
-        att[:, 4 * HD :] = o4[...]
-
-    y_ref[0] = jnp.dot(att[...], w_ref[...], preferred_element_type=jnp.float32).astype(jnp.bfloat16)
-
-
-def project(order, pos, outs, weight, *after):
-    count = order.shape[0]
-    width = weight.shape[1] // 8
-    whole = pl.BlockSpec((FT, HD), lambda i, *_: (0, 0))
+def assemble_kernel(pos, o0, o1, o2, o3, o4, att):
+    for s, o in enumerate((o0, o1, o2, o3)):
+        head = lax.rem(pos[0] + s, SIDE)
+        att[:, pl.ds(pl.multiple_of(head * HD, HD), HD)] = o[...]
+    att[:, SIDE * HD :] = o4[...]
+
+
+def assemble(pos, outs):
+    return pl.pallas_call(
+        assemble_kernel,
+        in_specs=[pl.BlockSpec(memory_space=pltpu.SMEM)] + [VMEM] * 5,
+        out_specs=VMEM,
+        out_shape=jax.ShapeDtypeStruct((FT, 5 * HD), jnp.bfloat16),
+        compiler_params=pltpu.CompilerParams(vmem_limit_bytes=LIMIT),
+        name="assemble",
+    )(pos, *outs)
+
+
+def project_kernel(order, blocks, att, att_other, w_mine, w_other, *refs):
+    del order, blocks
+    out, step = refs[-1], FT // 2
+    for r in range(0, FT, step):
+        rows = slice(r, r + step)
+        total = jnp.dot(att[rows, :], w_mine[...], preferred_element_type=jnp.float32)
+        total = total + jnp.dot(att_other[rows, :], w_other[...], preferred_element_type=jnp.float32)
+        out[pl.program_id(0), rows, :] = total.astype(jnp.bfloat16)
+
+
+def project(order, core, att, att_other, weight, other_weight, *after):
+    count, width = order.shape[0], weight.shape[1] // 8
     return pl.pallas_call(
         project_kernel,
         grid_spec=pltpu.PrefetchScalarGridSpec(
             num_scalar_prefetch=2,
             grid=(count,),
-            in_specs=[whole] * 5
-            + [pl.BlockSpec((5 * HD, width), lambda i, order, pos: (0, order[i]))]
+            in_specs=[
+                VMEM,
+                VMEM,
+                pl.BlockSpec((5 * HD, width), lambda i, order, blocks: (0, blocks[i])),
+                pl.BlockSpec((5 * HD, width), lambda i, order, blocks: (0, blocks[i])),
+            ]
             + [ANY] * len(after),
-            out_specs=pl.BlockSpec((1, FT, width), lambda i, *_: (i, 0, 0)),
-            scratch_shapes=[pltpu.VMEM((FT, 5 * HD), jnp.bfloat16)],
+            out_specs=VMEM,
         ),
         out_shape=jax.ShapeDtypeStruct((count, FT, width), jnp.bfloat16),
         compiler_params=pltpu.CompilerParams(vmem_limit_bytes=LIMIT),
-        cost_estimate=pl.CostEstimate(
-            flops=2 * count * FT * 5 * HD * width, bytes_accessed=count * FT * width * 2, transcendentals=0
-        ),
         name="project",
-    )(order, pos, *outs, *in_hbm(weight), *after)
+    )(order, 2 * order + core, att, att_other, *in_hbm(weight, other_weight), *after)
 
 
 def add(*terms):
@@ -385,22 +399,24 @@
     return total.astype(jnp.bfloat16)
 
 
-def finish_kernel(own, more_up, plain_up, more_down, plain_down, out):
+def onward_kernel(near, from_down, from_up, send_up, send_down):
     half = FT // 2
     wide = lambda v: v.astype(jnp.float32)
-    out[0:half, :] = (wide(own[0:half, :]) + wide(more_up[...]) + wide(plain_down[...])).astype(jnp.bfloat16)
-    out[half:, :] = (wide(own[half:, :]) + wide(more_down[...]) + wide(plain_up[...])).astype(jnp.bfloat16)
-
-
-def finish(*args):
-    return pl.pallas_call(
-        finish_kernel,
-        in_specs=[VMEM] * 5,
-        out_specs=pl.BlockSpec(args[0].shape, lambda: (0, 0)),
-        out_shape=jax.ShapeDtypeStruct(args[0].shape, jnp.bfloat16),
-        compiler_params=pltpu.CompilerParams(vmem_limit_bytes=LIMIT),
-        name="finish",
-    )(*args)
+    send_up[0:half, :] = (wide(near[0, 0:half, :]) + wide(from_down[...])).astype(jnp.bfloat16)
+    send_up[half:, :] = near[0, half:, :]
+    send_down[0:half, :] = near[1, 0:half, :]
+    send_down[half:, :] = (wide(near[1, half:, :]) + wide(from_up[...])).astype(jnp.bfloat16)
+
+
+def onward(near, from_down, from_up):
+    return pl.pallas_call(
+        onward_kernel,
+        in_specs=[VMEM] * 3,
+        out_specs=[VMEM] * 2,
+        out_shape=[jax.ShapeDtypeStruct(near.shape[1:], jnp.bfloat16)] * 2,
+        compiler_params=pltpu.CompilerParams(vmem_limit_bytes=LIMIT),
+        name="onward",
+    )(near, from_down, from_up)
 
 
 def shards(queries, key_rows, value_rows, out_weight, band_start, band_width):
@@ -422,10 +438,13 @@
 
     pieces = pick(line[None], queries, key_rows, value_rows)
     pieces = [pieces[0]] + [line_shift(pieces[s], s) for s in range(1, SIDE)]
+
+    other_weight = core_swap(out_weight)
+
     q, kv, k_last, v_last = stack(pieces)
 
     groups = [cross_shift(kv, s) for s in range(1, SIDE)]
-    state = attend_line(f0, f0, bs, bw, q, kv)
+    state = attend_line(f0, f0, bs, bw, q, kv, other_weight)
 
     here_and_across = frames_at(-ring, 0)
     *last_state, s_1, s_2, s_3 = attend_last_line(here_and_across, f0, bs, bw, queries, k_last, v_last, state[0])
@@ -437,21 +456,20 @@
     o_last = attend_bands(frame[None], jnp.concatenate([f1, f2, f3]), bs, bw, queries, last, last_state, token)
     outs.append(o_last[0])
 
-    def summed(ahead, *after):
-        target = (y + jnp.array(ahead, jnp.int32)) % SIDE * 2
-        away = project(target + 1 - core, line[None], outs, out_weight, *after)
-        given = core_swap(away)
-        kept = project(target + core, line[None], outs, out_weight, away)
-        return [add(kept[i], given[i]) for i in range(len(ahead))]
+    att = assemble(line[None], outs)
+    att_other = core_swap(att)
+
+    def share(ahead, *after):
+        order = (y + jnp.array(ahead, jnp.int32)) % SIDE
+        return project(order, core, att, att_other, out_weight, other_weight, *after)
 
     half = FT // 2
-    (two,) = summed([2])
-    from_down, from_up = y_shift(two[:half], 1), y_shift(two[half:], 3)
-    up, down = summed([1, 3], two)
-    plain_up, plain_down = y_shift(up[half:], 1), y_shift(down[:half], 3)
-    (own,) = summed([0], up)
-    more_up, more_down = y_shift(add(up[:half], from_down), 1), y_shift(add(down[half:], from_up), 3)
-    return finish(own, more_up, plain_up, more_down, plain_down)
+    two = share([2])
+    from_down, from_up = y_shift(two[0, :half], 1), y_shift(two[0, half:], 3)
+    near = share([1, 3], two)
+    send_up, send_down = onward(near, from_down, from_up)
+    own = share([0], near)
+    return add(own[0], y_shift(send_up, 1), y_shift(send_down, 3))
 
 
 def solution(mesh):

time: 135 us -> 128 us (0.948); the launches traced: 132 us -> 127 us
  Pallas kernels: 60.4 us -> 54.9 us
  starting transfers between devices: 27.2 us -> 29.9 us
  waiting for transfers between devices: 43 us -> 40.8 us
    pallas_call x6 -> x3, Pallas kernels: 16 us -> 11.3 us  [project(): pl.pallas_call(project_kernel, grid_spec=pltpu.PrefetchScalarGridSpec(num...]
    ppermute x3 -> x2, starting transfers between devices: 0.62 us -> 4.38 us  [core_swap(): return lax.ppermute(v, BOTH, pairs(lambda x, z, y, c: (x, z, y, 1 - c)))]
    ppermute x6, waiting for transfers between devices: 4.48 us -> 0.72 us  [cross_shift(): lax.ppermute(v, BOTH, pairs(lambda x, z, y, c: (x + s, z, y, c) if c == 0...]
    ppermute x3 -> x2, waiting for transfers between devices: 0.13 us -> 1.96 us  [core_swap(): return lax.ppermute(v, BOTH, pairs(lambda x, z, y, c: (x, z, y, 1 - c)))]
    ppermute x6 -> x4, starting transfers between devices: 7.19 us -> 6.62 us  [y_shift(): return lax.ppermute(v, BOTH, pairs(lambda x, z, y, c: (x, z, y + s, c)))]
    ppermute x6 -> x4, waiting for transfers between devices: 19.1 us -> 19.2 us  [y_shift(): return lax.ppermute(v, BOTH, pairs(lambda x, z, y, c: (x, z, y + s, c)))]
  transfers between devices with their start and end apart: 21 -> 18, of which waited for: 9 -> 7; matrix products, arithmetic and copies ran while one was open for 1% -> 0% of each run, Pallas kernels for 37% -> 40%
where the time goes in v4:
time: 128 us; the launch traced here: 127 us
  Pallas kernels  54.9 us (43%)
  waiting for transfers between devices  40.8 us (32%)
  starting transfers between devices  29.9 us (23%)
  other arithmetic  1.43 us (1%)
    pallas_call x2, Pallas kernels, attend_groups(): pl.pallas_call(functools.partial(groups_kernel, len(groups), finished), g...  19.7 us
    ppermute x4, waiting for transfers between devices, y_shift(): return lax.ppermute(v, BOTH, pairs(lambda x, z, y, c: (x, z, y + s, c)))  19.2 us
    ppermute x6, waiting for transfers between devices, line_shift(): lax.ppermute(v, BOTH, pairs(lambda x, z, y, c: (x, z + s, y, c) if c == 0...  18.9 us
    pallas_call x3, Pallas kernels, project(): pl.pallas_call(project_kernel, grid_spec=pltpu.PrefetchScalarGridSpec(num...  11.3 us
    pallas_call x1, Pallas kernels, attend_line(): pl.pallas_call(line_kernel, grid_spec=pltpu.PrefetchScalarGridSpec(num_sc...  10.2 us
    ppermute x6, starting transfers between devices, line_shift(): lax.ppermute(v, BOTH, pairs(lambda x, z, y, c: (x, z + s, y, c) if c == 0...  9.88 us
    ppermute x6, starting transfers between devices, cross_shift(): lax.ppermute(v, BOTH, pairs(lambda x, z, y, c: (x + s, z, y, c) if c == 0...  8.99 us
    ppermute x4, starting transfers between devices, y_shift(): return lax.ppermute(v, BOTH, pairs(lambda x, z, y, c: (x, z, y + s, c)))  6.62 us
  transfers between devices with their start and end apart: 18, of which 7 were waited for; matrix products, arithmetic and copies ran while one was open for 0% of the time, Pallas kernels for 40%

profile of v4, /device:TPU:32, one launch (start us, length us, event | category | flops | bytes accessed | tf_op | source)
XLA Modules:
  0.0 127.4 jit_solution(11649382014569502492)
XLA Ops:
  0.0 2.0 %pick.1 = (bf16[5,640,128]{2,1,0:T(8,128)(2,1)S(1)}, bf16[5,640,128]{2,1,0:T(8,128)(2,1)S(1)}, bf16[5,640,128]{2,1,0:T(8,128)(2,1)S(1)}, bf16[5,640,128]{2,1,0:T(8,128)(2,1)S(1)}) custom-call(s32[1]{0:T(128)} %bitcast.2.pos, bf16[640,640]{1,0:T(8,128)(2,1)} %q.3, bf16[640,640]{1,0:T(8,128)(2,1)} %k_any.1, bf16[640,640]{1,0:T(8,128)(2,1)} %v_any.1), custom_call_target="tpu_custom_call" | custom-call | tf_op jit(solution)/shard_map/pick/pallas_call | solution.py:82
  2.0 2.0 %collective-permute-start = (bf16[5,640,128]{2,1,0:T(8,128)(2,1)S(1)}, bf16[5,640,128]{2,1,0:T(8,128)(2,1)S(1)}, u32[]{:S(2)}, u32[]{:S(2)}) collective-permute-start(bf16[5,640,128]{2,1,0:T(8,128)(2,1)S(1)} %get-tuple-element.27), channel_id=1, source_target_pairs={{0,8},{1,33},{2,10},{3,35},{4,12},{5,37},{6,14},{7,39},{8,16},{9,4... | collective-permute-start | bytes 2457608 | tf_op jit(solution)/shard_map/ppermute | solution.py:33
  5.1 2.5 %collective-permute-start.2 = (bf16[5,640,128]{2,1,0:T(8,128)(2,1)S(1)}, bf16[5,640,128]{2,1,0:T(8,128)(2,1)S(1)}, u32[]{:S(2)}, u32[]{:S(2)}) collective-permute-start(bf16[5,640,128]{2,1,0:T(8,128)(2,1)S(1)} %get-tuple-element.29), channel_id=1, source_target_pairs={{0,24},{1,97},{2,26},{3,99},{4,28},{5,101},{6,30},{7,103},{8,0},{9... | collective-permute-start | bytes 2457608 | tf_op jit(solution)/shard_map/ppermute | solution.py:33
  7.6 15.0 %collective-permute-done.refs_1_ = bf16[5,640,128]{2,1,0:T(8,128)(2,1)S(1)} collective-permute-done((bf16[5,640,128]{2,1,0:T(8,128)(2,1)S(1)}, bf16[5,640,128]{2,1,0:T(8,128)(2,1)S(1)}, u32[]{:S(2)}, u32[]{:S(2)}) %collective-permute-start) | collective-permute-done | bytes 819232 | tf_op jit(solution)/shard_map/ppermute | solution.py:33
  22.6 3.6 %collective-permute-done.2.refs_3_ = bf16[5,640,128]{2,1,0:T(8,128)(2,1)S(1)} collective-permute-done((bf16[5,640,128]{2,1,0:T(8,128)(2,1)S(1)}, bf16[5,640,128]{2,1,0:T(8,128)(2,1)S(1)}, u32[]{:S(2)}, u32[]{:S(2)}) %collective-permute-start.2) | collective-permute-done | bytes 819232 | tf_op jit(solution)/shard_map/ppermute | solution.py:33
  26.2 1.9 %stack.1 = (bf16[4,640,128]{2,1,0:T(8,128)(2,1)}, bf16[8,640,128]{2,1,0:T(8,128)(2,1)}, bf16[4,640,128]{2,1,0:T(8,128)(2,1)}, bf16[4,640,128]{2,1,0:T(8,128)(2,1)}) custom-call(bf16[5,640,128]{2,1,0:T(8,128)(2,1)S(1)} %get-tuple-element.26.refs_0_, bf16[5,640,128]{2,1,0:T(8,128)(2,1)S(1)} %collective-permute-done.refs_1_, ...), custom_call_target="tpu_custom_call" | custom-call | tf_op jit(solution)/shard_map/stack/pallas_call | solution.py:109
  29.7 2.7 %collective-permute-start.3 = (bf16[8,640,128]{2,1,0:T(8,128)(2,1)}, bf16[8,640,128]{2,1,0:T(8,128)(2,1)S(1)}, u32[]{:S(2)}, u32[]{:S(2)}) collective-permute-start(bf16[8,640,128]{2,1,0:T(8,128)(2,1)} %get-tuple-element.31.kv), channel_id=1, source_target_pairs={{0,64},{1,17},{2,66},{3,19},{4,68},{5,21},{6,70},{7,23},{8,72},{9,... | collective-permute-start | bytes 3932168 | tf_op jit(solution)/shard_map/ppermute | solution.py:37
  34.1 10.2 %attend_line.1 = (bf16[4,640,128]{2,1,0:T(8,128)(2,1)}, f32[4,8,128]{2,1,0:T(8,128)}) custom-call(s32[4]{0:T(128)S(1)} %broadcast_select_fusion.4.qid.kid, s32[4]{0:T(128)S(1)} %broadcast_select_fusion.4.qid.kid, s32[256]{0:T(256)S(1)} %reshape.9.bs, s32[16]{0:T(128)S(1)} %copy-done, bf16[4,640,128]{2,1,0:T(8,128)(2,1)} %get-tuple-element.30.q, ...), custom_call_target="tpu_custom_call" | custom-call | flops 1845493760 | bytes 8388608 | tf_op jit(solution)/shard_map/attend_line/pallas_call | solution.py:236
  44.3 5.0 %attend_last_line.1 = (bf16[1,640,128]{2,1,0:T(8,128)(2,1)}, f32[1,8,128]{2,1,0:T(8,128)}, bf16[4,2,256,128]{3,2,1,0:T(8,128)(2,1)}, bf16[4,2,256,128]{3,2,1,0:T(8,128)(2,1)}, bf16[4,2,256,128]{3,2,1,0:T(8,128)(2,1)}) custom-call(s32[4]{0:T(128)S(1)} %broadcast_select_fusion.qid, s32[4]{0:T(128)S(1)} %broadcast_select_fusion.4.qid.kid, s32[256]{0:T(256)S(1)} %reshape.9.bs, ...), custom_call_target="tpu_custom_call" | custom-call | flops 461373440 | bytes 8388608 | tf_op jit(solution)/shard_map/attend_last_line/pallas_call | solution.py:256
  50.7 1.8 %collective-permute-start.12 = (bf16[4,2,256,128]{3,2,1,0:T(8,128)(2,1)}, bf16[4,2,256,128]{3,2,1,0:T(8,128)(2,1)S(1)}, u32[]{:S(2)}, u32[]{:S(2)}) collective-permute-start(bf16[4,2,256,128]{3,2,1,0:T(8,128)(2,1)} %get-tuple-element.41), channel_id=1, source_target_pairs={{0,96},{1,25},{2,98},{3,27},{4,100},{5,29},{6,102},{7,31},{8,104},... | collective-permute-start | bytes 1572872 | tf_op jit(solution)/shard_map/ppermute | solution.py:37
  52.5 9.1 %attend_groups.2 = (bf16[4,640,128]{2,1,0:T(8,128)(2,1)}, f32[4,8,128]{2,1,0:T(8,128)}) custom-call(s32[4]{0:T(128)S(1)} %broadcast_select_fusion.4.qid.kid, s32[4]{0:T(128)S(1)} %broadcast_select_fusion.1.kid, s32[256]{0:T(256)S(1)} %reshape.9.bs, s32[16]{0:T(128)S(1)} %copy-done, bf16[4,640,128]{2,1,0:T(8,128)(2,1)} %get-tuple-element.30.q, ...), custom_call_target="tpu_custom_call" | custom-call | flops 1342177280 | bytes 8388608 | tf_op jit(solution)/shard_map/attend_groups/pallas_call | solution.py:298
  62.3 10.6 %attend_groups.3 = (bf16[4,640,128]{2,1,0:T(8,128)(2,1)S(1)}, f32[8,128]{1,0:T(8,128)}) custom-call(s32[4]{0:T(128)S(1)} %broadcast_select_fusion.4.qid.kid, s32[8]{0:T(128)S(1)} %pad_add_fusion.kid, s32[256]{0:T(256)S(1)} %reshape.9.bs, s32[16]{0:T(128)S(1)} %copy-done, bf16[4,640,128]{2,1,0:T(8,128)(2,1)} %get-tuple-element.30.q, ...), custom_call_target="tpu_custom_call" | custom-call | flops 2684354560 | bytes 8388608 | tf_op jit(solution)/shard_map/attend_groups/pallas_call | solution.py:298
  73.6 1.9 %collective-permute-start.8 = (bf16[640,128]{1,0:T(8,128)(2,1)S(1)}, bf16[640,128]{1,0:T(8,128)(2,1)S(1)}, u32[]{:S(2)}, u32[]{:S(2)}) collective-permute-start(bf16[640,128]{1,0:T(8,128)(2,1)S(1)} %get-tuple-element.52), channel_id=1, source_target_pairs={{0,16},{1,65},{2,18},{3,67},{4,20},{5,69},{6,22},{7,71},{8,24},{9,... | collective-permute-start | bytes 491528 | tf_op jit(solution)/shard_map/ppermute | solution.py:33
  75.5 1.7 %collective-permute-start.9 = (bf16[640,128]{1,0:T(8,128)(2,1)S(1)}, bf16[640,128]{1,0:T(8,128)(2,1)S(1)}, u32[]{:S(2)}, u32[]{:S(2)}) collective-permute-start(bf16[640,128]{1,0:T(8,128)(2,1)S(1)} %get-tuple-element.51), channel_id=1, source_target_pairs={{0,8},{1,33},{2,10},{3,35},{4,12},{5,37},{6,14},{7,39},{8,16},{9,4... | collective-permute-start | bytes 491528 | tf_op jit(solution)/shard_map/ppermute | solution.py:33
  77.3 4.6 %attend_bands.1 = bf16[1,640,128]{2,1,0:T(8,128)(2,1)S(1)} custom-call(s32[1]{0:T(128)} %bitcast.7.qid, s32[12]{0:T(128)S(1)} %pad_add_fusion.1.kid, s32[256]{0:T(256)S(1)} %reshape.9.bs, s32[16]{0:T(128)S(1)} %copy-done, bf16[640,640]{1,0:T(8,128)(2,1)} %q.3, bf16[4,2,256,128]{3,2,1,0:T(8,128)(2,1)S(1)} %collective-permute-done.10.g1, ...), custom_call_target="tpu_custom_call" | custom-call | flops 1006632960 | bytes 8388608 | tf_op jit(solution)/shard_map/attend_bands/pallas_call | solution.py:327
  82.4 4.4 %collective-permute-start.13 = (bf16[640,640]{1,0:T(8,128)(2,1)S(1)}, bf16[640,640]{1,0:T(8,128)(2,1)S(1)}, u32[]{:S(2)}, u32[]{:S(2)}) collective-permute-start(bf16[640,640]{1,0:T(8,128)(2,1)S(1)} %assemble.1.att), channel_id=1, source_target_pairs={{0,1},{1,0},{2,3},{3,2},{4,5},{5,4},{6,7},{7,6},{8,9},{9,8},{10,11... | collective-permute-start | bytes 2457608 | tf_op jit(solution)/shard_map/ppermute | solution.py:45
  86.8 2.0 %collective-permute-done.13.att_other = bf16[640,640]{1,0:T(8,128)(2,1)S(1)} collective-permute-done((bf16[640,640]{1,0:T(8,128)(2,1)S(1)}, bf16[640,640]{1,0:T(8,128)(2,1)S(1)}, u32[]{:S(2)}, u32[]{:S(2)}) %collective-permute-start.13) | collective-permute-done | bytes 819232 | tf_op jit(solution)/shard_map/ppermute | solution.py:45
  88.7 3.0 %project.3.refs_0_ = bf16[1,640,640]{2,1,0:T(8,128)(2,1)S(1)} custom-call(s32[1]{0:T(128)S(6)} %select_n.152.order, s32[1]{0:T(128)S(6)} %add.225.blocks, bf16[640,640]{1,0:T(8,128)(2,1)S(1)} %assemble.1.att, bf16[640,640]{1,0:T(8,128)(2,1)S(1)} %collective-permute-done.13.att_other, bf16[640,5120]{1,0:T(8,128)(2,1)} %w_mine.5, ...), custom_call_target="tpu_custom_call" | custom-call | tf_op jit(solution)/shard_map/project/pallas_call | solution.py:375
  93.5 1.7 %collective-permute-start.15 = (bf16[320,640]{1,0:T(8,128)(2,1)S(1)}, bf16[320,640]{1,0:T(8,128)(2,1)S(1)}, u32[]{:S(2)}, u32[]{:S(2)}) collective-permute-start(bf16[320,640]{1,0:T(8,128)(2,1)S(1)} %get-tuple-element.49), channel_id=1, source_target_pairs={{0,6},{1,7},{2,0},{3,1},{4,2},{5,3},{6,4},{7,5},{8,14},{9,15},{10,... | collective-permute-start | bytes 1228808 | tf_op jit(solution)/shard_map/ppermute | solution.py:41
  95.2 5.2 %project.4.refs_0_.near = bf16[2,640,640]{2,1,0:T(8,128)(2,1)S(1)} custom-call(s32[2]{0:T(128)S(1)} %get-tuple-element.48.order, s32[2]{0:T(128)S(1)} %get-tuple-element.47.blocks, bf16[640,640]{1,0:T(8,128)(2,1)S(1)} %assemble.1.att, bf16[640,640]{1,0:T(8,128)(2,1)S(1)} %collective-permute-done.13.att_other, bf16[640,5120]{1,0:T(8,128)(2,1)} %w_mine.5, ...), custom_call_target="tpu_custom_call" | custom-call | tf_op jit(solution)/shard_map/project/pallas_call | solution.py:375
  100.4 4.5 %collective-permute-done.14.from_down = bf16[320,640]{1,0:T(8,128)(2,1)S(1)} collective-permute-done((bf16[320,640]{1,0:T(8,128)(2,1)S(1)}, bf16[320,640]{1,0:T(8,128)(2,1)S(1)}, u32[]{:S(2)}, u32[]{:S(2)}) %collective-permute-start.14) | collective-permute-done | bytes 409632 | tf_op jit(solution)/shard_map/ppermute | solution.py:41
  106.8 1.7 %collective-permute-start.17 = (bf16[640,640]{1,0:T(8,128)(2,1)S(1)}, bf16[640,640]{1,0:T(8,128)(2,1)S(1)}, u32[]{:S(2)}, u32[]{:S(2)}) collective-permute-start(bf16[640,640]{1,0:T(8,128)(2,1)S(1)} %get-tuple-element.46), channel_id=1, source_target_pairs={{0,6},{1,7},{2,0},{3,1},{4,2},{5,3},{6,4},{7,5},{8,14},{9,15},{10,... | collective-permute-start | bytes 2457608 | tf_op jit(solution)/shard_map/ppermute | solution.py:41
  108.5 3.0 %project.5 = bf16[1,640,640]{2,1,0:T(8,128)(2,1)S(1)} custom-call(s32[1]{0:T(128)S(6)} %select_n.128.order, s32[1]{0:T(128)S(6)} %add.186.blocks, bf16[640,640]{1,0:T(8,128)(2,1)S(1)} %assemble.1.att, bf16[640,640]{1,0:T(8,128)(2,1)S(1)} %collective-permute-done.13.att_other, bf16[640,5120]{1,0:T(8,128)(2,1)} %w_mine.5, ...), custom_call_target="tpu_custom_call" | custom-call | tf_op jit(solution)/shard_map/project/pallas_call | solution.py:375
  111.5 14.7 %collective-permute-done.16 = bf16[640,640]{1,0:T(8,128)(2,1)S(1)} collective-permute-done((bf16[640,640]{1,0:T(8,128)(2,1)S(1)}, bf16[640,640]{1,0:T(8,128)(2,1)S(1)}, u32[]{:S(2)}, u32[]{:S(2)}) %collective-permute-start.16) | collective-permute-done | bytes 819232 | tf_op jit(solution)/shard_map/ppermute | solution.py:41
  (41 shorter events, 12.7 us)
Async XLA Ops:
  0.0 34.1 %collective-permute-start.6 = (bf16[640,5120]{1,0:T(8,128)(2,1)}, bf16[640,5120]{1,0:T(8,128)(2,1)}, u32[]{:S(2)}, u32[]{:S(2)}) collective-permute-start(bf16[640,5120]{1,0:T(8,128)(2,1)} %w_mine.5), channel_id=1, source_target_pairs={{0,1},{1,0},{2,3},{3,2},{4,5},{5,4},{6,7},{7,6},{8,9},{9,8},{10,11... | collective-permute-start | bytes 19660808 | tf_op jit(solution)/shard_map/ppermute | solution.py:45
  2.0 20.7 %collective-permute-start = (bf16[5,640,128]{2,1,0:T(8,128)(2,1)S(1)}, bf16[5,640,128]{2,1,0:T(8,128)(2,1)S(1)}, u32[]{:S(2)}, u32[]{:S(2)}) collective-permute-start(bf16[5,640,128]{2,1,0:T(8,128)(2,1)S(1)} %get-tuple-element.27), channel_id=1, source_target_pairs={{0,8},{1,33},{2,10},{3,35},{4,12},{5,37},{6,14},{7,39},{8,16},{9,4... | collective-permute-start | bytes 2457608 | tf_op jit(solution)/shard_map/ppermute | solution.py:33
  4.0 18.7 %collective-permute-start.1 = (bf16[5,640,128]{2,1,0:T(8,128)(2,1)S(1)}, bf16[5,640,128]{2,1,0:T(8,128)(2,1)S(1)}, u32[]{:S(2)}, u32[]{:S(2)}) collective-permute-start(bf16[5,640,128]{2,1,0:T(8,128)(2,1)S(1)} %get-tuple-element.28), channel_id=1, source_target_pairs={{0,16},{1,65},{2,18},{3,67},{4,20},{5,69},{6,22},{7,71},{8,24},{9,... | collective-permute-start | bytes 2457608 | tf_op jit(solution)/shard_map/ppermute | solution.py:33
  5.1 21.1 %collective-permute-start.2 = (bf16[5,640,128]{2,1,0:T(8,128)(2,1)S(1)}, bf16[5,640,128]{2,1,0:T(8,128)(2,1)S(1)}, u32[]{:S(2)}, u32[]{:S(2)}) collective-permute-start(bf16[5,640,128]{2,1,0:T(8,128)(2,1)S(1)} %get-tuple-element.29), channel_id=1, source_target_pairs={{0,24},{1,97},{2,26},{3,99},{4,28},{5,101},{6,30},{7,103},{8,0},{9... | collective-permute-start | bytes 2457608 | tf_op jit(solution)/shard_map/ppermute | solution.py:33
  26.2 7.6 %copy-start.1 = (s32[16,16]{1,0:T(8,128)S(1)}, s32[16,16]{1,0:T(8,128)}, u32[]{:S(2)}) copy-start(s32[16,16]{1,0:T(8,128)} %param.13) | copy-start | bytes 3076
  26.2 7.9 %copy-start = (s32[16]{0:T(128)S(1)}, s32[16]{0:T(128)}, u32[]{:S(2)}) copy-start(s32[16]{0:T(128)} %bw.9) | copy-start | bytes 196
  28.1 22.6 %collective-permute-start.5 = (bf16[8,640,128]{2,1,0:T(8,128)(2,1)}, bf16[8,640,128]{2,1,0:T(8,128)(2,1)}, u32[]{:S(2)}, u32[]{:S(2)}) collective-permute-start(bf16[8,640,128]{2,1,0:T(8,128)(2,1)} %get-tuple-element.31.kv), channel_id=1, source_target_pairs={{0,32},{1,9},{2,34},{3,11},{4,36},{5,13},{6,38},{7,15},{8,40},{9,1... | collective-permute-start | bytes 3932168 | tf_op jit(solution)/shard_map/ppermute | solution.py:37
  29.7 32.7 %collective-permute-start.3 = (bf16[8,640,128]{2,1,0:T(8,128)(2,1)}, bf16[8,640,128]{2,1,0:T(8,128)(2,1)S(1)}, u32[]{:S(2)}, u32[]{:S(2)}) collective-permute-start(bf16[8,640,128]{2,1,0:T(8,128)(2,1)} %get-tuple-element.31.kv), channel_id=1, source_target_pairs={{0,64},{1,17},{2,66},{3,19},{4,68},{5,21},{6,70},{7,23},{8,72},{9,... | collective-permute-start | bytes 3932168 | tf_op jit(solution)/shard_map/ppermute | solution.py:37
  32.4 29.9 %collective-permute-start.4 = (bf16[8,640,128]{2,1,0:T(8,128)(2,1)}, bf16[8,640,128]{2,1,0:T(8,128)(2,1)S(1)}, u32[]{:S(2)}, u32[]{:S(2)}) collective-permute-start(bf16[8,640,128]{2,1,0:T(8,128)(2,1)} %get-tuple-element.31.kv), channel_id=1, source_target_pairs={{0,96},{1,25},{2,98},{3,27},{4,100},{5,29},{6,102},{7,31},{8,104},... | collective-permute-start | bytes 3932168 | tf_op jit(solution)/shard_map/ppermute | solution.py:37
  49.2 26.2 %collective-permute-start.10 = (bf16[4,2,256,128]{3,2,1,0:T(8,128)(2,1)}, bf16[4,2,256,128]{3,2,1,0:T(8,128)(2,1)S(1)}, u32[]{:S(2)}, u32[]{:S(2)}) collective-permute-start(bf16[4,2,256,128]{3,2,1,0:T(8,128)(2,1)} %get-tuple-element.39), channel_id=1, source_target_pairs={{0,32},{1,9},{2,34},{3,11},{4,36},{5,13},{6,38},{7,15},{8,40},{9,1... | collective-permute-start | bytes 1572872 | tf_op jit(solution)/shard_map/ppermute | solution.py:37
  49.8 27.4 %collective-permute-start.11 = (bf16[4,2,256,128]{3,2,1,0:T(8,128)(2,1)}, bf16[4,2,256,128]{3,2,1,0:T(8,128)(2,1)S(1)}, u32[]{:S(2)}, u32[]{:S(2)}) collective-permute-start(bf16[4,2,256,128]{3,2,1,0:T(8,128)(2,1)} %get-tuple-element.40), channel_id=1, source_target_pairs={{0,64},{1,17},{2,66},{3,19},{4,68},{5,21},{6,70},{7,23},{8,72},{9,... | collective-permute-start | bytes 1572872 | tf_op jit(solution)/shard_map/ppermute | solution.py:37
  50.7 26.6 %collective-permute-start.12 = (bf16[4,2,256,128]{3,2,1,0:T(8,128)(2,1)}, bf16[4,2,256,128]{3,2,1,0:T(8,128)(2,1)S(1)}, u32[]{:S(2)}, u32[]{:S(2)}) collective-permute-start(bf16[4,2,256,128]{3,2,1,0:T(8,128)(2,1)} %get-tuple-element.41), channel_id=1, source_target_pairs={{0,96},{1,25},{2,98},{3,27},{4,100},{5,29},{6,102},{7,31},{8,104},... | collective-permute-start | bytes 1572872 | tf_op jit(solution)/shard_map/ppermute | solution.py:37
  73.0 8.9 %collective-permute-start.7 = (bf16[640,128]{1,0:T(8,128)(2,1)S(1)}, bf16[640,128]{1,0:T(8,128)(2,1)S(1)}, u32[]{:S(2)}, u32[]{:S(2)}) collective-permute-start(bf16[640,128]{1,0:T(8,128)(2,1)S(1)} %get-tuple-element.53), channel_id=1, source_target_pairs={{0,24},{1,97},{2,26},{3,99},{4,28},{5,101},{6,30},{7,103},{8,0},{9... | collective-permute-start | bytes 491528 | tf_op jit(solution)/shard_map/ppermute | solution.py:33
  73.6 8.3 %collective-permute-start.8 = (bf16[640,128]{1,0:T(8,128)(2,1)S(1)}, bf16[640,128]{1,0:T(8,128)(2,1)S(1)}, u32[]{:S(2)}, u32[]{:S(2)}) collective-permute-start(bf16[640,128]{1,0:T(8,128)(2,1)S(1)} %get-tuple-element.52), channel_id=1, source_target_pairs={{0,16},{1,65},{2,18},{3,67},{4,20},{5,69},{6,22},{7,71},{8,24},{9,... | collective-permute-start | bytes 491528 | tf_op jit(solution)/shard_map/ppermute | solution.py:33
  75.5 6.7 %collective-permute-start.9 = (bf16[640,128]{1,0:T(8,128)(2,1)S(1)}, bf16[640,128]{1,0:T(8,128)(2,1)S(1)}, u32[]{:S(2)}, u32[]{:S(2)}) collective-permute-start(bf16[640,128]{1,0:T(8,128)(2,1)S(1)} %get-tuple-element.51), channel_id=1, source_target_pairs={{0,8},{1,33},{2,10},{3,35},{4,12},{5,37},{6,14},{7,39},{8,16},{9,4... | collective-permute-start | bytes 491528 | tf_op jit(solution)/shard_map/ppermute | solution.py:33
  82.4 6.3 %collective-permute-start.13 = (bf16[640,640]{1,0:T(8,128)(2,1)S(1)}, bf16[640,640]{1,0:T(8,128)(2,1)S(1)}, u32[]{:S(2)}, u32[]{:S(2)}) collective-permute-start(bf16[640,640]{1,0:T(8,128)(2,1)S(1)} %assemble.1.att), channel_id=1, source_target_pairs={{0,1},{1,0},{2,3},{3,2},{4,5},{5,4},{6,7},{7,6},{8,9},{9,8},{10,11... | collective-permute-start | bytes 2457608 | tf_op jit(solution)/shard_map/ppermute | solution.py:45
  91.7 3.4 %copy-start.2 = (s32[2]{0:T(128)S(1)}, s32[2]{0:T(128)}, u32[]{:S(2)}) copy-start(s32[2]{0:T(128)} %constant.180.clone) | copy-start | bytes 28
  91.8 13.1 %collective-permute-start.14 = (bf16[320,640]{1,0:T(8,128)(2,1)S(1)}, bf16[320,640]{1,0:T(8,128)(2,1)S(1)}, u32[]{:S(2)}, u32[]{:S(2)}) collective-permute-start(bf16[320,640]{1,0:T(8,128)(2,1)S(1)} %get-tuple-element.50), channel_id=1, source_target_pairs={{0,2},{1,3},{2,4},{3,5},{4,6},{5,7},{6,0},{7,1},{8,10},{9,11},{10,... | collective-permute-start | bytes 1228808 | tf_op jit(solution)/shard_map/ppermute | solution.py:41
  93.5 11.5 %collective-permute-start.15 = (bf16[320,640]{1,0:T(8,128)(2,1)S(1)}, bf16[320,640]{1,0:T(8,128)(2,1)S(1)}, u32[]{:S(2)}, u32[]{:S(2)}) collective-permute-start(bf16[320,640]{1,0:T(8,128)(2,1)S(1)} %get-tuple-element.49), channel_id=1, source_target_pairs={{0,6},{1,7},{2,0},{3,1},{4,2},{5,3},{6,4},{7,5},{8,14},{9,15},{10,... | collective-permute-start | bytes 1228808 | tf_op jit(solution)/shard_map/ppermute | solution.py:41
  105.2 21.0 %collective-permute-start.16 = (bf16[640,640]{1,0:T(8,128)(2,1)S(1)}, bf16[640,640]{1,0:T(8,128)(2,1)S(1)}, u32[]{:S(2)}, u32[]{:S(2)}) collective-permute-start(bf16[640,640]{1,0:T(8,128)(2,1)S(1)} %get-tuple-element.45), channel_id=1, source_target_pairs={{0,2},{1,3},{2,4},{3,5},{4,6},{5,7},{6,0},{7,1},{8,10},{9,11},{10,... | collective-permute-start | bytes 2457608 | tf_op jit(solution)/shard_map/ppermute | solution.py:41
  106.8 19.4 %collective-permute-start.17 = (bf16[640,640]{1,0:T(8,128)(2,1)S(1)}, bf16[640,640]{1,0:T(8,128)(2,1)S(1)}, u32[]{:S(2)}, u32[]{:S(2)}) collective-permute-start(bf16[640,640]{1,0:T(8,128)(2,1)S(1)} %get-tuple-element.46), channel_id=1, source_target_pairs={{0,6},{1,7},{2,0},{3,1},{4,2},{5,3},{6,4},{7,5},{8,14},{9,15},{10,... | collective-permute-start | bytes 2457608 | tf_op jit(solution)/shard_map/ppermute | solution.py:41

commit v5 on v4

--- a/solution.py
+++ b/solution.py
@@ -90,28 +90,26 @@
     )(pos, *in_hbm(queries, keys, values))
 
 
-def stack_kernel(*refs):
-    pieces, (q, kv, k_last, v_last, sems) = refs[:SIDE], refs[SIDE:]
+def stack_kernel(parts, *refs):
+    pieces, outs, sems = refs[:SIDE], refs[SIDE:-1], refs[-1]
     copies = []
-    for s, piece in enumerate(pieces):
-        targets = (q.at[s], kv.at[s], kv.at[SIDE + s], k_last.at[s], v_last.at[s])
-        for j, target in enumerate(targets):
-            copies.append(pltpu.make_async_copy(piece.at[j], target, sems.at[s, j]))
+    for out, rows in zip(outs, parts):
+        for j, part in enumerate(rows):
+            for s, piece in enumerate(pieces):
+                copies.append(pltpu.make_async_copy(piece.at[part], out.at[j * SIDE + s], sems.at[len(copies)]))
     for copy in copies:
         copy.start()
     for copy in copies:
         copy.wait()
 
 
-def stack(pieces):
-    shape = (SIDE, FT, HD)
-    both = (2 * SIDE, FT, HD)
-    return pl.pallas_call(
-        stack_kernel,
+def stack(pieces, *parts):
+    return pl.pallas_call(
+        functools.partial(stack_kernel, parts),
         in_specs=[VMEM] * SIDE,
-        out_specs=[ANY] * 4,
-        out_shape=[pltpu.HBM(s, jnp.bfloat16) for s in (shape, both, shape, shape)],
-        scratch_shapes=[pltpu.SemaphoreType.DMA((SIDE, 5))],
+        out_specs=[ANY] * len(parts),
+        out_shape=[pltpu.HBM((SIDE * len(rows), FT, HD), jnp.bfloat16) for rows in parts],
+        scratch_shapes=[pltpu.SemaphoreType.DMA((SIDE * sum(map(len, parts)),))],
         compiler_params=pltpu.CompilerParams(vmem_limit_bytes=LIMIT),
         name="stack",
     )(*pieces)
@@ -392,6 +390,42 @@
     )(order, 2 * order + core, att, att_other, *in_hbm(weight, other_weight), *after)
 
 
+def first_share_kernel(blocks, att, weight, other, base, later):
+    del blocks
+    base[...] = jnp.dot(att[...], weight[...], preferred_element_type=jnp.float32)
+    later[...] = other[...]
+
+
+def first_share(blocks, att, weight, other_weight):
+    width = weight.shape[1] // 8
+    block = pl.BlockSpec((5 * HD, width), lambda i, blocks: (0, blocks[0]))
+    return pl.pallas_call(
+        first_share_kernel,
+        grid_spec=pltpu.PrefetchScalarGridSpec(
+            num_scalar_prefetch=1, grid=(1,), in_specs=[VMEM, block, block], out_specs=[VMEM] * 2
+        ),
+        out_shape=[pltpu.VMEM((FT, width), jnp.float32), pltpu.VMEM((5 * HD, width), jnp.bfloat16)],
+        compiler_params=pltpu.CompilerParams(vmem_limit_bytes=LIMIT),
+        name="first_share",
+    )(blocks, att, *in_hbm(weight, other_weight))
+
+
+def second_share_kernel(att_other, base, weight, out):
+    total = base[...] + jnp.dot(att_other[...], weight[...], preferred_element_type=jnp.float32)
+    out[...] = total.astype(jnp.bfloat16)
+
+
+def second_share(att_other, base, weight):
+    return pl.pallas_call(
+        second_share_kernel,
+        in_specs=[VMEM] * 3,
+        out_specs=VMEM,
+        out_shape=pltpu.VMEM(base.shape, jnp.bfloat16),
+        compiler_params=pltpu.CompilerParams(vmem_limit_bytes=LIMIT),
+        name="second_share",
+    )(att_other, base, weight)
+
+
 def add(*terms):
     total = terms[0].astype(jnp.float32)
     for t in terms[1:]:
@@ -437,11 +471,13 @@
     bs, bw = band_start.reshape(-1), band_width
 
     pieces = pick(line[None], queries, key_rows, value_rows)
-    pieces = [pieces[0]] + [line_shift(pieces[s], s) for s in range(1, SIDE)]
+    one, three = line_shift(pieces[1], 1), line_shift(pieces[3], 3)
+    pieces = [pieces[0], one, line_shift(pieces[2], 2), three]
 
     other_weight = core_swap(out_weight)
 
-    q, kv, k_last, v_last = stack(pieces)
+    (kv,) = stack(pieces, (1, 2))
+    q, k_last, v_last = stack(pieces, (0,), (3,), (4,))
 
     groups = [cross_shift(kv, s) for s in range(1, SIDE)]
     state = attend_line(f0, f0, bs, bw, q, kv, other_weight)
@@ -464,8 +500,9 @@
         return project(order, core, att, att_other, out_weight, other_weight, *after)
 
     half = FT // 2
-    two = share([2])
-    from_down, from_up = y_shift(two[0, :half], 1), y_shift(two[0, half:], 3)
+    far = (y[None] + 2) % SIDE * 2 + core
+    two = second_share(att_other, *first_share(far, att, out_weight, other_weight))
+    from_down, from_up = y_shift(two[:half], 1), y_shift(two[half:], 3)
     near = share([1, 3], two)
     send_up, send_down = onward(near, from_down, from_up)
     own = share([0], near)

time: 128 us -> 126 us (0.984)
  waiting for transfers between devices: 40.8 us -> 37.5 us
  Pallas kernels: 54.9 us -> 56.7 us
    pallas_call x1 -> x4, Pallas kernels: 1.86 us -> 5.72 us  [the longest x2 2.5 us: stack(): pl.pallas_call(functools.partial(stack_kernel, parts), in_specs=[VMEM] *...]
    pallas_call x3 -> x2, Pallas kernels: 11.3 us -> 8.25 us  [project(): pl.pallas_call(project_kernel, grid_spec=pltpu.PrefetchScalarGridSpec(num...]
    ppermute x2, waiting for transfers between devices: 1.96 us -> 0.01 us  [core_swap(): return lax.ppermute(v, BOTH, pairs(lambda x, z, y, c: (x, z, y, 1 - c)))]
  transfers between devices with their start and end apart: 18 -> 18, of which waited for: 7 -> 5; matrix products, arithmetic and copies ran while one was open for 0% -> 0% of each run, Pallas kernels for 40% -> 44%
where the time goes in v5:
time: 126 us; the launch traced here: 125 us
  Pallas kernels  56.7 us (45%)
  waiting for transfers between devices  37.5 us (30%)
  starting transfers between devices  29.2 us (23%)
  other arithmetic  1.43 us (1%)
    pallas_call x2, Pallas kernels, attend_groups(): pl.pallas_call(functools.partial(groups_kernel, len(groups), finished), g...  20.6 us
    ppermute x6, waiting for transfers between devices, line_shift(): lax.ppermute(v, BOTH, pairs(lambda x, z, y, c: (x, z + s, y, c) if c == 0...  18.9 us
    ppermute x4, waiting for transfers between devices, y_shift(): return lax.ppermute(v, BOTH, pairs(lambda x, z, y, c: (x, z, y + s, c)))  18.6 us
    pallas_call x1, Pallas kernels, attend_line(): pl.pallas_call(line_kernel, grid_spec=pltpu.PrefetchScalarGridSpec(num_sc...  10.2 us
    ppermute x6, starting transfers between devices, line_shift(): lax.ppermute(v, BOTH, pairs(lambda x, z, y, c: (x, z + s, y, c) if c == 0...  9.88 us
    ppermute x6, starting transfers between devices, cross_shift(): lax.ppermute(v, BOTH, pairs(lambda x, z, y, c: (x + s, z, y, c) if c == 0...  8.99 us
    pallas_call x2, Pallas kernels, project(): pl.pallas_call(project_kernel, grid_spec=pltpu.PrefetchScalarGridSpec(num...  8.25 us
    ppermute x4, starting transfers between devices, y_shift(): return lax.ppermute(v, BOTH, pairs(lambda x, z, y, c: (x, z, y + s, c)))  6.61 us
  transfers between devices with their start and end apart: 18, of which 5 were waited for; matrix products, arithmetic and copies ran while one was open for 0% of the time, Pallas kernels for 44%

profile of v5, /device:TPU:32, one launch (start us, length us, event | category | flops | bytes accessed | tf_op | source)
XLA Modules:
  0.0 125.2 jit_solution(4310263446177688315)
XLA Ops:
  0.0 2.0 %pick.1 = (bf16[5,640,128]{2,1,0:T(8,128)(2,1)S(1)}, bf16[5,640,128]{2,1,0:T(8,128)(2,1)S(1)}, bf16[5,640,128]{2,1,0:T(8,128)(2,1)S(1)}, bf16[5,640,128]{2,1,0:T(8,128)(2,1)S(1)}) custom-call(s32[1]{0:T(128)} %bitcast.2.pos, bf16[640,640]{1,0:T(8,128)(2,1)} %q.3, bf16[640,640]{1,0:T(8,128)(2,1)} %k_any.1, bf16[640,640]{1,0:T(8,128)(2,1)} %v_any.1), custom_call_target="tpu_custom_call" | custom-call | tf_op jit(solution)/shard_map/pick/pallas_call | solution.py:82
  2.0 2.0 %collective-permute-start = (bf16[5,640,128]{2,1,0:T(8,128)(2,1)S(1)}, bf16[5,640,128]{2,1,0:T(8,128)(2,1)S(1)}, u32[]{:S(2)}, u32[]{:S(2)}) collective-permute-start(bf16[5,640,128]{2,1,0:T(8,128)(2,1)S(1)} %get-tuple-element.28), channel_id=1, source_target_pairs={{0,8},{1,33},{2,10},{3,35},{4,12},{5,37},{6,14},{7,39},{8,16},{9,4... | collective-permute-start | bytes 2457608 | tf_op jit(solution)/shard_map/ppermute | solution.py:33
  5.1 2.5 %collective-permute-start.2 = (bf16[5,640,128]{2,1,0:T(8,128)(2,1)S(1)}, bf16[5,640,128]{2,1,0:T(8,128)(2,1)S(1)}, u32[]{:S(2)}, u32[]{:S(2)}) collective-permute-start(bf16[5,640,128]{2,1,0:T(8,128)(2,1)S(1)} %get-tuple-element.30), channel_id=1, source_target_pairs={{0,24},{1,97},{2,26},{3,99},{4,28},{5,101},{6,30},{7,103},{8,0},{9... | collective-permute-start | bytes 2457608 | tf_op jit(solution)/shard_map/ppermute | solution.py:33
  7.6 15.0 %collective-permute-done.refs_1_ = bf16[5,640,128]{2,1,0:T(8,128)(2,1)S(1)} collective-permute-done((bf16[5,640,128]{2,1,0:T(8,128)(2,1)S(1)}, bf16[5,640,128]{2,1,0:T(8,128)(2,1)S(1)}, u32[]{:S(2)}, u32[]{:S(2)}) %collective-permute-start) | collective-permute-done | bytes 819232 | tf_op jit(solution)/shard_map/ppermute | solution.py:33
  22.6 3.6 %collective-permute-done.2.refs_3_ = bf16[5,640,128]{2,1,0:T(8,128)(2,1)S(1)} collective-permute-done((bf16[5,640,128]{2,1,0:T(8,128)(2,1)S(1)}, bf16[5,640,128]{2,1,0:T(8,128)(2,1)S(1)}, u32[]{:S(2)}, u32[]{:S(2)}) %collective-permute-start.2) | collective-permute-done | bytes 819232 | tf_op jit(solution)/shard_map/ppermute | solution.py:33
  28.9 2.7 %collective-permute-start.3 = (bf16[8,640,128]{2,1,0:T(8,128)(2,1)}, bf16[8,640,128]{2,1,0:T(8,128)(2,1)}, u32[]{:S(2)}, u32[]{:S(2)}) collective-permute-start(bf16[8,640,128]{2,1,0:T(8,128)(2,1)} %stack.3.kv), channel_id=1, source_target_pairs={{0,64},{1,17},{2,66},{3,19},{4,68},{5,21},{6,70},{7,23},{8,72},{9,... | collective-permute-start | bytes 3932168 | tf_op jit(solution)/shard_map/ppermute | solution.py:37
  34.7 10.2 %attend_line.1 = (bf16[4,640,128]{2,1,0:T(8,128)(2,1)}, f32[4,8,128]{2,1,0:T(8,128)}) custom-call(s32[4]{0:T(128)S(1)} %broadcast_select_fusion.4.qid.kid, s32[4]{0:T(128)S(1)} %broadcast_select_fusion.4.qid.kid, s32[256]{0:T(256)S(1)} %reshape.9.bs, s32[16]{0:T(128)S(1)} %copy-done, bf16[4,640,128]{2,1,0:T(8,128)(2,1)} %get-tuple-element.31.q, ...), custom_call_target="tpu_custom_call" | custom-call | flops 1845493760 | bytes 8388608 | tf_op jit(solution)/shard_map/attend_line/pallas_call | solution.py:234
  44.9 4.9 %attend_last_line.1 = (bf16[1,640,128]{2,1,0:T(8,128)(2,1)}, f32[1,8,128]{2,1,0:T(8,128)}, bf16[4,2,256,128]{3,2,1,0:T(8,128)(2,1)}, bf16[4,2,256,128]{3,2,1,0:T(8,128)(2,1)}, bf16[4,2,256,128]{3,2,1,0:T(8,128)(2,1)}) custom-call(s32[4]{0:T(128)S(1)} %broadcast_select_fusion.qid, s32[4]{0:T(128)S(1)} %broadcast_select_fusion.4.qid.kid, s32[256]{0:T(256)S(1)} %reshape.9.bs, ...), custom_call_target="tpu_custom_call" | custom-call | flops 461373440 | bytes 8388608 | tf_op jit(solution)/shard_map/attend_last_line/pallas_call | solution.py:254
  51.3 1.8 %collective-permute-start.12 = (bf16[4,2,256,128]{3,2,1,0:T(8,128)(2,1)}, bf16[4,2,256,128]{3,2,1,0:T(8,128)(2,1)S(1)}, u32[]{:S(2)}, u32[]{:S(2)}) collective-permute-start(bf16[4,2,256,128]{3,2,1,0:T(8,128)(2,1)} %get-tuple-element.41), channel_id=1, source_target_pairs={{0,96},{1,25},{2,98},{3,27},{4,100},{5,29},{6,102},{7,31},{8,104},... | collective-permute-start | bytes 1572872 | tf_op jit(solution)/shard_map/ppermute | solution.py:37
  53.1 9.1 %attend_groups.2 = (bf16[4,640,128]{2,1,0:T(8,128)(2,1)}, f32[4,8,128]{2,1,0:T(8,128)}) custom-call(s32[4]{0:T(128)S(1)} %broadcast_select_fusion.4.qid.kid, s32[4]{0:T(128)S(1)} %broadcast_select_fusion.1.kid, s32[256]{0:T(256)S(1)} %reshape.9.bs, s32[16]{0:T(128)S(1)} %copy-done, bf16[4,640,128]{2,1,0:T(8,128)(2,1)} %get-tuple-element.31.q, ...), custom_call_target="tpu_custom_call" | custom-call | flops 1342177280 | bytes 8388608 | tf_op jit(solution)/shard_map/attend_groups/pallas_call | solution.py:296
  62.3 11.5 %attend_groups.3 = (bf16[4,640,128]{2,1,0:T(8,128)(2,1)S(1)}, f32[8,128]{1,0:T(8,128)}) custom-call(s32[4]{0:T(128)S(1)} %broadcast_select_fusion.4.qid.kid, s32[8]{0:T(128)S(1)} %pad_add_fusion.kid, s32[256]{0:T(256)S(1)} %reshape.9.bs, s32[16]{0:T(128)S(1)} %copy-done, bf16[4,640,128]{2,1,0:T(8,128)(2,1)} %get-tuple-element.31.q, ...), custom_call_target="tpu_custom_call" | custom-call | flops 2684354560 | bytes 8388608 | tf_op jit(solution)/shard_map/attend_groups/pallas_call | solution.py:296
  74.4 1.9 %collective-permute-start.8 = (bf16[640,128]{1,0:T(8,128)(2,1)S(1)}, bf16[640,128]{1,0:T(8,128)(2,1)S(1)}, u32[]{:S(2)}, u32[]{:S(2)}) collective-permute-start(bf16[640,128]{1,0:T(8,128)(2,1)S(1)} %get-tuple-element.54), channel_id=1, source_target_pairs={{0,16},{1,65},{2,18},{3,67},{4,20},{5,69},{6,22},{7,71},{8,24},{9,... | collective-permute-start | bytes 491528 | tf_op jit(solution)/shard_map/ppermute | solution.py:33
  76.3 1.7 %collective-permute-start.9 = (bf16[640,128]{1,0:T(8,128)(2,1)S(1)}, bf16[640,128]{1,0:T(8,128)(2,1)S(1)}, u32[]{:S(2)}, u32[]{:S(2)}) collective-permute-start(bf16[640,128]{1,0:T(8,128)(2,1)S(1)} %get-tuple-element.53), channel_id=1, source_target_pairs={{0,8},{1,33},{2,10},{3,35},{4,12},{5,37},{6,14},{7,39},{8,16},{9,4... | collective-permute-start | bytes 491528 | tf_op jit(solution)/shard_map/ppermute | solution.py:33
  78.1 4.6 %attend_bands.1 = bf16[1,640,128]{2,1,0:T(8,128)(2,1)S(1)} custom-call(s32[1]{0:T(128)} %bitcast.7.qid, s32[12]{0:T(128)S(1)} %pad_add_fusion.1.kid, s32[256]{0:T(256)S(1)} %reshape.9.bs, s32[16]{0:T(128)S(1)} %copy-done, bf16[640,640]{1,0:T(8,128)(2,1)} %q.3, bf16[4,2,256,128]{3,2,1,0:T(8,128)(2,1)S(1)} %collective-permute-done.10.g1, ...), custom_call_target="tpu_custom_call" | custom-call | flops 1006632960 | bytes 8388608 | tf_op jit(solution)/shard_map/attend_bands/pallas_call | solution.py:325
  83.2 3.7 %collective-permute-start.13 = (bf16[640,640]{1,0:T(8,128)(2,1)S(1)}, bf16[640,640]{1,0:T(8,128)(2,1)S(1)}, u32[]{:S(2)}, u32[]{:S(2)}) collective-permute-start(bf16[640,640]{1,0:T(8,128)(2,1)S(1)} %assemble.1.att), channel_id=1, source_target_pairs={{0,1},{1,0},{2,3},{3,2},{4,5},{5,4},{6,7},{7,6},{8,9},{9,8},{10,11... | collective-permute-start | bytes 2457608 | tf_op jit(solution)/shard_map/ppermute | solution.py:45
  87.0 2.3 %first_share.1 = (f32[640,640]{1,0:T(8,128)S(1)}, bf16[640,640]{1,0:T(8,128)(2,1)S(1)}) custom-call(s32[1]{0:T(128)S(6)} %add.224.blocks, bf16[640,640]{1,0:T(8,128)(2,1)S(1)} %assemble.1.att, bf16[640,5120]{1,0:T(8,128)(2,1)} %w_mine.3, bf16[640,5120]{1,0:T(8,128)(2,1)} %collective-permute-done.6.after.other.w_other), custom_call_target="tpu_custom_call" | custom-call | tf_op jit(solution)/shard_map/first_share/pallas_call | solution.py:402
  90.3 1.6 %collective-permute-start.14 = (bf16[320,640]{1,0:T(8,128)(2,1)S(1)}, bf16[320,640]{1,0:T(8,128)(2,1)S(1)}, u32[]{:S(2)}, u32[]{:S(2)}) collective-permute-start(bf16[320,640]{1,0:T(8,128)(2,1)S(1)} %get-tuple-element.52), channel_id=1, source_target_pairs={{0,2},{1,3},{2,4},{3,5},{4,6},{5,7},{6,0},{7,1},{8,10},{9,11},{10,... | collective-permute-start | bytes 1228808 | tf_op jit(solution)/shard_map/ppermute | solution.py:41
  92.0 1.7 %collective-permute-start.15 = (bf16[320,640]{1,0:T(8,128)(2,1)S(1)}, bf16[320,640]{1,0:T(8,128)(2,1)S(1)}, u32[]{:S(2)}, u32[]{:S(2)}) collective-permute-start(bf16[320,640]{1,0:T(8,128)(2,1)S(1)} %get-tuple-element.51), channel_id=1, source_target_pairs={{0,6},{1,7},{2,0},{3,1},{4,2},{5,3},{6,4},{7,5},{8,14},{9,15},{10,... | collective-permute-start | bytes 1228808 | tf_op jit(solution)/shard_map/ppermute | solution.py:41
  93.6 5.2 %project.2.refs_0_.near = bf16[2,640,640]{2,1,0:T(8,128)(2,1)S(1)} custom-call(s32[2]{0:T(128)S(1)} %get-tuple-element.50.order, s32[2]{0:T(128)S(1)} %get-tuple-element.49.blocks, bf16[640,640]{1,0:T(8,128)(2,1)S(1)} %assemble.1.att, bf16[640,640]{1,0:T(8,128)(2,1)S(1)} %collective-permute-done.13.att_other, bf16[640,5120]{1,0:T(8,128)(2,1)} %w_mine.3, ...), custom_call_target="tpu_custom_call" | custom-call | tf_op jit(solution)/shard_map/project/pallas_call | solution.py:373
  98.9 4.2 %collective-permute-done.14.from_down = bf16[320,640]{1,0:T(8,128)(2,1)S(1)} collective-permute-done((bf16[320,640]{1,0:T(8,128)(2,1)S(1)}, bf16[320,640]{1,0:T(8,128)(2,1)S(1)}, u32[]{:S(2)}, u32[]{:S(2)}) %collective-permute-start.14) | collective-permute-done | bytes 409632 | tf_op jit(solution)/shard_map/ppermute | solution.py:41
  103.3 1.6 %collective-permute-start.16 = (bf16[640,640]{1,0:T(8,128)(2,1)S(1)}, bf16[640,640]{1,0:T(8,128)(2,1)S(1)}, u32[]{:S(2)}, u32[]{:S(2)}) collective-permute-start(bf16[640,640]{1,0:T(8,128)(2,1)S(1)} %get-tuple-element.47), channel_id=1, source_target_pairs={{0,2},{1,3},{2,4},{3,5},{4,6},{5,7},{6,0},{7,1},{8,10},{9,11},{10,... | collective-permute-start | bytes 2457608 | tf_op jit(solution)/shard_map/ppermute | solution.py:41
  105.0 1.7 %collective-permute-start.17 = (bf16[640,640]{1,0:T(8,128)(2,1)S(1)}, bf16[640,640]{1,0:T(8,128)(2,1)S(1)}, u32[]{:S(2)}, u32[]{:S(2)}) collective-permute-start(bf16[640,640]{1,0:T(8,128)(2,1)S(1)} %get-tuple-element.48), channel_id=1, source_target_pairs={{0,6},{1,7},{2,0},{3,1},{4,2},{5,3},{6,4},{7,5},{8,14},{9,15},{10,... | collective-permute-start | bytes 2457608 | tf_op jit(solution)/shard_map/ppermute | solution.py:41
  106.6 3.0 %project.3 = bf16[1,640,640]{2,1,0:T(8,128)(2,1)S(1)} custom-call(s32[1]{0:T(128)S(6)} %select_n.128.order, s32[1]{0:T(128)S(6)} %add.185.blocks, bf16[640,640]{1,0:T(8,128)(2,1)S(1)} %assemble.1.att, bf16[640,640]{1,0:T(8,128)(2,1)S(1)} %collective-permute-done.13.att_other, bf16[640,5120]{1,0:T(8,128)(2,1)} %w_mine.3, ...), custom_call_target="tpu_custom_call" | custom-call | tf_op jit(solution)/shard_map/project/pallas_call | solution.py:373
  109.7 14.4 %collective-permute-done.16 = bf16[640,640]{1,0:T(8,128)(2,1)S(1)} collective-permute-done((bf16[640,640]{1,0:T(8,128)(2,1)S(1)}, bf16[640,640]{1,0:T(8,128)(2,1)S(1)}, u32[]{:S(2)}, u32[]{:S(2)}) %collective-permute-start.16) | collective-permute-done | bytes 819232 | tf_op jit(solution)/shard_map/ppermute | solution.py:41
  (43 shorter events, 12.0 us)
Async XLA Ops:
  0.0 34.7 %collective-permute-start.6 = (bf16[640,5120]{1,0:T(8,128)(2,1)}, bf16[640,5120]{1,0:T(8,128)(2,1)}, u32[]{:S(2)}, u32[]{:S(2)}) collective-permute-start(bf16[640,5120]{1,0:T(8,128)(2,1)} %w_mine.3), channel_id=1, source_target_pairs={{0,1},{1,0},{2,3},{3,2},{4,5},{5,4},{6,7},{7,6},{8,9},{9,8},{10,11... | collective-permute-start | bytes 19660808 | tf_op jit(solution)/shard_map/ppermute | solution.py:45
  2.0 20.7 %collective-permute-start = (bf16[5,640,128]{2,1,0:T(8,128)(2,1)S(1)}, bf16[5,640,128]{2,1,0:T(8,128)(2,1)S(1)}, u32[]{:S(2)}, u32[]{:S(2)}) collective-permute-start(bf16[5,640,128]{2,1,0:T(8,128)(2,1)S(1)} %get-tuple-element.28), channel_id=1, source_target_pairs={{0,8},{1,33},{2,10},{3,35},{4,12},{5,37},{6,14},{7,39},{8,16},{9,4... | collective-permute-start | bytes 2457608 | tf_op jit(solution)/shard_map/ppermute | solution.py:33
  4.0 18.7 %collective-permute-start.1 = (bf16[5,640,128]{2,1,0:T(8,128)(2,1)S(1)}, bf16[5,640,128]{2,1,0:T(8,128)(2,1)S(1)}, u32[]{:S(2)}, u32[]{:S(2)}) collective-permute-start(bf16[5,640,128]{2,1,0:T(8,128)(2,1)S(1)} %get-tuple-element.29), channel_id=1, source_target_pairs={{0,16},{1,65},{2,18},{3,67},{4,20},{5,69},{6,22},{7,71},{8,24},{9,... | collective-permute-start | bytes 2457608 | tf_op jit(solution)/shard_map/ppermute | solution.py:33
  5.1 21.1 %collective-permute-start.2 = (bf16[5,640,128]{2,1,0:T(8,128)(2,1)S(1)}, bf16[5,640,128]{2,1,0:T(8,128)(2,1)S(1)}, u32[]{:S(2)}, u32[]{:S(2)}) collective-permute-start(bf16[5,640,128]{2,1,0:T(8,128)(2,1)S(1)} %get-tuple-element.30), channel_id=1, source_target_pairs={{0,24},{1,97},{2,26},{3,99},{4,28},{5,101},{6,30},{7,103},{8,0},{9... | collective-permute-start | bytes 2457608 | tf_op jit(solution)/shard_map/ppermute | solution.py:33
  26.2 6.9 %copy-start.1 = (s32[16,16]{1,0:T(8,128)S(1)}, s32[16,16]{1,0:T(8,128)}, u32[]{:S(2)}) copy-start(s32[16,16]{1,0:T(8,128)} %param.12) | copy-start | bytes 3076
  27.4 24.0 %collective-permute-start.5 = (bf16[8,640,128]{2,1,0:T(8,128)(2,1)}, bf16[8,640,128]{2,1,0:T(8,128)(2,1)}, u32[]{:S(2)}, u32[]{:S(2)}) collective-permute-start(bf16[8,640,128]{2,1,0:T(8,128)(2,1)} %stack.3.kv), channel_id=1, source_target_pairs={{0,32},{1,9},{2,34},{3,11},{4,36},{5,13},{6,38},{7,15},{8,40},{9,1... | collective-permute-start | bytes 3932168 | tf_op jit(solution)/shard_map/ppermute | solution.py:37
  28.9 33.3 %collective-permute-start.3 = (bf16[8,640,128]{2,1,0:T(8,128)(2,1)}, bf16[8,640,128]{2,1,0:T(8,128)(2,1)}, u32[]{:S(2)}, u32[]{:S(2)}) collective-permute-start(bf16[8,640,128]{2,1,0:T(8,128)(2,1)} %stack.3.kv), channel_id=1, source_target_pairs={{0,64},{1,17},{2,66},{3,19},{4,68},{5,21},{6,70},{7,23},{8,72},{9,... | collective-permute-start | bytes 3932168 | tf_op jit(solution)/shard_map/ppermute | solution.py:37
  31.7 30.6 %collective-permute-start.4 = (bf16[8,640,128]{2,1,0:T(8,128)(2,1)}, bf16[8,640,128]{2,1,0:T(8,128)(2,1)}, u32[]{:S(2)}, u32[]{:S(2)}) collective-permute-start(bf16[8,640,128]{2,1,0:T(8,128)(2,1)} %stack.3.kv), channel_id=1, source_target_pairs={{0,96},{1,25},{2,98},{3,27},{4,100},{5,29},{6,102},{7,31},{8,104},... | collective-permute-start | bytes 3932168 | tf_op jit(solution)/shard_map/ppermute | solution.py:37
  33.4 1.4 %copy-start = (s32[16]{0:T(128)S(1)}, s32[16]{0:T(128)}, u32[]{:S(2)}) copy-start(s32[16]{0:T(128)} %bw.9) | copy-start | bytes 196
  49.9 26.5 %collective-permute-start.10 = (bf16[4,2,256,128]{3,2,1,0:T(8,128)(2,1)}, bf16[4,2,256,128]{3,2,1,0:T(8,128)(2,1)S(1)}, u32[]{:S(2)}, u32[]{:S(2)}) collective-permute-start(bf16[4,2,256,128]{3,2,1,0:T(8,128)(2,1)} %get-tuple-element.39), channel_id=1, source_target_pairs={{0,32},{1,9},{2,34},{3,11},{4,36},{5,13},{6,38},{7,15},{8,40},{9,1... | collective-permute-start | bytes 1572872 | tf_op jit(solution)/shard_map/ppermute | solution.py:37
  50.4 27.7 %collective-permute-start.11 = (bf16[4,2,256,128]{3,2,1,0:T(8,128)(2,1)}, bf16[4,2,256,128]{3,2,1,0:T(8,128)(2,1)S(1)}, u32[]{:S(2)}, u32[]{:S(2)}) collective-permute-start(bf16[4,2,256,128]{3,2,1,0:T(8,128)(2,1)} %get-tuple-element.40), channel_id=1, source_target_pairs={{0,64},{1,17},{2,66},{3,19},{4,68},{5,21},{6,70},{7,23},{8,72},{9,... | collective-permute-start | bytes 1572872 | tf_op jit(solution)/shard_map/ppermute | solution.py:37
  51.3 26.8 %collective-permute-start.12 = (bf16[4,2,256,128]{3,2,1,0:T(8,128)(2,1)}, bf16[4,2,256,128]{3,2,1,0:T(8,128)(2,1)S(1)}, u32[]{:S(2)}, u32[]{:S(2)}) collective-permute-start(bf16[4,2,256,128]{3,2,1,0:T(8,128)(2,1)} %get-tuple-element.41), channel_id=1, source_target_pairs={{0,96},{1,25},{2,98},{3,27},{4,100},{5,29},{6,102},{7,31},{8,104},... | collective-permute-start | bytes 1572872 | tf_op jit(solution)/shard_map/ppermute | solution.py:37
  73.8 8.9 %collective-permute-start.7 = (bf16[640,128]{1,0:T(8,128)(2,1)S(1)}, bf16[640,128]{1,0:T(8,128)(2,1)S(1)}, u32[]{:S(2)}, u32[]{:S(2)}) collective-permute-start(bf16[640,128]{1,0:T(8,128)(2,1)S(1)} %get-tuple-element.55), channel_id=1, source_target_pairs={{0,24},{1,97},{2,26},{3,99},{4,28},{5,101},{6,30},{7,103},{8,0},{9... | collective-permute-start | bytes 491528 | tf_op jit(solution)/shard_map/ppermute | solution.py:33
  74.4 8.3 %collective-permute-start.8 = (bf16[640,128]{1,0:T(8,128)(2,1)S(1)}, bf16[640,128]{1,0:T(8,128)(2,1)S(1)}, u32[]{:S(2)}, u32[]{:S(2)}) collective-permute-start(bf16[640,128]{1,0:T(8,128)(2,1)S(1)} %get-tuple-element.54), channel_id=1, source_target_pairs={{0,16},{1,65},{2,18},{3,67},{4,20},{5,69},{6,22},{7,71},{8,24},{9,... | collective-permute-start | bytes 491528 | tf_op jit(solution)/shard_map/ppermute | solution.py:33
  76.3 6.7 %collective-permute-start.9 = (bf16[640,128]{1,0:T(8,128)(2,1)S(1)}, bf16[640,128]{1,0:T(8,128)(2,1)S(1)}, u32[]{:S(2)}, u32[]{:S(2)}) collective-permute-start(bf16[640,128]{1,0:T(8,128)(2,1)S(1)} %get-tuple-element.53), channel_id=1, source_target_pairs={{0,8},{1,33},{2,10},{3,35},{4,12},{5,37},{6,14},{7,39},{8,16},{9,4... | collective-permute-start | bytes 491528 | tf_op jit(solution)/shard_map/ppermute | solution.py:33
  83.2 6.1 %collective-permute-start.13 = (bf16[640,640]{1,0:T(8,128)(2,1)S(1)}, bf16[640,640]{1,0:T(8,128)(2,1)S(1)}, u32[]{:S(2)}, u32[]{:S(2)}) collective-permute-start(bf16[640,640]{1,0:T(8,128)(2,1)S(1)} %assemble.1.att), channel_id=1, source_target_pairs={{0,1},{1,0},{2,3},{3,2},{4,5},{5,4},{6,7},{7,6},{8,9},{9,8},{10,11... | collective-permute-start | bytes 2457608 | tf_op jit(solution)/shard_map/ppermute | solution.py:45
  90.2 3.4 %copy-start.2 = (s32[2]{0:T(128)S(1)}, s32[2]{0:T(128)}, u32[]{:S(2)}) copy-start(s32[2]{0:T(128)} %constant.177.clone) | copy-start | bytes 28
  90.3 12.8 %collective-permute-start.14 = (bf16[320,640]{1,0:T(8,128)(2,1)S(1)}, bf16[320,640]{1,0:T(8,128)(2,1)S(1)}, u32[]{:S(2)}, u32[]{:S(2)}) collective-permute-start(bf16[320,640]{1,0:T(8,128)(2,1)S(1)} %get-tuple-element.52), channel_id=1, source_target_pairs={{0,2},{1,3},{2,4},{3,5},{4,6},{5,7},{6,0},{7,1},{8,10},{9,11},{10,... | collective-permute-start | bytes 1228808 | tf_op jit(solution)/shard_map/ppermute | solution.py:41
  92.0 11.1 %collective-permute-start.15 = (bf16[320,640]{1,0:T(8,128)(2,1)S(1)}, bf16[320,640]{1,0:T(8,128)(2,1)S(1)}, u32[]{:S(2)}, u32[]{:S(2)}) collective-permute-start(bf16[320,640]{1,0:T(8,128)(2,1)S(1)} %get-tuple-element.51), channel_id=1, source_target_pairs={{0,6},{1,7},{2,0},{3,1},{4,2},{5,3},{6,4},{7,5},{8,14},{9,15},{10,... | collective-permute-start | bytes 1228808 | tf_op jit(solution)/shard_map/ppermute | solution.py:41
  103.3 20.7 %collective-permute-start.16 = (bf16[640,640]{1,0:T(8,128)(2,1)S(1)}, bf16[640,640]{1,0:T(8,128)(2,1)S(1)}, u32[]{:S(2)}, u32[]{:S(2)}) collective-permute-start(bf16[640,640]{1,0:T(8,128)(2,1)S(1)} %get-tuple-element.47), channel_id=1, source_target_pairs={{0,2},{1,3},{2,4},{3,5},{4,6},{5,7},{6,0},{7,1},{8,10},{9,11},{10,... | collective-permute-start | bytes 2457608 | tf_op jit(solution)/shard_map/ppermute | solution.py:41
  105.0 19.0 %collective-permute-start.17 = (bf16[640,640]{1,0:T(8,128)(2,1)S(1)}, bf16[640,640]{1,0:T(8,128)(2,1)S(1)}, u32[]{:S(2)}, u32[]{:S(2)}) collective-permute-start(bf16[640,640]{1,0:T(8,128)(2,1)S(1)} %get-tuple-element.48), channel_id=1, source_target_pairs={{0,6},{1,7},{2,0},{3,1},{4,2},{5,3},{6,4},{7,5},{8,14},{9,15},{10,... | collective-permute-start | bytes 2457608 | tf_op jit(solution)/shard_map/ppermute | solution.py:41

commit v6 on v5

--- a/solution.py
+++ b/solution.py
@@ -153,7 +153,7 @@
         rows = slice(r * ROWS, (r + 1) * ROWS)
         top = jnp.max(scores, axis=1, keepdims=True) * LOG2_SCALE
         if state:
-            level = jnp.broadcast_to(state[1][0, r : r + 1, :], (ROWS, HD)).T[:, 0:1]
+            level = state[1][0, rows, 0:1]
             top = jnp.maximum(top, level)
         probs = jnp.exp2(scores * LOG2_SCALE - top).astype(jnp.bfloat16)
         mixed = lax.dot_general(probs, vv, NN, preferred_element_type=jnp.float32)
@@ -168,9 +168,9 @@
 
 def put_state(out, levels):
     def emit(r, result, top, totals):
-        out[0, r * ROWS : (r + 1) * ROWS, :] = result
-        level = top + jnp.log2(totals)
-        levels[0, r : r + 1, :] = jnp.broadcast_to(level, (ROWS, HD)).T[0:1, :]
+        rows = slice(r * ROWS, (r + 1) * ROWS)
+        out[0, rows, :] = result
+        levels[0, rows, :] = jnp.broadcast_to(top + jnp.log2(totals), (ROWS, HD))
 
     return emit
 
@@ -213,7 +213,6 @@
 
 
 ITEM = pl.BlockSpec((1, FT, HD), lambda i, *_: (i, 0, 0))
-LEVEL = pl.BlockSpec((1, 8, HD), lambda i, *_: (i, 0, 0))
 
 
 def cost(items, blocks):
@@ -226,7 +225,7 @@
 
 
 def state_shape(items):
-    return [pltpu.HBM((items, FT, HD), jnp.bfloat16), pltpu.HBM((items, 8, HD), jnp.float32)]
+    return [pltpu.HBM((items, FT, HD), jnp.bfloat16), pltpu.HBM((items, FT, HD), jnp.float32)]
 
 
 def attend_line(qid, kid, bs, bw, q, kv, after):
@@ -237,7 +236,7 @@
             num_scalar_prefetch=4,
             grid=(SIDE,),
             in_specs=[ITEM, pl.BlockSpec(kv.shape, lambda i, *_: (0, 0, 0)), ANY],
-            out_specs=[ITEM, LEVEL],
+            out_specs=[ITEM, ITEM],
             scratch_shapes=packed(blocks),
         ),
         out_shape=state_shape(SIDE),
@@ -257,7 +256,7 @@
             num_scalar_prefetch=4,
             grid=(1,),
             in_specs=[pl.BlockSpec((FT, HD), lambda i, *_: (0, SIDE)), whole, whole, ANY],
-            out_specs=[ITEM, LEVEL] + [pl.BlockSpec(sent, lambda i, *_: (0, 0, 0, 0))] * 3,
+            out_specs=[ITEM, ITEM] + [pl.BlockSpec(sent, lambda i, *_: (0, 0, 0, 0))] * 3,
             scratch_shapes=packed(blocks),
         ),
         out_shape=state_shape(1) + [pltpu.HBM(sent, jnp.bfloat16)] * 3,
@@ -292,13 +291,13 @@
         out_specs = [ITEM, pl.BlockSpec((8, HD), lambda i, *_: (0, 0))]
         out_shape = [jax.ShapeDtypeStruct((SIDE, FT, HD), jnp.bfloat16), pltpu.HBM((8, HD), jnp.float32)]
     else:
-        out_specs, out_shape = [ITEM, LEVEL], state_shape(SIDE)
+        out_specs, out_shape = [ITEM, ITEM], state_shape(SIDE)
     return pl.pallas_call(
         functools.partial(groups_kernel, len(groups), finished),
         grid_spec=pltpu.PrefetchScalarGridSpec(
             num_scalar_prefetch=4,
             grid=(SIDE,),
-            in_specs=[ITEM] + [pl.BlockSpec(g.shape, lambda i, *_: (0, 0, 0)) for g in groups] + [ITEM, LEVEL],
+            in_specs=[ITEM] + [pl.BlockSpec(g.shape, lambda i, *_: (0, 0, 0)) for g in groups] + [ITEM, ITEM],
             out_specs=out_specs,
             scratch_shapes=packed(blocks),
         ),
@@ -329,7 +328,7 @@
             grid=(1,),
             in_specs=[pl.BlockSpec((FT, HD), lambda i, *_: (0, SIDE))]
             + [pl.BlockSpec(g.shape, lambda i, *_: (0, 0, 0, 0)) for g in groups]
-            + [ITEM, LEVEL, ANY],
+            + [ITEM, ITEM, ANY],
             out_specs=ITEM,
             scratch_shapes=packed(blocks),
         ),
@@ -436,10 +435,8 @@
 def onward_kernel(near, from_down, from_up, send_up, send_down):
     half = FT // 2
     wide = lambda v: v.astype(jnp.float32)
-    send_up[0:half, :] = (wide(near[0, 0:half, :]) + wide(from_down[...])).astype(jnp.bfloat16)
-    send_up[half:, :] = near[0, half:, :]
-    send_down[0:half, :] = near[1, 0:half, :]
-    send_down[half:, :] = (wide(near[1, half:, :]) + wide(from_up[...])).astype(jnp.bfloat16)
+    send_up[...] = (wide(near[0, 0:half, :]) + wide(from_down[...])).astype(jnp.bfloat16)
+    send_down[...] = (wide(near[1, half:, :]) + wide(from_up[...])).astype(jnp.bfloat16)
 
 
 def onward(near, from_down, from_up):
@@ -447,10 +444,28 @@
         onward_kernel,
         in_specs=[VMEM] * 3,
         out_specs=[VMEM] * 2,
-        out_shape=[jax.ShapeDtypeStruct(near.shape[1:], jnp.bfloat16)] * 2,
+        out_shape=[jax.ShapeDtypeStruct(from_up.shape, jnp.bfloat16)] * 2,
         compiler_params=pltpu.CompilerParams(vmem_limit_bytes=LIMIT),
         name="onward",
     )(near, from_down, from_up)
+
+
+def finish_kernel(own, more_up, plain_up, more_down, plain_down, out):
+    half = FT // 2
+    wide = lambda v: v.astype(jnp.float32)
+    out[0:half, :] = (wide(own[0:half, :]) + wide(more_up[...]) + wide(plain_down[...])).astype(jnp.bfloat16)
+    out[half:, :] = (wide(own[half:, :]) + wide(more_down[...]) + wide(plain_up[...])).astype(jnp.bfloat16)
+
+
+def finish(*args):
+    return pl.pallas_call(
+        finish_kernel,
+        in_specs=[VMEM] * 5,
+        out_specs=pl.BlockSpec(args[0].shape, lambda: (0, 0)),
+        out_shape=jax.ShapeDtypeStruct(args[0].shape, jnp.bfloat16),
+        compiler_params=pltpu.CompilerParams(vmem_limit_bytes=LIMIT),
+        name="finish",
+    )(*args)
 
 
 def shards(queries, key_rows, value_rows, out_weight, band_start, band_width):
@@ -504,9 +519,10 @@
     two = second_share(att_other, *first_share(far, att, out_weight, other_weight))
     from_down, from_up = y_shift(two[:half], 1), y_shift(two[half:], 3)
     near = share([1, 3], two)
+    plain_up, plain_down = y_shift(near[0, half:], 1), y_shift(near[1, :half], 3)
     send_up, send_down = onward(near, from_down, from_up)
     own = share([0], near)
-    return add(own[0], y_shift(send_up, 1), y_shift(send_down, 3))
+    return finish(own[0], y_shift(send_up, 1), plain_up, y_shift(send_down, 3), plain_down)
 
 
 def solution(mesh):

time: 126 us -> 122 us (0.968)
  waiting for transfers between devices: 37.5 us -> 30.6 us
  starting transfers between devices: 29.2 us -> 32.7 us
    ppermute x4 -> x6, waiting for transfers between devices: 18.6 us -> 11.9 us  [y_shift(): return lax.ppermute(v, BOTH, pairs(lambda x, z, y, c: (x, z, y + s, c)))]
    ppermute x4 -> x6, starting transfers between devices: 6.61 us -> 9.92 us  [y_shift(): return lax.ppermute(v, BOTH, pairs(lambda x, z, y, c: (x, z, y + s, c)))]
  transfers between devices with their start and end apart: 18 -> 20, of which waited for: 5 -> 8; matrix products, arithmetic and copies ran while one was open for 0% -> 0% of each run, Pallas kernels for 44% -> 46%
where the time goes in v6:
time: 122 us
  Pallas kernels  57.6 us (47%)
  starting transfers between devices  32.7 us (27%)
  waiting for transfers between devices  30.6 us (25%)
    pallas_call x2, Pallas kernels, attend_groups(): pl.pallas_call(functools.partial(groups_kernel, len(groups), finished), g...  20.3 us
    ppermute x6, waiting for transfers between devices, line_shift(): lax.ppermute(v, BOTH, pairs(lambda x, z, y, c: (x, z + s, y, c) if c == 0...  18.7 us
    ppermute x6, waiting for transfers between devices, y_shift(): return lax.ppermute(v, BOTH, pairs(lambda x, z, y, c: (x, z, y + s, c)))  11.9 us
    pallas_call x1, Pallas kernels, attend_line(): pl.pallas_call(line_kernel, grid_spec=pltpu.PrefetchScalarGridSpec(num_sc...  10 us
    ppermute x6, starting transfers between devices, y_shift(): return lax.ppermute(v, BOTH, pairs(lambda x, z, y, c: (x, z, y + s, c)))  9.92 us
    ppermute x6, starting transfers between devices, line_shift(): lax.ppermute(v, BOTH, pairs(lambda x, z, y, c: (x, z + s, y, c) if c == 0...  9.89 us
    ppermute x6, starting transfers between devices, cross_shift(): lax.ppermute(v, BOTH, pairs(lambda x, z, y, c: (x + s, z, y, c) if c == 0...  8.98 us
    pallas_call x2, Pallas kernels, project(): pl.pallas_call(project_kernel, grid_spec=pltpu.PrefetchScalarGridSpec(num...  8.25 us
  transfers between devices with their start and end apart: 20, of which 8 were waited for; matrix products, arithmetic and copies ran while one was open for 0% of the time, Pallas kernels for 46%

profile of v6, /device:TPU:32, one launch (start us, length us, event | category | flops | bytes accessed | tf_op | source)
XLA Modules:
  0.0 121.5 jit_solution(7726585526147743822)
XLA Ops:
  0.0 2.0 %pick.1 = (bf16[5,640,128]{2,1,0:T(8,128)(2,1)S(1)}, bf16[5,640,128]{2,1,0:T(8,128)(2,1)S(1)}, bf16[5,640,128]{2,1,0:T(8,128)(2,1)S(1)}, bf16[5,640,128]{2,1,0:T(8,128)(2,1)S(1)}) custom-call(s32[1]{0:T(128)} %bitcast.2.pos, bf16[640,640]{1,0:T(8,128)(2,1)} %q.3, bf16[640,640]{1,0:T(8,128)(2,1)} %k_any.1, bf16[640,640]{1,0:T(8,128)(2,1)} %v_any.1), custom_call_target="tpu_custom_call" | custom-call | tf_op jit(solution)/shard_map/pick/pallas_call | solution.py:82
  2.0 2.0 %collective-permute-start = (bf16[5,640,128]{2,1,0:T(8,128)(2,1)S(1)}, bf16[5,640,128]{2,1,0:T(8,128)(2,1)S(1)}, u32[]{:S(2)}, u32[]{:S(2)}) collective-permute-start(bf16[5,640,128]{2,1,0:T(8,128)(2,1)S(1)} %get-tuple-element.28), channel_id=1, source_target_pairs={{0,8},{1,33},{2,10},{3,35},{4,12},{5,37},{6,14},{7,39},{8,16},{9,4... | collective-permute-start | bytes 2457608 | tf_op jit(solution)/shard_map/ppermute | solution.py:33
  5.1 2.5 %collective-permute-start.2 = (bf16[5,640,128]{2,1,0:T(8,128)(2,1)S(1)}, bf16[5,640,128]{2,1,0:T(8,128)(2,1)S(1)}, u32[]{:S(2)}, u32[]{:S(2)}) collective-permute-start(bf16[5,640,128]{2,1,0:T(8,128)(2,1)S(1)} %get-tuple-element.30), channel_id=1, source_target_pairs={{0,24},{1,97},{2,26},{3,99},{4,28},{5,101},{6,30},{7,103},{8,0},{9... | collective-permute-start | bytes 2457608 | tf_op jit(solution)/shard_map/ppermute | solution.py:33
  7.6 15.0 %collective-permute-done.refs_1_ = bf16[5,640,128]{2,1,0:T(8,128)(2,1)S(1)} collective-permute-done((bf16[5,640,128]{2,1,0:T(8,128)(2,1)S(1)}, bf16[5,640,128]{2,1,0:T(8,128)(2,1)S(1)}, u32[]{:S(2)}, u32[]{:S(2)}) %collective-permute-start) | collective-permute-done | bytes 819232 | tf_op jit(solution)/shard_map/ppermute | solution.py:33
  22.6 3.6 %collective-permute-done.2.refs_3_ = bf16[5,640,128]{2,1,0:T(8,128)(2,1)S(1)} collective-permute-done((bf16[5,640,128]{2,1,0:T(8,128)(2,1)S(1)}, bf16[5,640,128]{2,1,0:T(8,128)(2,1)S(1)}, u32[]{:S(2)}, u32[]{:S(2)}) %collective-permute-start.2) | collective-permute-done | bytes 819232 | tf_op jit(solution)/shard_map/ppermute | solution.py:33
  28.9 2.7 %collective-permute-start.3 = (bf16[8,640,128]{2,1,0:T(8,128)(2,1)}, bf16[8,640,128]{2,1,0:T(8,128)(2,1)}, u32[]{:S(2)}, u32[]{:S(2)}) collective-permute-start(bf16[8,640,128]{2,1,0:T(8,128)(2,1)} %stack.3.kv), channel_id=1, source_target_pairs={{0,64},{1,17},{2,66},{3,19},{4,68},{5,21},{6,70},{7,23},{8,72},{9,... | collective-permute-start | bytes 3932168 | tf_op jit(solution)/shard_map/ppermute | solution.py:37
  34.8 10.0 %attend_line.1 = (bf16[4,640,128]{2,1,0:T(8,128)(2,1)}, f32[4,640,128]{2,1,0:T(8,128)}) custom-call(s32[4]{0:T(128)S(1)} %broadcast_select_fusion.4.qid.kid, s32[4]{0:T(128)S(1)} %broadcast_select_fusion.4.qid.kid, s32[256]{0:T(256)S(1)} %reshape.7.bs, s32[16]{0:T(128)S(1)} %copy-done, bf16[4,640,128]{2,1,0:T(8,128)(2,1)} %get-tuple-element.31.q, ...), custom_call_target="tpu_custom_call" | custom-call | flops 1845493760 | bytes 8388608 | tf_op jit(solution)/shard_map/attend_line/pallas_call | solution.py:233
  44.8 5.0 %attend_last_line.1 = (bf16[1,640,128]{2,1,0:T(8,128)(2,1)}, f32[1,640,128]{2,1,0:T(8,128)}, bf16[4,2,256,128]{3,2,1,0:T(8,128)(2,1)}, bf16[4,2,256,128]{3,2,1,0:T(8,128)(2,1)}, bf16[4,2,256,128]{3,2,1,0:T(8,128)(2,1)}) custom-call(s32[4]{0:T(128)S(1)} %broadcast_select_fusion.qid, s32[4]{0:T(128)S(1)} %broadcast_select_fusion.4.qid.kid, s32[256]{0:T(256)S(1)} %reshape.7.bs, ...), custom_call_target="tpu_custom_call" | custom-call | flops 461373440 | bytes 8388608 | tf_op jit(solution)/shard_map/attend_last_line/pallas_call | solution.py:253
  51.2 1.8 %collective-permute-start.12 = (bf16[4,2,256,128]{3,2,1,0:T(8,128)(2,1)}, bf16[4,2,256,128]{3,2,1,0:T(8,128)(2,1)S(1)}, u32[]{:S(2)}, u32[]{:S(2)}) collective-permute-start(bf16[4,2,256,128]{3,2,1,0:T(8,128)(2,1)} %get-tuple-element.41), channel_id=1, source_target_pairs={{0,96},{1,25},{2,98},{3,27},{4,100},{5,29},{6,102},{7,31},{8,104},... | collective-permute-start | bytes 1572872 | tf_op jit(solution)/shard_map/ppermute | solution.py:37
  53.0 8.7 %attend_groups.2 = (bf16[4,640,128]{2,1,0:T(8,128)(2,1)}, f32[4,640,128]{2,1,0:T(8,128)}) custom-call(s32[4]{0:T(128)S(1)} %broadcast_select_fusion.4.qid.kid, s32[4]{0:T(128)S(1)} %broadcast_select_fusion.1.kid, s32[256]{0:T(256)S(1)} %reshape.7.bs, s32[16]{0:T(128)S(1)} %copy-done, bf16[4,640,128]{2,1,0:T(8,128)(2,1)} %get-tuple-element.31.q, ...), custom_call_target="tpu_custom_call" | custom-call | flops 1342177280 | bytes 8388608 | tf_op jit(solution)/shard_map/attend_groups/pallas_call | solution.py:295
  61.7 11.6 %attend_groups.3 = (bf16[4,640,128]{2,1,0:T(8,128)(2,1)S(1)}, f32[8,128]{1,0:T(8,128)}) custom-call(s32[4]{0:T(128)S(1)} %broadcast_select_fusion.4.qid.kid, s32[8]{0:T(128)S(1)} %pad_add_fusion.kid, s32[256]{0:T(256)S(1)} %reshape.7.bs, s32[16]{0:T(128)S(1)} %copy-done, bf16[4,640,128]{2,1,0:T(8,128)(2,1)} %get-tuple-element.31.q, ...), custom_call_target="tpu_custom_call" | custom-call | flops 2684354560 | bytes 8388608 | tf_op jit(solution)/shard_map/attend_groups/pallas_call | solution.py:295
  74.0 1.9 %collective-permute-start.8 = (bf16[640,128]{1,0:T(8,128)(2,1)S(1)}, bf16[640,128]{1,0:T(8,128)(2,1)S(1)}, u32[]{:S(2)}, u32[]{:S(2)}) collective-permute-start(bf16[640,128]{1,0:T(8,128)(2,1)S(1)} %get-tuple-element.56), channel_id=1, source_target_pairs={{0,16},{1,65},{2,18},{3,67},{4,20},{5,69},{6,22},{7,71},{8,24},{9,... | collective-permute-start | bytes 491528 | tf_op jit(solution)/shard_map/ppermute | solution.py:33
  75.9 1.7 %collective-permute-start.9 = (bf16[640,128]{1,0:T(8,128)(2,1)S(1)}, bf16[640,128]{1,0:T(8,128)(2,1)S(1)}, u32[]{:S(2)}, u32[]{:S(2)}) collective-permute-start(bf16[640,128]{1,0:T(8,128)(2,1)S(1)} %get-tuple-element.55), channel_id=1, source_target_pairs={{0,8},{1,33},{2,10},{3,35},{4,12},{5,37},{6,14},{7,39},{8,16},{9,4... | collective-permute-start | bytes 491528 | tf_op jit(solution)/shard_map/ppermute | solution.py:33
  77.7 4.8 %attend_bands.1 = bf16[1,640,128]{2,1,0:T(8,128)(2,1)S(1)} custom-call(s32[1]{0:T(128)} %bitcast.7.qid, s32[12]{0:T(128)S(1)} %pad_add_fusion.1.kid, s32[256]{0:T(256)S(1)} %reshape.7.bs, s32[16]{0:T(128)S(1)} %copy-done, bf16[640,640]{1,0:T(8,128)(2,1)} %q.3, bf16[4,2,256,128]{3,2,1,0:T(8,128)(2,1)S(1)} %collective-permute-done.10.g1, ...), custom_call_target="tpu_custom_call" | custom-call | flops 1006632960 | bytes 8388608 | tf_op jit(solution)/shard_map/attend_bands/pallas_call | solution.py:324
  82.8 3.9 %collective-permute-start.13 = (bf16[640,640]{1,0:T(8,128)(2,1)S(1)}, bf16[640,640]{1,0:T(8,128)(2,1)S(1)}, u32[]{:S(2)}, u32[]{:S(2)}) collective-permute-start(bf16[640,640]{1,0:T(8,128)(2,1)S(1)} %assemble.1.att), channel_id=1, source_target_pairs={{0,1},{1,0},{2,3},{3,2},{4,5},{5,4},{6,7},{7,6},{8,9},{9,8},{10,11... | collective-permute-start | bytes 2457608 | tf_op jit(solution)/shard_map/ppermute | solution.py:45
  86.7 2.3 %first_share.1 = (f32[640,640]{1,0:T(8,128)S(1)}, bf16[640,640]{1,0:T(8,128)(2,1)S(1)}) custom-call(s32[1]{0:T(128)S(6)} %add.218.blocks, bf16[640,640]{1,0:T(8,128)(2,1)S(1)} %assemble.1.att, bf16[640,5120]{1,0:T(8,128)(2,1)} %w_mine.3, bf16[640,5120]{1,0:T(8,128)(2,1)} %collective-permute-done.6.after.other.w_other), custom_call_target="tpu_custom_call" | custom-call | tf_op jit(solution)/shard_map/first_share/pallas_call | solution.py:401
  90.0 1.6 %collective-permute-start.14 = (bf16[320,640]{1,0:T(8,128)(2,1)S(1)}, bf16[320,640]{1,0:T(8,128)(2,1)S(1)}, u32[]{:S(2)}, u32[]{:S(2)}) collective-permute-start(bf16[320,640]{1,0:T(8,128)(2,1)S(1)} %get-tuple-element.54), channel_id=1, source_target_pairs={{0,2},{1,3},{2,4},{3,5},{4,6},{5,7},{6,0},{7,1},{8,10},{9,11},{10,... | collective-permute-start | bytes 1228808 | tf_op jit(solution)/shard_map/ppermute | solution.py:41
  91.6 1.7 %collective-permute-start.15 = (bf16[320,640]{1,0:T(8,128)(2,1)S(1)}, bf16[320,640]{1,0:T(8,128)(2,1)S(1)}, u32[]{:S(2)}, u32[]{:S(2)}) collective-permute-start(bf16[320,640]{1,0:T(8,128)(2,1)S(1)} %get-tuple-element.53), channel_id=1, source_target_pairs={{0,6},{1,7},{2,0},{3,1},{4,2},{5,3},{6,4},{7,5},{8,14},{9,15},{10,... | collective-permute-start | bytes 1228808 | tf_op jit(solution)/shard_map/ppermute | solution.py:41
  93.3 5.2 %project.2.refs_0_.near = bf16[2,640,640]{2,1,0:T(8,128)(2,1)S(1)} custom-call(s32[2]{0:T(128)S(1)} %get-tuple-element.50.order, s32[2]{0:T(128)S(1)} %get-tuple-element.49.blocks, bf16[640,640]{1,0:T(8,128)(2,1)S(1)} %assemble.1.att, bf16[640,640]{1,0:T(8,128)(2,1)S(1)} %collective-permute-done.13.att_other, bf16[640,5120]{1,0:T(8,128)(2,1)} %w_mine.3, ...), custom_call_target="tpu_custom_call" | custom-call | tf_op jit(solution)/shard_map/project/pallas_call | solution.py:372
  99.1 2.9 %collective-permute-start.19 = (bf16[320,640]{1,0:T(8,128)(2,1)S(1)}, bf16[320,640]{1,0:T(8,128)(2,1)S(1)}, u32[]{:S(2)}, u32[]{:S(2)}) collective-permute-start(bf16[320,640]{1,0:T(8,128)(2,1)S(1)} %get-tuple-element.51), channel_id=1, source_target_pairs={{0,6},{1,7},{2,0},{3,1},{4,2},{5,3},{6,4},{7,5},{8,14},{9,15},{10,... | collective-permute-start | bytes 1228808 | tf_op jit(solution)/shard_map/ppermute | solution.py:41
  105.8 1.7 %collective-permute-start.18 = (bf16[320,640]{1,0:T(8,128)(2,1)S(1)}, bf16[320,640]{1,0:T(8,128)(2,1)S(1)}, u32[]{:S(2)}, u32[]{:S(2)}) collective-permute-start(bf16[320,640]{1,0:T(8,128)(2,1)S(1)} %get-tuple-element.48), channel_id=1, source_target_pairs={{0,6},{1,7},{2,0},{3,1},{4,2},{5,3},{6,4},{7,5},{8,14},{9,15},{10,... | collective-permute-start | bytes 1228808 | tf_op jit(solution)/shard_map/ppermute | solution.py:41
  107.5 3.0 %project.3 = bf16[1,640,640]{2,1,0:T(8,128)(2,1)S(1)} custom-call(s32[1]{0:T(128)S(6)} %select_n.128.order, s32[1]{0:T(128)S(6)} %add.179.blocks, bf16[640,640]{1,0:T(8,128)(2,1)S(1)} %assemble.1.att, bf16[640,640]{1,0:T(8,128)(2,1)S(1)} %collective-permute-done.13.att_other, bf16[640,5120]{1,0:T(8,128)(2,1)} %w_mine.3, ...), custom_call_target="tpu_custom_call" | custom-call | tf_op jit(solution)/shard_map/project/pallas_call | solution.py:372
  110.5 1.8 %collective-permute-done.17.plain_up = bf16[320,640]{1,0:T(8,128)(2,1)S(1)} collective-permute-done((bf16[320,640]{1,0:T(8,128)(2,1)S(1)}, bf16[320,640]{1,0:T(8,128)(2,1)S(1)}, u32[]{:S(2)}, u32[]{:S(2)}) %collective-permute-start.17) | collective-permute-done | bytes 409632 | tf_op jit(solution)/shard_map/ppermute | solution.py:41
  112.8 7.5 %collective-permute-done.16.more_up = bf16[320,640]{1,0:T(8,128)(2,1)S(1)} collective-permute-done((bf16[320,640]{1,0:T(8,128)(2,1)S(1)}, bf16[320,640]{1,0:T(8,128)(2,1)S(1)}, u32[]{:S(2)}, u32[]{:S(2)}) %collective-permute-start.16) | collective-permute-done | bytes 409632 | tf_op jit(solution)/shard_map/ppermute | solution.py:41
  (48 shorter events, 16.5 us)
Async XLA Ops:
  0.0 34.7 %collective-permute-start.6 = (bf16[640,5120]{1,0:T(8,128)(2,1)}, bf16[640,5120]{1,0:T(8,128)(2,1)}, u32[]{:S(2)}, u32[]{:S(2)}) collective-permute-start(bf16[640,5120]{1,0:T(8,128)(2,1)} %w_mine.3), channel_id=1, source_target_pairs={{0,1},{1,0},{2,3},{3,2},{4,5},{5,4},{6,7},{7,6},{8,9},{9,8},{10,11... | collective-permute-start | bytes 19660808 | tf_op jit(solution)/shard_map/ppermute | solution.py:45
  2.0 20.7 %collective-permute-start = (bf16[5,640,128]{2,1,0:T(8,128)(2,1)S(1)}, bf16[5,640,128]{2,1,0:T(8,128)(2,1)S(1)}, u32[]{:S(2)}, u32[]{:S(2)}) collective-permute-start(bf16[5,640,128]{2,1,0:T(8,128)(2,1)S(1)} %get-tuple-element.28), channel_id=1, source_target_pairs={{0,8},{1,33},{2,10},{3,35},{4,12},{5,37},{6,14},{7,39},{8,16},{9,4... | collective-permute-start | bytes 2457608 | tf_op jit(solution)/shard_map/ppermute | solution.py:33
  4.0 18.7 %collective-permute-start.1 = (bf16[5,640,128]{2,1,0:T(8,128)(2,1)S(1)}, bf16[5,640,128]{2,1,0:T(8,128)(2,1)S(1)}, u32[]{:S(2)}, u32[]{:S(2)}) collective-permute-start(bf16[5,640,128]{2,1,0:T(8,128)(2,1)S(1)} %get-tuple-element.29), channel_id=1, source_target_pairs={{0,16},{1,65},{2,18},{3,67},{4,20},{5,69},{6,22},{7,71},{8,24},{9,... | collective-permute-start | bytes 2457608 | tf_op jit(solution)/shard_map/ppermute | solution.py:33
  5.1 21.1 %collective-permute-start.2 = (bf16[5,640,128]{2,1,0:T(8,128)(2,1)S(1)}, bf16[5,640,128]{2,1,0:T(8,128)(2,1)S(1)}, u32[]{:S(2)}, u32[]{:S(2)}) collective-permute-start(bf16[5,640,128]{2,1,0:T(8,128)(2,1)S(1)} %get-tuple-element.30), channel_id=1, source_target_pairs={{0,24},{1,97},{2,26},{3,99},{4,28},{5,101},{6,30},{7,103},{8,0},{9... | collective-permute-start | bytes 2457608 | tf_op jit(solution)/shard_map/ppermute | solution.py:33
  26.2 6.9 %copy-start.1 = (s32[16,16]{1,0:T(8,128)S(1)}, s32[16,16]{1,0:T(8,128)}, u32[]{:S(2)}) copy-start(s32[16,16]{1,0:T(8,128)} %param.12) | copy-start | bytes 3076
  27.4 23.8 %collective-permute-start.5 = (bf16[8,640,128]{2,1,0:T(8,128)(2,1)}, bf16[8,640,128]{2,1,0:T(8,128)(2,1)}, u32[]{:S(2)}, u32[]{:S(2)}) collective-permute-start(bf16[8,640,128]{2,1,0:T(8,128)(2,1)} %stack.3.kv), channel_id=1, source_target_pairs={{0,32},{1,9},{2,34},{3,11},{4,36},{5,13},{6,38},{7,15},{8,40},{9,1... | collective-permute-start | bytes 3932168 | tf_op jit(solution)/shard_map/ppermute | solution.py:37
  28.9 32.8 %collective-permute-start.3 = (bf16[8,640,128]{2,1,0:T(8,128)(2,1)}, bf16[8,640,128]{2,1,0:T(8,128)(2,1)}, u32[]{:S(2)}, u32[]{:S(2)}) collective-permute-start(bf16[8,640,128]{2,1,0:T(8,128)(2,1)} %stack.3.kv), channel_id=1, source_target_pairs={{0,64},{1,17},{2,66},{3,19},{4,68},{5,21},{6,70},{7,23},{8,72},{9,... | collective-permute-start | bytes 3932168 | tf_op jit(solution)/shard_map/ppermute | solution.py:37
  31.7 30.1 %collective-permute-start.4 = (bf16[8,640,128]{2,1,0:T(8,128)(2,1)}, bf16[8,640,128]{2,1,0:T(8,128)(2,1)}, u32[]{:S(2)}, u32[]{:S(2)}) collective-permute-start(bf16[8,640,128]{2,1,0:T(8,128)(2,1)} %stack.3.kv), channel_id=1, source_target_pairs={{0,96},{1,25},{2,98},{3,27},{4,100},{5,29},{6,102},{7,31},{8,104},... | collective-permute-start | bytes 3932168 | tf_op jit(solution)/shard_map/ppermute | solution.py:37
  33.4 1.4 %copy-start = (s32[16]{0:T(128)S(1)}, s32[16]{0:T(128)}, u32[]{:S(2)}) copy-start(s32[16]{0:T(128)} %bw.9) | copy-start | bytes 196
  49.7 26.1 %collective-permute-start.10 = (bf16[4,2,256,128]{3,2,1,0:T(8,128)(2,1)}, bf16[4,2,256,128]{3,2,1,0:T(8,128)(2,1)S(1)}, u32[]{:S(2)}, u32[]{:S(2)}) collective-permute-start(bf16[4,2,256,128]{3,2,1,0:T(8,128)(2,1)} %get-tuple-element.39), channel_id=1, source_target_pairs={{0,32},{1,9},{2,34},{3,11},{4,36},{5,13},{6,38},{7,15},{8,40},{9,1... | collective-permute-start | bytes 1572872 | tf_op jit(solution)/shard_map/ppermute | solution.py:37
  50.3 27.3 %collective-permute-start.11 = (bf16[4,2,256,128]{3,2,1,0:T(8,128)(2,1)}, bf16[4,2,256,128]{3,2,1,0:T(8,128)(2,1)S(1)}, u32[]{:S(2)}, u32[]{:S(2)}) collective-permute-start(bf16[4,2,256,128]{3,2,1,0:T(8,128)(2,1)} %get-tuple-element.40), channel_id=1, source_target_pairs={{0,64},{1,17},{2,66},{3,19},{4,68},{5,21},{6,70},{7,23},{8,72},{9,... | collective-permute-start | bytes 1572872 | tf_op jit(solution)/shard_map/ppermute | solution.py:37
  51.2 26.5 %collective-permute-start.12 = (bf16[4,2,256,128]{3,2,1,0:T(8,128)(2,1)}, bf16[4,2,256,128]{3,2,1,0:T(8,128)(2,1)S(1)}, u32[]{:S(2)}, u32[]{:S(2)}) collective-permute-start(bf16[4,2,256,128]{3,2,1,0:T(8,128)(2,1)} %get-tuple-element.41), channel_id=1, source_target_pairs={{0,96},{1,25},{2,98},{3,27},{4,100},{5,29},{6,102},{7,31},{8,104},... | collective-permute-start | bytes 1572872 | tf_op jit(solution)/shard_map/ppermute | solution.py:37
  73.4 9.1 %collective-permute-start.7 = (bf16[640,128]{1,0:T(8,128)(2,1)S(1)}, bf16[640,128]{1,0:T(8,128)(2,1)S(1)}, u32[]{:S(2)}, u32[]{:S(2)}) collective-permute-start(bf16[640,128]{1,0:T(8,128)(2,1)S(1)} %get-tuple-element.57), channel_id=1, source_target_pairs={{0,24},{1,97},{2,26},{3,99},{4,28},{5,101},{6,30},{7,103},{8,0},{9... | collective-permute-start | bytes 491528 | tf_op jit(solution)/shard_map/ppermute | solution.py:33
  74.0 8.5 %collective-permute-start.8 = (bf16[640,128]{1,0:T(8,128)(2,1)S(1)}, bf16[640,128]{1,0:T(8,128)(2,1)S(1)}, u32[]{:S(2)}, u32[]{:S(2)}) collective-permute-start(bf16[640,128]{1,0:T(8,128)(2,1)S(1)} %get-tuple-element.56), channel_id=1, source_target_pairs={{0,16},{1,65},{2,18},{3,67},{4,20},{5,69},{6,22},{7,71},{8,24},{9,... | collective-permute-start | bytes 491528 | tf_op jit(solution)/shard_map/ppermute | solution.py:33
  75.9 6.7 %collective-permute-start.9 = (bf16[640,128]{1,0:T(8,128)(2,1)S(1)}, bf16[640,128]{1,0:T(8,128)(2,1)S(1)}, u32[]{:S(2)}, u32[]{:S(2)}) collective-permute-start(bf16[640,128]{1,0:T(8,128)(2,1)S(1)} %get-tuple-element.55), channel_id=1, source_target_pairs={{0,8},{1,33},{2,10},{3,35},{4,12},{5,37},{6,14},{7,39},{8,16},{9,4... | collective-permute-start | bytes 491528 | tf_op jit(solution)/shard_map/ppermute | solution.py:33
  82.8 6.2 %collective-permute-start.13 = (bf16[640,640]{1,0:T(8,128)(2,1)S(1)}, bf16[640,640]{1,0:T(8,128)(2,1)S(1)}, u32[]{:S(2)}, u32[]{:S(2)}) collective-permute-start(bf16[640,640]{1,0:T(8,128)(2,1)S(1)} %assemble.1.att), channel_id=1, source_target_pairs={{0,1},{1,0},{2,3},{3,2},{4,5},{5,4},{6,7},{7,6},{8,9},{9,8},{10,11... | collective-permute-start | bytes 2457608 | tf_op jit(solution)/shard_map/ppermute | solution.py:45
  89.9 3.4 %copy-start.2 = (s32[2]{0:T(128)S(1)}, s32[2]{0:T(128)}, u32[]{:S(2)}) copy-start(s32[2]{0:T(128)} %constant.177.clone) | copy-start | bytes 28
  90.0 13.3 %collective-permute-start.14 = (bf16[320,640]{1,0:T(8,128)(2,1)S(1)}, bf16[320,640]{1,0:T(8,128)(2,1)S(1)}, u32[]{:S(2)}, u32[]{:S(2)}) collective-permute-start(bf16[320,640]{1,0:T(8,128)(2,1)S(1)} %get-tuple-element.54), channel_id=1, source_target_pairs={{0,2},{1,3},{2,4},{3,5},{4,6},{5,7},{6,0},{7,1},{8,10},{9,11},{10,... | collective-permute-start | bytes 1228808 | tf_op jit(solution)/shard_map/ppermute | solution.py:41
  91.6 12.4 %collective-permute-start.15 = (bf16[320,640]{1,0:T(8,128)(2,1)S(1)}, bf16[320,640]{1,0:T(8,128)(2,1)S(1)}, u32[]{:S(2)}, u32[]{:S(2)}) collective-permute-start(bf16[320,640]{1,0:T(8,128)(2,1)S(1)} %get-tuple-element.53), channel_id=1, source_target_pairs={{0,6},{1,7},{2,0},{3,1},{4,2},{5,3},{6,4},{7,5},{8,14},{9,15},{10,... | collective-permute-start | bytes 1228808 | tf_op jit(solution)/shard_map/ppermute | solution.py:41
  98.6 13.7 %collective-permute-start.17 = (bf16[320,640]{1,0:T(8,128)(2,1)S(1)}, bf16[320,640]{1,0:T(8,128)(2,1)S(1)}, u32[]{:S(2)}, u32[]{:S(2)}) collective-permute-start(bf16[320,640]{1,0:T(8,128)(2,1)S(1)} %get-tuple-element.52), channel_id=1, source_target_pairs={{0,2},{1,3},{2,4},{3,5},{4,6},{5,7},{6,0},{7,1},{8,10},{9,11},{10,... | collective-permute-start | bytes 1228808 | tf_op jit(solution)/shard_map/ppermute | solution.py:41
  99.1 13.7 %collective-permute-start.19 = (bf16[320,640]{1,0:T(8,128)(2,1)S(1)}, bf16[320,640]{1,0:T(8,128)(2,1)S(1)}, u32[]{:S(2)}, u32[]{:S(2)}) collective-permute-start(bf16[320,640]{1,0:T(8,128)(2,1)S(1)} %get-tuple-element.51), channel_id=1, source_target_pairs={{0,6},{1,7},{2,0},{3,1},{4,2},{5,3},{6,4},{7,5},{8,14},{9,15},{10,... | collective-permute-start | bytes 1228808 | tf_op jit(solution)/shard_map/ppermute | solution.py:41
  104.2 16.1 %collective-permute-start.16 = (bf16[320,640]{1,0:T(8,128)(2,1)S(1)}, bf16[320,640]{1,0:T(8,128)(2,1)S(1)}, u32[]{:S(2)}, u32[]{:S(2)}) collective-permute-start(bf16[320,640]{1,0:T(8,128)(2,1)S(1)} %get-tuple-element.47), channel_id=1, source_target_pairs={{0,2},{1,3},{2,4},{3,5},{4,6},{5,7},{6,0},{7,1},{8,10},{9,11},{10,... | collective-permute-start | bytes 1228808 | tf_op jit(solution)/shard_map/ppermute | solution.py:41
  105.8 14.5 %collective-permute-start.18 = (bf16[320,640]{1,0:T(8,128)(2,1)S(1)}, bf16[320,640]{1,0:T(8,128)(2,1)S(1)}, u32[]{:S(2)}, u32[]{:S(2)}) collective-permute-start(bf16[320,640]{1,0:T(8,128)(2,1)S(1)} %get-tuple-element.48), channel_id=1, source_target_pairs={{0,6},{1,7},{2,0},{3,1},{4,2},{5,3},{6,4},{7,5},{8,14},{9,15},{10,... | collective-permute-start | bytes 1228808 | tf_op jit(solution)/shard_map/ppermute | solution.py:41

commit v7 on v6

--- a/solution.py
+++ b/solution.py
@@ -13,7 +13,7 @@
 FT = 640
 FRAMES = 16
 SIDE = 4
-ROWS = 128
+ROWS = 320
 LOG2_SCALE = 1.4426950408889634 / HD**0.5
 NT = (((1,), (1,)), ((), ()))
 NN = (((1,), (0,)), ((), ()))

time: 122 us -> 122 us (level)
  Pallas kernels: 57.6 us -> 56.1 us
  transfers between devices with their start and end apart: 20 -> 20, of which waited for: 8 -> 9; matrix products, arithmetic and copies ran while one was open for 0% -> 0% of each run, Pallas kernels for 46% -> 45%
where the time goes in v7:
time: 122 us; the launch traced here: 121 us
  Pallas kernels  56.1 us (46%)
  starting transfers between devices  32.6 us (27%)
  waiting for transfers between devices  31.3 us (26%)
    pallas_call x2, Pallas kernels, attend_groups(): pl.pallas_call(functools.partial(groups_kernel, len(groups), finished), g...  19.5 us
    ppermute x6, waiting for transfers between devices, line_shift(): lax.ppermute(v, BOTH, pairs(lambda x, z, y, c: (x, z + s, y, c) if c == 0...  19 us
    ppermute x6, waiting for transfers between devices, y_shift(): return lax.ppermute(v, BOTH, pairs(lambda x, z, y, c: (x, z, y + s, c)))  11.9 us
    ppermute x6, starting transfers between devices, y_shift(): return lax.ppermute(v, BOTH, pairs(lambda x, z, y, c: (x, z, y + s, c)))  9.92 us
    ppermute x6, starting transfers between devices, line_shift(): lax.ppermute(v, BOTH, pairs(lambda x, z, y, c: (x, z + s, y, c) if c == 0...  9.89 us
    pallas_call x1, Pallas kernels, attend_line(): pl.pallas_call(line_kernel, grid_spec=pltpu.PrefetchScalarGridSpec(num_sc...  9.71 us
    ppermute x6, starting transfers between devices, cross_shift(): lax.ppermute(v, BOTH, pairs(lambda x, z, y, c: (x + s, z, y, c) if c == 0...  9 us
    pallas_call x2, Pallas kernels, project(): pl.pallas_call(project_kernel, grid_spec=pltpu.PrefetchScalarGridSpec(num...  8.25 us
  transfers between devices with their start and end apart: 20, of which 9 were waited for; matrix products, arithmetic and copies ran while one was open for 0% of the time, Pallas kernels for 45%

profile of v7, /device:TPU:32, one launch (start us, length us, event | category | flops | bytes accessed | tf_op | source)
XLA Modules:
  0.0 120.7 jit_solution(4158446017032900419)
XLA Ops:
  0.0 2.0 %pick.1 = (bf16[5,640,128]{2,1,0:T(8,128)(2,1)S(1)}, bf16[5,640,128]{2,1,0:T(8,128)(2,1)S(1)}, bf16[5,640,128]{2,1,0:T(8,128)(2,1)S(1)}, bf16[5,640,128]{2,1,0:T(8,128)(2,1)S(1)}) custom-call(s32[1]{0:T(128)} %bitcast.2.pos, bf16[640,640]{1,0:T(8,128)(2,1)} %q.3, bf16[640,640]{1,0:T(8,128)(2,1)} %k_any.1, bf16[640,640]{1,0:T(8,128)(2,1)} %v_any.1), custom_call_target="tpu_custom_call" | custom-call | tf_op jit(solution)/shard_map/pick/pallas_call | solution.py:82
  2.0 2.0 %collective-permute-start = (bf16[5,640,128]{2,1,0:T(8,128)(2,1)S(1)}, bf16[5,640,128]{2,1,0:T(8,128)(2,1)S(1)}, u32[]{:S(2)}, u32[]{:S(2)}) collective-permute-start(bf16[5,640,128]{2,1,0:T(8,128)(2,1)S(1)} %get-tuple-element.28), channel_id=1, source_target_pairs={{0,8},{1,33},{2,10},{3,35},{4,12},{5,37},{6,14},{7,39},{8,16},{9,4... | collective-permute-start | bytes 2457608 | tf_op jit(solution)/shard_map/ppermute | solution.py:33
  5.1 2.5 %collective-permute-start.2 = (bf16[5,640,128]{2,1,0:T(8,128)(2,1)S(1)}, bf16[5,640,128]{2,1,0:T(8,128)(2,1)S(1)}, u32[]{:S(2)}, u32[]{:S(2)}) collective-permute-start(bf16[5,640,128]{2,1,0:T(8,128)(2,1)S(1)} %get-tuple-element.30), channel_id=1, source_target_pairs={{0,24},{1,97},{2,26},{3,99},{4,28},{5,101},{6,30},{7,103},{8,0},{9... | collective-permute-start | bytes 2457608 | tf_op jit(solution)/shard_map/ppermute | solution.py:33
  7.6 15.0 %collective-permute-done.refs_1_ = bf16[5,640,128]{2,1,0:T(8,128)(2,1)S(1)} collective-permute-done((bf16[5,640,128]{2,1,0:T(8,128)(2,1)S(1)}, bf16[5,640,128]{2,1,0:T(8,128)(2,1)S(1)}, u32[]{:S(2)}, u32[]{:S(2)}) %collective-permute-start) | collective-permute-done | bytes 819232 | tf_op jit(solution)/shard_map/ppermute | solution.py:33
  22.6 3.6 %collective-permute-done.2.refs_3_ = bf16[5,640,128]{2,1,0:T(8,128)(2,1)S(1)} collective-permute-done((bf16[5,640,128]{2,1,0:T(8,128)(2,1)S(1)}, bf16[5,640,128]{2,1,0:T(8,128)(2,1)S(1)}, u32[]{:S(2)}, u32[]{:S(2)}) %collective-permute-start.2) | collective-permute-done | bytes 819232 | tf_op jit(solution)/shard_map/ppermute | solution.py:33
  28.9 2.7 %collective-permute-start.3 = (bf16[8,640,128]{2,1,0:T(8,128)(2,1)}, bf16[8,640,128]{2,1,0:T(8,128)(2,1)}, u32[]{:S(2)}, u32[]{:S(2)}) collective-permute-start(bf16[8,640,128]{2,1,0:T(8,128)(2,1)} %stack.3.kv), channel_id=1, source_target_pairs={{0,64},{1,17},{2,66},{3,19},{4,68},{5,21},{6,70},{7,23},{8,72},{9,... | collective-permute-start | bytes 3932168 | tf_op jit(solution)/shard_map/ppermute | solution.py:37
  34.8 9.7 %attend_line.1 = (bf16[4,640,128]{2,1,0:T(8,128)(2,1)}, f32[4,640,128]{2,1,0:T(8,128)}) custom-call(s32[4]{0:T(128)S(1)} %broadcast_select_fusion.4.qid.kid, s32[4]{0:T(128)S(1)} %broadcast_select_fusion.4.qid.kid, s32[256]{0:T(256)S(1)} %reshape.7.bs, s32[16]{0:T(128)S(1)} %copy-done, bf16[4,640,128]{2,1,0:T(8,128)(2,1)} %get-tuple-element.31.q, ...), custom_call_target="tpu_custom_call" | custom-call | flops 1845493760 | bytes 8388608 | tf_op jit(solution)/shard_map/attend_line/pallas_call | solution.py:233
  44.5 4.9 %attend_last_line.1 = (bf16[1,640,128]{2,1,0:T(8,128)(2,1)}, f32[1,640,128]{2,1,0:T(8,128)}, bf16[4,2,256,128]{3,2,1,0:T(8,128)(2,1)}, bf16[4,2,256,128]{3,2,1,0:T(8,128)(2,1)}, bf16[4,2,256,128]{3,2,1,0:T(8,128)(2,1)}) custom-call(s32[4]{0:T(128)S(1)} %broadcast_select_fusion.qid, s32[4]{0:T(128)S(1)} %broadcast_select_fusion.4.qid.kid, s32[256]{0:T(256)S(1)} %reshape.7.bs, ...), custom_call_target="tpu_custom_call" | custom-call | flops 461373440 | bytes 8388608 | tf_op jit(solution)/shard_map/attend_last_line/pallas_call | solution.py:253
  50.8 1.8 %collective-permute-start.12 = (bf16[4,2,256,128]{3,2,1,0:T(8,128)(2,1)}, bf16[4,2,256,128]{3,2,1,0:T(8,128)(2,1)S(1)}, u32[]{:S(2)}, u32[]{:S(2)}) collective-permute-start(bf16[4,2,256,128]{3,2,1,0:T(8,128)(2,1)} %get-tuple-element.41), channel_id=1, source_target_pairs={{0,96},{1,25},{2,98},{3,27},{4,100},{5,29},{6,102},{7,31},{8,104},... | collective-permute-start | bytes 1572872 | tf_op jit(solution)/shard_map/ppermute | solution.py:37
  52.6 8.7 %attend_groups.2 = (bf16[4,640,128]{2,1,0:T(8,128)(2,1)}, f32[4,640,128]{2,1,0:T(8,128)}) custom-call(s32[4]{0:T(128)S(1)} %broadcast_select_fusion.4.qid.kid, s32[4]{0:T(128)S(1)} %broadcast_select_fusion.1.kid, s32[256]{0:T(256)S(1)} %reshape.7.bs, s32[16]{0:T(128)S(1)} %copy-done, bf16[4,640,128]{2,1,0:T(8,128)(2,1)} %get-tuple-element.31.q, ...), custom_call_target="tpu_custom_call" | custom-call | flops 1342177280 | bytes 8388608 | tf_op jit(solution)/shard_map/attend_groups/pallas_call | solution.py:295
  61.7 10.8 %attend_groups.3 = (bf16[4,640,128]{2,1,0:T(8,128)(2,1)S(1)}, f32[8,128]{1,0:T(8,128)}) custom-call(s32[4]{0:T(128)S(1)} %broadcast_select_fusion.4.qid.kid, s32[8]{0:T(128)S(1)} %pad_add_fusion.kid, s32[256]{0:T(256)S(1)} %reshape.7.bs, s32[16]{0:T(128)S(1)} %copy-done, bf16[4,640,128]{2,1,0:T(8,128)(2,1)} %get-tuple-element.31.q, ...), custom_call_target="tpu_custom_call" | custom-call | flops 2684354560 | bytes 8388608 | tf_op jit(solution)/shard_map/attend_groups/pallas_call | solution.py:295
  73.2 1.9 %collective-permute-start.8 = (bf16[640,128]{1,0:T(8,128)(2,1)S(1)}, bf16[640,128]{1,0:T(8,128)(2,1)S(1)}, u32[]{:S(2)}, u32[]{:S(2)}) collective-permute-start(bf16[640,128]{1,0:T(8,128)(2,1)S(1)} %get-tuple-element.56), channel_id=1, source_target_pairs={{0,16},{1,65},{2,18},{3,67},{4,20},{5,69},{6,22},{7,71},{8,24},{9,... | collective-permute-start | bytes 491528 | tf_op jit(solution)/shard_map/ppermute | solution.py:33
  75.1 1.7 %collective-permute-start.9 = (bf16[640,128]{1,0:T(8,128)(2,1)S(1)}, bf16[640,128]{1,0:T(8,128)(2,1)S(1)}, u32[]{:S(2)}, u32[]{:S(2)}) collective-permute-start(bf16[640,128]{1,0:T(8,128)(2,1)S(1)} %get-tuple-element.55), channel_id=1, source_target_pairs={{0,8},{1,33},{2,10},{3,35},{4,12},{5,37},{6,14},{7,39},{8,16},{9,4... | collective-permute-start | bytes 491528 | tf_op jit(solution)/shard_map/ppermute | solution.py:33
  76.9 4.5 %attend_bands.1 = bf16[1,640,128]{2,1,0:T(8,128)(2,1)S(1)} custom-call(s32[1]{0:T(128)} %bitcast.7.qid, s32[12]{0:T(128)S(1)} %pad_add_fusion.1.kid, s32[256]{0:T(256)S(1)} %reshape.7.bs, s32[16]{0:T(128)S(1)} %copy-done, bf16[640,640]{1,0:T(8,128)(2,1)} %q.3, bf16[4,2,256,128]{3,2,1,0:T(8,128)(2,1)S(1)} %collective-permute-done.10.g1, ...), custom_call_target="tpu_custom_call" | custom-call | flops 1006632960 | bytes 8388608 | tf_op jit(solution)/shard_map/attend_bands/pallas_call | solution.py:324
  82.0 3.8 %collective-permute-start.13 = (bf16[640,640]{1,0:T(8,128)(2,1)S(1)}, bf16[640,640]{1,0:T(8,128)(2,1)S(1)}, u32[]{:S(2)}, u32[]{:S(2)}) collective-permute-start(bf16[640,640]{1,0:T(8,128)(2,1)S(1)} %assemble.1.att), channel_id=1, source_target_pairs={{0,1},{1,0},{2,3},{3,2},{4,5},{5,4},{6,7},{7,6},{8,9},{9,8},{10,11... | collective-permute-start | bytes 2457608 | tf_op jit(solution)/shard_map/ppermute | solution.py:45
  85.8 2.3 %first_share.1 = (f32[640,640]{1,0:T(8,128)S(1)}, bf16[640,640]{1,0:T(8,128)(2,1)S(1)}) custom-call(s32[1]{0:T(128)S(6)} %add.218.blocks, bf16[640,640]{1,0:T(8,128)(2,1)S(1)} %assemble.1.att, bf16[640,5120]{1,0:T(8,128)(2,1)} %w_mine.3, bf16[640,5120]{1,0:T(8,128)(2,1)} %collective-permute-done.6.after.other.w_other), custom_call_target="tpu_custom_call" | custom-call | tf_op jit(solution)/shard_map/first_share/pallas_call | solution.py:401
  90.8 1.7 %collective-permute-start.15 = (bf16[320,640]{1,0:T(8,128)(2,1)S(1)}, bf16[320,640]{1,0:T(8,128)(2,1)S(1)}, u32[]{:S(2)}, u32[]{:S(2)}) collective-permute-start(bf16[320,640]{1,0:T(8,128)(2,1)S(1)} %get-tuple-element.53), channel_id=1, source_target_pairs={{0,6},{1,7},{2,0},{3,1},{4,2},{5,3},{6,4},{7,5},{8,14},{9,15},{10,... | collective-permute-start | bytes 1228808 | tf_op jit(solution)/shard_map/ppermute | solution.py:41
  92.5 5.2 %project.2.refs_0_.near = bf16[2,640,640]{2,1,0:T(8,128)(2,1)S(1)} custom-call(s32[2]{0:T(128)S(1)} %get-tuple-element.50.order, s32[2]{0:T(128)S(1)} %get-tuple-element.49.blocks, bf16[640,640]{1,0:T(8,128)(2,1)S(1)} %assemble.1.att, bf16[640,640]{1,0:T(8,128)(2,1)S(1)} %collective-permute-done.13.att_other, bf16[640,5120]{1,0:T(8,128)(2,1)} %w_mine.3, ...), custom_call_target="tpu_custom_call" | custom-call | tf_op jit(solution)/shard_map/project/pallas_call | solution.py:372
  98.2 2.9 %collective-permute-start.19 = (bf16[320,640]{1,0:T(8,128)(2,1)S(1)}, bf16[320,640]{1,0:T(8,128)(2,1)S(1)}, u32[]{:S(2)}, u32[]{:S(2)}) collective-permute-start(bf16[320,640]{1,0:T(8,128)(2,1)S(1)} %get-tuple-element.51), channel_id=1, source_target_pairs={{0,6},{1,7},{2,0},{3,1},{4,2},{5,3},{6,4},{7,5},{8,14},{9,15},{10,... | collective-permute-start | bytes 1228808 | tf_op jit(solution)/shard_map/ppermute | solution.py:41
  103.4 1.6 %collective-permute-start.16 = (bf16[320,640]{1,0:T(8,128)(2,1)S(1)}, bf16[320,640]{1,0:T(8,128)(2,1)S(1)}, u32[]{:S(2)}, u32[]{:S(2)}) collective-permute-start(bf16[320,640]{1,0:T(8,128)(2,1)S(1)} %get-tuple-element.47), channel_id=1, source_target_pairs={{0,2},{1,3},{2,4},{3,5},{4,6},{5,7},{6,0},{7,1},{8,10},{9,11},{10,... | collective-permute-start | bytes 1228808 | tf_op jit(solution)/shard_map/ppermute | solution.py:41
  105.0 1.7 %collective-permute-start.18 = (bf16[320,640]{1,0:T(8,128)(2,1)S(1)}, bf16[320,640]{1,0:T(8,128)(2,1)S(1)}, u32[]{:S(2)}, u32[]{:S(2)}) collective-permute-start(bf16[320,640]{1,0:T(8,128)(2,1)S(1)} %get-tuple-element.48), channel_id=1, source_target_pairs={{0,6},{1,7},{2,0},{3,1},{4,2},{5,3},{6,4},{7,5},{8,14},{9,15},{10,... | collective-permute-start | bytes 1228808 | tf_op jit(solution)/shard_map/ppermute | solution.py:41
  106.7 3.0 %project.3 = bf16[1,640,640]{2,1,0:T(8,128)(2,1)S(1)} custom-call(s32[1]{0:T(128)S(6)} %select_n.128.order, s32[1]{0:T(128)S(6)} %add.179.blocks, bf16[640,640]{1,0:T(8,128)(2,1)S(1)} %assemble.1.att, bf16[640,640]{1,0:T(8,128)(2,1)S(1)} %collective-permute-done.13.att_other, bf16[640,5120]{1,0:T(8,128)(2,1)} %w_mine.3, ...), custom_call_target="tpu_custom_call" | custom-call | tf_op jit(solution)/shard_map/project/pallas_call | solution.py:372
  109.7 1.8 %collective-permute-done.17.plain_up = bf16[320,640]{1,0:T(8,128)(2,1)S(1)} collective-permute-done((bf16[320,640]{1,0:T(8,128)(2,1)S(1)}, bf16[320,640]{1,0:T(8,128)(2,1)S(1)}, u32[]{:S(2)}, u32[]{:S(2)}) %collective-permute-start.17) | collective-permute-done | bytes 409632 | tf_op jit(solution)/shard_map/ppermute | solution.py:41
  112.0 7.5 %collective-permute-done.16.more_up = bf16[320,640]{1,0:T(8,128)(2,1)S(1)} collective-permute-done((bf16[320,640]{1,0:T(8,128)(2,1)S(1)}, bf16[320,640]{1,0:T(8,128)(2,1)S(1)}, u32[]{:S(2)}, u32[]{:S(2)}) %collective-permute-start.16) | collective-permute-done | bytes 409632 | tf_op jit(solution)/shard_map/ppermute | solution.py:41
  (48 shorter events, 17.2 us)
Async XLA Ops:
  0.0 34.7 %collective-permute-start.6 = (bf16[640,5120]{1,0:T(8,128)(2,1)}, bf16[640,5120]{1,0:T(8,128)(2,1)}, u32[]{:S(2)}, u32[]{:S(2)}) collective-permute-start(bf16[640,5120]{1,0:T(8,128)(2,1)} %w_mine.3), channel_id=1, source_target_pairs={{0,1},{1,0},{2,3},{3,2},{4,5},{5,4},{6,7},{7,6},{8,9},{9,8},{10,11... | collective-permute-start | bytes 19660808 | tf_op jit(solution)/shard_map/ppermute | solution.py:45
  2.0 20.7 %collective-permute-start = (bf16[5,640,128]{2,1,0:T(8,128)(2,1)S(1)}, bf16[5,640,128]{2,1,0:T(8,128)(2,1)S(1)}, u32[]{:S(2)}, u32[]{:S(2)}) collective-permute-start(bf16[5,640,128]{2,1,0:T(8,128)(2,1)S(1)} %get-tuple-element.28), channel_id=1, source_target_pairs={{0,8},{1,33},{2,10},{3,35},{4,12},{5,37},{6,14},{7,39},{8,16},{9,4... | collective-permute-start | bytes 2457608 | tf_op jit(solution)/shard_map/ppermute | solution.py:33
  4.0 18.7 %collective-permute-start.1 = (bf16[5,640,128]{2,1,0:T(8,128)(2,1)S(1)}, bf16[5,640,128]{2,1,0:T(8,128)(2,1)S(1)}, u32[]{:S(2)}, u32[]{:S(2)}) collective-permute-start(bf16[5,640,128]{2,1,0:T(8,128)(2,1)S(1)} %get-tuple-element.29), channel_id=1, source_target_pairs={{0,16},{1,65},{2,18},{3,67},{4,20},{5,69},{6,22},{7,71},{8,24},{9,... | collective-permute-start | bytes 2457608 | tf_op jit(solution)/shard_map/ppermute | solution.py:33
  5.1 21.1 %collective-permute-start.2 = (bf16[5,640,128]{2,1,0:T(8,128)(2,1)S(1)}, bf16[5,640,128]{2,1,0:T(8,128)(2,1)S(1)}, u32[]{:S(2)}, u32[]{:S(2)}) collective-permute-start(bf16[5,640,128]{2,1,0:T(8,128)(2,1)S(1)} %get-tuple-element.30), channel_id=1, source_target_pairs={{0,24},{1,97},{2,26},{3,99},{4,28},{5,101},{6,30},{7,103},{8,0},{9... | collective-permute-start | bytes 2457608 | tf_op jit(solution)/shard_map/ppermute | solution.py:33
  26.2 6.9 %copy-start.1 = (s32[16,16]{1,0:T(8,128)S(1)}, s32[16,16]{1,0:T(8,128)}, u32[]{:S(2)}) copy-start(s32[16,16]{1,0:T(8,128)} %param.12) | copy-start | bytes 3076
  27.4 23.4 %collective-permute-start.5 = (bf16[8,640,128]{2,1,0:T(8,128)(2,1)}, bf16[8,640,128]{2,1,0:T(8,128)(2,1)}, u32[]{:S(2)}, u32[]{:S(2)}) collective-permute-start(bf16[8,640,128]{2,1,0:T(8,128)(2,1)} %stack.3.kv), channel_id=1, source_target_pairs={{0,32},{1,9},{2,34},{3,11},{4,36},{5,13},{6,38},{7,15},{8,40},{9,1... | collective-permute-start | bytes 3932168 | tf_op jit(solution)/shard_map/ppermute | solution.py:37
  28.9 32.8 %collective-permute-start.3 = (bf16[8,640,128]{2,1,0:T(8,128)(2,1)}, bf16[8,640,128]{2,1,0:T(8,128)(2,1)}, u32[]{:S(2)}, u32[]{:S(2)}) collective-permute-start(bf16[8,640,128]{2,1,0:T(8,128)(2,1)} %stack.3.kv), channel_id=1, source_target_pairs={{0,64},{1,17},{2,66},{3,19},{4,68},{5,21},{6,70},{7,23},{8,72},{9,... | collective-permute-start | bytes 3932168 | tf_op jit(solution)/shard_map/ppermute | solution.py:37
  31.7 30.0 %collective-permute-start.4 = (bf16[8,640,128]{2,1,0:T(8,128)(2,1)}, bf16[8,640,128]{2,1,0:T(8,128)(2,1)}, u32[]{:S(2)}, u32[]{:S(2)}) collective-permute-start(bf16[8,640,128]{2,1,0:T(8,128)(2,1)} %stack.3.kv), channel_id=1, source_target_pairs={{0,96},{1,25},{2,98},{3,27},{4,100},{5,29},{6,102},{7,31},{8,104},... | collective-permute-start | bytes 3932168 | tf_op jit(solution)/shard_map/ppermute | solution.py:37
  33.4 1.4 %copy-start = (s32[16]{0:T(128)S(1)}, s32[16]{0:T(128)}, u32[]{:S(2)}) copy-start(s32[16]{0:T(128)} %bw.9) | copy-start | bytes 196
  49.4 25.7 %collective-permute-start.10 = (bf16[4,2,256,128]{3,2,1,0:T(8,128)(2,1)}, bf16[4,2,256,128]{3,2,1,0:T(8,128)(2,1)S(1)}, u32[]{:S(2)}, u32[]{:S(2)}) collective-permute-start(bf16[4,2,256,128]{3,2,1,0:T(8,128)(2,1)} %get-tuple-element.39), channel_id=1, source_target_pairs={{0,32},{1,9},{2,34},{3,11},{4,36},{5,13},{6,38},{7,15},{8,40},{9,1... | collective-permute-start | bytes 1572872 | tf_op jit(solution)/shard_map/ppermute | solution.py:37
  50.0 26.9 %collective-permute-start.11 = (bf16[4,2,256,128]{3,2,1,0:T(8,128)(2,1)}, bf16[4,2,256,128]{3,2,1,0:T(8,128)(2,1)S(1)}, u32[]{:S(2)}, u32[]{:S(2)}) collective-permute-start(bf16[4,2,256,128]{3,2,1,0:T(8,128)(2,1)} %get-tuple-element.40), channel_id=1, source_target_pairs={{0,64},{1,17},{2,66},{3,19},{4,68},{5,21},{6,70},{7,23},{8,72},{9,... | collective-permute-start | bytes 1572872 | tf_op jit(solution)/shard_map/ppermute | solution.py:37
  50.8 26.1 %collective-permute-start.12 = (bf16[4,2,256,128]{3,2,1,0:T(8,128)(2,1)}, bf16[4,2,256,128]{3,2,1,0:T(8,128)(2,1)S(1)}, u32[]{:S(2)}, u32[]{:S(2)}) collective-permute-start(bf16[4,2,256,128]{3,2,1,0:T(8,128)(2,1)} %get-tuple-element.41), channel_id=1, source_target_pairs={{0,96},{1,25},{2,98},{3,27},{4,100},{5,29},{6,102},{7,31},{8,104},... | collective-permute-start | bytes 1572872 | tf_op jit(solution)/shard_map/ppermute | solution.py:37
  72.6 8.8 %collective-permute-start.7 = (bf16[640,128]{1,0:T(8,128)(2,1)S(1)}, bf16[640,128]{1,0:T(8,128)(2,1)S(1)}, u32[]{:S(2)}, u32[]{:S(2)}) collective-permute-start(bf16[640,128]{1,0:T(8,128)(2,1)S(1)} %get-tuple-element.57), channel_id=1, source_target_pairs={{0,24},{1,97},{2,26},{3,99},{4,28},{5,101},{6,30},{7,103},{8,0},{9... | collective-permute-start | bytes 491528 | tf_op jit(solution)/shard_map/ppermute | solution.py:33
  73.2 8.2 %collective-permute-start.8 = (bf16[640,128]{1,0:T(8,128)(2,1)S(1)}, bf16[640,128]{1,0:T(8,128)(2,1)S(1)}, u32[]{:S(2)}, u32[]{:S(2)}) collective-permute-start(bf16[640,128]{1,0:T(8,128)(2,1)S(1)} %get-tuple-element.56), channel_id=1, source_target_pairs={{0,16},{1,65},{2,18},{3,67},{4,20},{5,69},{6,22},{7,71},{8,24},{9,... | collective-permute-start | bytes 491528 | tf_op jit(solution)/shard_map/ppermute | solution.py:33
  75.1 6.7 %collective-permute-start.9 = (bf16[640,128]{1,0:T(8,128)(2,1)S(1)}, bf16[640,128]{1,0:T(8,128)(2,1)S(1)}, u32[]{:S(2)}, u32[]{:S(2)}) collective-permute-start(bf16[640,128]{1,0:T(8,128)(2,1)S(1)} %get-tuple-element.55), channel_id=1, source_target_pairs={{0,8},{1,33},{2,10},{3,35},{4,12},{5,37},{6,14},{7,39},{8,16},{9,4... | collective-permute-start | bytes 491528 | tf_op jit(solution)/shard_map/ppermute | solution.py:33
  82.0 6.2 %collective-permute-start.13 = (bf16[640,640]{1,0:T(8,128)(2,1)S(1)}, bf16[640,640]{1,0:T(8,128)(2,1)S(1)}, u32[]{:S(2)}, u32[]{:S(2)}) collective-permute-start(bf16[640,640]{1,0:T(8,128)(2,1)S(1)} %assemble.1.att), channel_id=1, source_target_pairs={{0,1},{1,0},{2,3},{3,2},{4,5},{5,4},{6,7},{7,6},{8,9},{9,8},{10,11... | collective-permute-start | bytes 2457608 | tf_op jit(solution)/shard_map/ppermute | solution.py:45
  89.1 3.4 %copy-start.2 = (s32[2]{0:T(128)S(1)}, s32[2]{0:T(128)}, u32[]{:S(2)}) copy-start(s32[2]{0:T(128)} %constant.177.clone) | copy-start | bytes 28
  89.2 13.3 %collective-permute-start.14 = (bf16[320,640]{1,0:T(8,128)(2,1)S(1)}, bf16[320,640]{1,0:T(8,128)(2,1)S(1)}, u32[]{:S(2)}, u32[]{:S(2)}) collective-permute-start(bf16[320,640]{1,0:T(8,128)(2,1)S(1)} %get-tuple-element.54), channel_id=1, source_target_pairs={{0,2},{1,3},{2,4},{3,5},{4,6},{5,7},{6,0},{7,1},{8,10},{9,11},{10,... | collective-permute-start | bytes 1228808 | tf_op jit(solution)/shard_map/ppermute | solution.py:41
  90.8 12.4 %collective-permute-start.15 = (bf16[320,640]{1,0:T(8,128)(2,1)S(1)}, bf16[320,640]{1,0:T(8,128)(2,1)S(1)}, u32[]{:S(2)}, u32[]{:S(2)}) collective-permute-start(bf16[320,640]{1,0:T(8,128)(2,1)S(1)} %get-tuple-element.53), channel_id=1, source_target_pairs={{0,6},{1,7},{2,0},{3,1},{4,2},{5,3},{6,4},{7,5},{8,14},{9,15},{10,... | collective-permute-start | bytes 1228808 | tf_op jit(solution)/shard_map/ppermute | solution.py:41
  97.8 13.7 %collective-permute-start.17 = (bf16[320,640]{1,0:T(8,128)(2,1)S(1)}, bf16[320,640]{1,0:T(8,128)(2,1)S(1)}, u32[]{:S(2)}, u32[]{:S(2)}) collective-permute-start(bf16[320,640]{1,0:T(8,128)(2,1)S(1)} %get-tuple-element.52), channel_id=1, source_target_pairs={{0,2},{1,3},{2,4},{3,5},{4,6},{5,7},{6,0},{7,1},{8,10},{9,11},{10,... | collective-permute-start | bytes 1228808 | tf_op jit(solution)/shard_map/ppermute | solution.py:41
  98.2 13.7 %collective-permute-start.19 = (bf16[320,640]{1,0:T(8,128)(2,1)S(1)}, bf16[320,640]{1,0:T(8,128)(2,1)S(1)}, u32[]{:S(2)}, u32[]{:S(2)}) collective-permute-start(bf16[320,640]{1,0:T(8,128)(2,1)S(1)} %get-tuple-element.51), channel_id=1, source_target_pairs={{0,6},{1,7},{2,0},{3,1},{4,2},{5,3},{6,4},{7,5},{8,14},{9,15},{10,... | collective-permute-start | bytes 1228808 | tf_op jit(solution)/shard_map/ppermute | solution.py:41
  103.4 16.1 %collective-permute-start.16 = (bf16[320,640]{1,0:T(8,128)(2,1)S(1)}, bf16[320,640]{1,0:T(8,128)(2,1)S(1)}, u32[]{:S(2)}, u32[]{:S(2)}) collective-permute-start(bf16[320,640]{1,0:T(8,128)(2,1)S(1)} %get-tuple-element.47), channel_id=1, source_target_pairs={{0,2},{1,3},{2,4},{3,5},{4,6},{5,7},{6,0},{7,1},{8,10},{9,11},{10,... | collective-permute-start | bytes 1228808 | tf_op jit(solution)/shard_map/ppermute | solution.py:41
  105.0 14.5 %collective-permute-start.18 = (bf16[320,640]{1,0:T(8,128)(2,1)S(1)}, bf16[320,640]{1,0:T(8,128)(2,1)S(1)}, u32[]{:S(2)}, u32[]{:S(2)}) collective-permute-start(bf16[320,640]{1,0:T(8,128)(2,1)S(1)} %get-tuple-element.48), channel_id=1, source_target_pairs={{0,6},{1,7},{2,0},{3,1},{4,2},{5,3},{6,4},{7,5},{8,14},{9,15},{10,... | collective-permute-start | bytes 1228808 | tf_op jit(solution)/shard_map/ppermute | solution.py:41

commit v8 on v7

--- a/solution.py
+++ b/solution.py
@@ -90,12 +90,15 @@
     )(pos, *in_hbm(queries, keys, values))
 
 
+HANDED = (0, 2, 1, 3)
+
+
 def stack_kernel(parts, *refs):
     pieces, outs, sems = refs[:SIDE], refs[SIDE:-1], refs[-1]
     copies = []
     for out, rows in zip(outs, parts):
         for j, part in enumerate(rows):
-            for s, piece in enumerate(pieces):
+            for s, piece in zip(HANDED, pieces):
                 copies.append(pltpu.make_async_copy(piece.at[part], out.at[j * SIDE + s], sems.at[len(copies)]))
     for copy in copies:
         copy.start()
@@ -112,7 +115,7 @@
         scratch_shapes=[pltpu.SemaphoreType.DMA((SIDE * sum(map(len, parts)),))],
         compiler_params=pltpu.CompilerParams(vmem_limit_bytes=LIMIT),
         name="stack",
-    )(*pieces)
+    )(*[pieces[s] for s in HANDED])
 
 
 def block_rows(n):
@@ -339,8 +342,8 @@
     )(qid, kid, bs, bw, *in_hbm(queries), *groups, *in_hbm(*state, after))
 
 
-def assemble_kernel(pos, o0, o1, o2, o3, o4, att):
-    for s, o in enumerate((o0, o1, o2, o3)):
+def assemble_kernel(pos, o0, o2, o1, o3, o4, att):
+    for s, o in zip(HANDED, (o0, o2, o1, o3)):
         head = lax.rem(pos[0] + s, SIDE)
         att[:, pl.ds(pl.multiple_of(head * HD, HD), HD)] = o[...]
     att[:, SIDE * HD :] = o4[...]
@@ -354,7 +357,7 @@
         out_shape=jax.ShapeDtypeStruct((FT, 5 * HD), jnp.bfloat16),
         compiler_params=pltpu.CompilerParams(vmem_limit_bytes=LIMIT),
         name="assemble",
-    )(pos, *outs)
+    )(pos, *[outs[s] for s in HANDED], outs[SIDE])
 
 
 def project_kernel(order, blocks, att, att_other, w_mine, w_other, *refs):

time: 122 us -> 121 us (level)
  transfers between devices with their start and end apart: 20 -> 20, of which waited for: 9 -> 8; matrix products, arithmetic and copies ran while one was open for 0% -> 0% of each run, Pallas kernels for 45% -> 45%
where the time goes in v8:
time: 121 us; the launch traced here: 120 us
  Pallas kernels  56.1 us (46%)
  starting transfers between devices  32.6 us (27%)
  waiting for transfers between devices  30.5 us (25%)
    pallas_call x2, Pallas kernels, attend_groups(): pl.pallas_call(functools.partial(groups_kernel, len(groups), finished), g...  19.5 us
    ppermute x6, waiting for transfers between devices, line_shift(): lax.ppermute(v, BOTH, pairs(lambda x, z, y, c: (x, z + s, y, c) if c == 0...  18.1 us
    ppermute x6, waiting for transfers between devices, y_shift(): return lax.ppermute(v, BOTH, pairs(lambda x, z, y, c: (x, z, y + s, c)))  11.9 us
    ppermute x6, starting transfers between devices, y_shift(): return lax.ppermute(v, BOTH, pairs(lambda x, z, y, c: (x, z, y + s, c)))  9.92 us
    pallas_call x1, Pallas kernels, attend_line(): pl.pallas_call(line_kernel, grid_spec=pltpu.PrefetchScalarGridSpec(num_sc...  9.71 us
    ppermute x6, starting transfers between devices, line_shift(): lax.ppermute(v, BOTH, pairs(lambda x, z, y, c: (x, z + s, y, c) if c == 0...  9.62 us
    ppermute x6, starting transfers between devices, cross_shift(): lax.ppermute(v, BOTH, pairs(lambda x, z, y, c: (x + s, z, y, c) if c == 0...  8.99 us
    pallas_call x2, Pallas kernels, project(): pl.pallas_call(project_kernel, grid_spec=pltpu.PrefetchScalarGridSpec(num...  8.25 us
  transfers between devices with their start and end apart: 20, of which 8 were waited for; matrix products, arithmetic and copies ran while one was open for 0% of the time, Pallas kernels for 45%

profile of v8, /device:TPU:32, one launch (start us, length us, event | category | flops | bytes accessed | tf_op | source)
XLA Modules:
  0.0 119.9 jit_solution(7972097036443697968)
XLA Ops:
  0.0 2.0 %pick.1 = (bf16[5,640,128]{2,1,0:T(8,128)(2,1)S(1)}, bf16[5,640,128]{2,1,0:T(8,128)(2,1)S(1)}, bf16[5,640,128]{2,1,0:T(8,128)(2,1)S(1)}, bf16[5,640,128]{2,1,0:T(8,128)(2,1)S(1)}) custom-call(s32[1]{0:T(128)} %bitcast.2.pos, bf16[640,640]{1,0:T(8,128)(2,1)} %q.3, bf16[640,640]{1,0:T(8,128)(2,1)} %k_any.1, bf16[640,640]{1,0:T(8,128)(2,1)} %v_any.1), custom_call_target="tpu_custom_call" | custom-call | tf_op jit(solution)/shard_map/pick/pallas_call | solution.py:82
  2.0 3.1 %collective-permute-start = (bf16[5,640,128]{2,1,0:T(8,128)(2,1)S(1)}, bf16[5,640,128]{2,1,0:T(8,128)(2,1)S(1)}, u32[]{:S(2)}, u32[]{:S(2)}) collective-permute-start(bf16[5,640,128]{2,1,0:T(8,128)(2,1)S(1)} %get-tuple-element.28), channel_id=1, source_target_pairs={{0,16},{1,65},{2,18},{3,67},{4,20},{5,69},{6,22},{7,71},{8,24},{9,... | collective-permute-start | bytes 2457608 | tf_op jit(solution)/shard_map/ppermute | solution.py:33
  5.0 2.0 %collective-permute-start.2 = (bf16[5,640,128]{2,1,0:T(8,128)(2,1)S(1)}, bf16[5,640,128]{2,1,0:T(8,128)(2,1)S(1)}, u32[]{:S(2)}, u32[]{:S(2)}) collective-permute-start(bf16[5,640,128]{2,1,0:T(8,128)(2,1)S(1)} %get-tuple-element.30), channel_id=1, source_target_pairs={{0,24},{1,97},{2,26},{3,99},{4,28},{5,101},{6,30},{7,103},{8,0},{9... | collective-permute-start | bytes 2457608 | tf_op jit(solution)/shard_map/ppermute | solution.py:33
  7.1 8.9 %collective-permute-done.refs_1_ = bf16[5,640,128]{2,1,0:T(8,128)(2,1)S(1)} collective-permute-done((bf16[5,640,128]{2,1,0:T(8,128)(2,1)S(1)}, bf16[5,640,128]{2,1,0:T(8,128)(2,1)S(1)}, u32[]{:S(2)}, u32[]{:S(2)}) %collective-permute-start) | collective-permute-done | bytes 819232 | tf_op jit(solution)/shard_map/ppermute | solution.py:33
  16.0 9.2 %collective-permute-done.1.refs_2_ = bf16[5,640,128]{2,1,0:T(8,128)(2,1)S(1)} collective-permute-done((bf16[5,640,128]{2,1,0:T(8,128)(2,1)S(1)}, bf16[5,640,128]{2,1,0:T(8,128)(2,1)S(1)}, u32[]{:S(2)}, u32[]{:S(2)}) %collective-permute-start.1) | collective-permute-done | bytes 819232 | tf_op jit(solution)/shard_map/ppermute | solution.py:33
  27.9 2.7 %collective-permute-start.3 = (bf16[8,640,128]{2,1,0:T(8,128)(2,1)}, bf16[8,640,128]{2,1,0:T(8,128)(2,1)}, u32[]{:S(2)}, u32[]{:S(2)}) collective-permute-start(bf16[8,640,128]{2,1,0:T(8,128)(2,1)} %stack.3.kv), channel_id=1, source_target_pairs={{0,64},{1,17},{2,66},{3,19},{4,68},{5,21},{6,70},{7,23},{8,72},{9,... | collective-permute-start | bytes 3932168 | tf_op jit(solution)/shard_map/ppermute | solution.py:37
  33.7 9.7 %attend_line.1 = (bf16[4,640,128]{2,1,0:T(8,128)(2,1)}, f32[4,640,128]{2,1,0:T(8,128)}) custom-call(s32[4]{0:T(128)S(1)} %broadcast_select_fusion.4.qid.kid, s32[4]{0:T(128)S(1)} %broadcast_select_fusion.4.qid.kid, s32[256]{0:T(256)S(1)} %reshape.7.bs, s32[16]{0:T(128)S(1)} %copy-done, bf16[4,640,128]{2,1,0:T(8,128)(2,1)} %get-tuple-element.31.q, ...), custom_call_target="tpu_custom_call" | custom-call | flops 1845493760 | bytes 8388608 | tf_op jit(solution)/shard_map/attend_line/pallas_call | solution.py:236
  43.4 4.9 %attend_last_line.1 = (bf16[1,640,128]{2,1,0:T(8,128)(2,1)}, f32[1,640,128]{2,1,0:T(8,128)}, bf16[4,2,256,128]{3,2,1,0:T(8,128)(2,1)}, bf16[4,2,256,128]{3,2,1,0:T(8,128)(2,1)}, bf16[4,2,256,128]{3,2,1,0:T(8,128)(2,1)}) custom-call(s32[4]{0:T(128)S(1)} %broadcast_select_fusion.qid, s32[4]{0:T(128)S(1)} %broadcast_select_fusion.4.qid.kid, s32[256]{0:T(256)S(1)} %reshape.7.bs, ...), custom_call_target="tpu_custom_call" | custom-call | flops 461373440 | bytes 8388608 | tf_op jit(solution)/shard_map/attend_last_line/pallas_call | solution.py:256
  49.8 1.8 %collective-permute-start.12 = (bf16[4,2,256,128]{3,2,1,0:T(8,128)(2,1)}, bf16[4,2,256,128]{3,2,1,0:T(8,128)(2,1)S(1)}, u32[]{:S(2)}, u32[]{:S(2)}) collective-permute-start(bf16[4,2,256,128]{3,2,1,0:T(8,128)(2,1)} %get-tuple-element.41), channel_id=1, source_target_pairs={{0,96},{1,25},{2,98},{3,27},{4,100},{5,29},{6,102},{7,31},{8,104},... | collective-permute-start | bytes 1572872 | tf_op jit(solution)/shard_map/ppermute | solution.py:37
  51.6 8.7 %attend_groups.2 = (bf16[4,640,128]{2,1,0:T(8,128)(2,1)}, f32[4,640,128]{2,1,0:T(8,128)}) custom-call(s32[4]{0:T(128)S(1)} %broadcast_select_fusion.4.qid.kid, s32[4]{0:T(128)S(1)} %broadcast_select_fusion.1.kid, s32[256]{0:T(256)S(1)} %reshape.7.bs, s32[16]{0:T(128)S(1)} %copy-done, bf16[4,640,128]{2,1,0:T(8,128)(2,1)} %get-tuple-element.31.q, ...), custom_call_target="tpu_custom_call" | custom-call | flops 1342177280 | bytes 8388608 | tf_op jit(solution)/shard_map/attend_groups/pallas_call | solution.py:298
  60.7 10.8 %attend_groups.3 = (bf16[4,640,128]{2,1,0:T(8,128)(2,1)S(1)}, f32[8,128]{1,0:T(8,128)}) custom-call(s32[4]{0:T(128)S(1)} %broadcast_select_fusion.4.qid.kid, s32[8]{0:T(128)S(1)} %pad_add_fusion.kid, s32[256]{0:T(256)S(1)} %reshape.7.bs, s32[16]{0:T(128)S(1)} %copy-done, bf16[4,640,128]{2,1,0:T(8,128)(2,1)} %get-tuple-element.31.q, ...), custom_call_target="tpu_custom_call" | custom-call | flops 2684354560 | bytes 8388608 | tf_op jit(solution)/shard_map/attend_groups/pallas_call | solution.py:298
  71.6 2.5 %collective-permute-start.7 = (bf16[640,128]{1,0:T(8,128)(2,1)S(1)}, bf16[640,128]{1,0:T(8,128)(2,1)S(1)}, u32[]{:S(2)}, u32[]{:S(2)}) collective-permute-start(bf16[640,128]{1,0:T(8,128)(2,1)S(1)} %get-tuple-element.57), channel_id=1, source_target_pairs={{0,16},{1,65},{2,18},{3,67},{4,20},{5,69},{6,22},{7,71},{8,24},{9,... | collective-permute-start | bytes 491528 | tf_op jit(solution)/shard_map/ppermute | solution.py:33
  76.2 4.5 %attend_bands.1 = bf16[1,640,128]{2,1,0:T(8,128)(2,1)S(1)} custom-call(s32[1]{0:T(128)} %bitcast.7.qid, s32[12]{0:T(128)S(1)} %pad_add_fusion.1.kid, s32[256]{0:T(256)S(1)} %reshape.7.bs, s32[16]{0:T(128)S(1)} %copy-done, bf16[640,640]{1,0:T(8,128)(2,1)} %q.3, bf16[4,2,256,128]{3,2,1,0:T(8,128)(2,1)S(1)} %collective-permute-done.10.g1, ...), custom_call_target="tpu_custom_call" | custom-call | flops 1006632960 | bytes 8388608 | tf_op jit(solution)/shard_map/attend_bands/pallas_call | solution.py:327
  80.9 4.1 %collective-permute-start.13 = (bf16[640,640]{1,0:T(8,128)(2,1)S(1)}, bf16[640,640]{1,0:T(8,128)(2,1)S(1)}, u32[]{:S(2)}, u32[]{:S(2)}) collective-permute-start(bf16[640,640]{1,0:T(8,128)(2,1)S(1)} %assemble.1.att), channel_id=1, source_target_pairs={{0,1},{1,0},{2,3},{3,2},{4,5},{5,4},{6,7},{7,6},{8,9},{9,8},{10,11... | collective-permute-start | bytes 2457608 | tf_op jit(solution)/shard_map/ppermute | solution.py:45
  85.0 2.3 %first_share.1 = (f32[640,640]{1,0:T(8,128)S(1)}, bf16[640,640]{1,0:T(8,128)(2,1)S(1)}) custom-call(s32[1]{0:T(128)S(6)} %add.218.blocks, bf16[640,640]{1,0:T(8,128)(2,1)S(1)} %assemble.1.att, bf16[640,5120]{1,0:T(8,128)(2,1)} %w_mine.3, bf16[640,5120]{1,0:T(8,128)(2,1)} %collective-permute-done.6.after.other.w_other), custom_call_target="tpu_custom_call" | custom-call | tf_op jit(solution)/shard_map/first_share/pallas_call | solution.py:404
  88.4 1.6 %collective-permute-start.14 = (bf16[320,640]{1,0:T(8,128)(2,1)S(1)}, bf16[320,640]{1,0:T(8,128)(2,1)S(1)}, u32[]{:S(2)}, u32[]{:S(2)}) collective-permute-start(bf16[320,640]{1,0:T(8,128)(2,1)S(1)} %get-tuple-element.54), channel_id=1, source_target_pairs={{0,2},{1,3},{2,4},{3,5},{4,6},{5,7},{6,0},{7,1},{8,10},{9,11},{10,... | collective-permute-start | bytes 1228808 | tf_op jit(solution)/shard_map/ppermute | solution.py:41
  90.0 1.7 %collective-permute-start.15 = (bf16[320,640]{1,0:T(8,128)(2,1)S(1)}, bf16[320,640]{1,0:T(8,128)(2,1)S(1)}, u32[]{:S(2)}, u32[]{:S(2)}) collective-permute-start(bf16[320,640]{1,0:T(8,128)(2,1)S(1)} %get-tuple-element.53), channel_id=1, source_target_pairs={{0,6},{1,7},{2,0},{3,1},{4,2},{5,3},{6,4},{7,5},{8,14},{9,15},{10,... | collective-permute-start | bytes 1228808 | tf_op jit(solution)/shard_map/ppermute | solution.py:41
  91.7 5.2 %project.2.refs_0_.near = bf16[2,640,640]{2,1,0:T(8,128)(2,1)S(1)} custom-call(s32[2]{0:T(128)S(1)} %get-tuple-element.50.order, s32[2]{0:T(128)S(1)} %get-tuple-element.49.blocks, bf16[640,640]{1,0:T(8,128)(2,1)S(1)} %assemble.1.att, bf16[640,640]{1,0:T(8,128)(2,1)S(1)} %collective-permute-done.13.att_other, bf16[640,5120]{1,0:T(8,128)(2,1)} %w_mine.3, ...), custom_call_target="tpu_custom_call" | custom-call | tf_op jit(solution)/shard_map/project/pallas_call | solution.py:375
  97.5 2.9 %collective-permute-start.19 = (bf16[320,640]{1,0:T(8,128)(2,1)S(1)}, bf16[320,640]{1,0:T(8,128)(2,1)S(1)}, u32[]{:S(2)}, u32[]{:S(2)}) collective-permute-start(bf16[320,640]{1,0:T(8,128)(2,1)S(1)} %get-tuple-element.51), channel_id=1, source_target_pairs={{0,6},{1,7},{2,0},{3,1},{4,2},{5,3},{6,4},{7,5},{8,14},{9,15},{10,... | collective-permute-start | bytes 1228808 | tf_op jit(solution)/shard_map/ppermute | solution.py:41
  102.6 1.6 %collective-permute-start.16 = (bf16[320,640]{1,0:T(8,128)(2,1)S(1)}, bf16[320,640]{1,0:T(8,128)(2,1)S(1)}, u32[]{:S(2)}, u32[]{:S(2)}) collective-permute-start(bf16[320,640]{1,0:T(8,128)(2,1)S(1)} %get-tuple-element.47), channel_id=1, source_target_pairs={{0,2},{1,3},{2,4},{3,5},{4,6},{5,7},{6,0},{7,1},{8,10},{9,11},{10,... | collective-permute-start | bytes 1228808 | tf_op jit(solution)/shard_map/ppermute | solution.py:41
  104.2 1.7 %collective-permute-start.18 = (bf16[320,640]{1,0:T(8,128)(2,1)S(1)}, bf16[320,640]{1,0:T(8,128)(2,1)S(1)}, u32[]{:S(2)}, u32[]{:S(2)}) collective-permute-start(bf16[320,640]{1,0:T(8,128)(2,1)S(1)} %get-tuple-element.48), channel_id=1, source_target_pairs={{0,6},{1,7},{2,0},{3,1},{4,2},{5,3},{6,4},{7,5},{8,14},{9,15},{10,... | collective-permute-start | bytes 1228808 | tf_op jit(solution)/shard_map/ppermute | solution.py:41
  105.9 3.0 %project.3 = bf16[1,640,640]{2,1,0:T(8,128)(2,1)S(1)} custom-call(s32[1]{0:T(128)S(6)} %select_n.128.order, s32[1]{0:T(128)S(6)} %add.179.blocks, bf16[640,640]{1,0:T(8,128)(2,1)S(1)} %assemble.1.att, bf16[640,640]{1,0:T(8,128)(2,1)S(1)} %collective-permute-done.13.att_other, bf16[640,5120]{1,0:T(8,128)(2,1)} %w_mine.3, ...), custom_call_target="tpu_custom_call" | custom-call | tf_op jit(solution)/shard_map/project/pallas_call | solution.py:375
  108.9 1.8 %collective-permute-done.17.plain_up = bf16[320,640]{1,0:T(8,128)(2,1)S(1)} collective-permute-done((bf16[320,640]{1,0:T(8,128)(2,1)S(1)}, bf16[320,640]{1,0:T(8,128)(2,1)S(1)}, u32[]{:S(2)}, u32[]{:S(2)}) %collective-permute-start.17) | collective-permute-done | bytes 409632 | tf_op jit(solution)/shard_map/ppermute | solution.py:41
  111.2 7.5 %collective-permute-done.16.more_up = bf16[320,640]{1,0:T(8,128)(2,1)S(1)} collective-permute-done((bf16[320,640]{1,0:T(8,128)(2,1)S(1)}, bf16[320,640]{1,0:T(8,128)(2,1)S(1)}, u32[]{:S(2)}, u32[]{:S(2)}) %collective-permute-start.16) | collective-permute-done | bytes 409632 | tf_op jit(solution)/shard_map/ppermute | solution.py:41
  (48 shorter events, 15.4 us)
Async XLA Ops:
  0.0 33.7 %collective-permute-start.6 = (bf16[640,5120]{1,0:T(8,128)(2,1)}, bf16[640,5120]{1,0:T(8,128)(2,1)}, u32[]{:S(2)}, u32[]{:S(2)}) collective-permute-start(bf16[640,5120]{1,0:T(8,128)(2,1)} %w_mine.3), channel_id=1, source_target_pairs={{0,1},{1,0},{2,3},{3,2},{4,5},{5,4},{6,7},{7,6},{8,9},{9,8},{10,11... | collective-permute-start | bytes 19660808 | tf_op jit(solution)/shard_map/ppermute | solution.py:45
  2.0 14.0 %collective-permute-start = (bf16[5,640,128]{2,1,0:T(8,128)(2,1)S(1)}, bf16[5,640,128]{2,1,0:T(8,128)(2,1)S(1)}, u32[]{:S(2)}, u32[]{:S(2)}) collective-permute-start(bf16[5,640,128]{2,1,0:T(8,128)(2,1)S(1)} %get-tuple-element.28), channel_id=1, source_target_pairs={{0,16},{1,65},{2,18},{3,67},{4,20},{5,69},{6,22},{7,71},{8,24},{9,... | collective-permute-start | bytes 2457608 | tf_op jit(solution)/shard_map/ppermute | solution.py:33
  5.0 20.1 %collective-permute-start.1 = (bf16[5,640,128]{2,1,0:T(8,128)(2,1)S(1)}, bf16[5,640,128]{2,1,0:T(8,128)(2,1)S(1)}, u32[]{:S(2)}, u32[]{:S(2)}) collective-permute-start(bf16[5,640,128]{2,1,0:T(8,128)(2,1)S(1)} %get-tuple-element.29), channel_id=1, source_target_pairs={{0,8},{1,33},{2,10},{3,35},{4,12},{5,37},{6,14},{7,39},{8,16},{9,4... | collective-permute-start | bytes 2457608 | tf_op jit(solution)/shard_map/ppermute | solution.py:33
  5.0 20.1 %collective-permute-start.2 = (bf16[5,640,128]{2,1,0:T(8,128)(2,1)S(1)}, bf16[5,640,128]{2,1,0:T(8,128)(2,1)S(1)}, u32[]{:S(2)}, u32[]{:S(2)}) collective-permute-start(bf16[5,640,128]{2,1,0:T(8,128)(2,1)S(1)} %get-tuple-element.30), channel_id=1, source_target_pairs={{0,24},{1,97},{2,26},{3,99},{4,28},{5,101},{6,30},{7,103},{8,0},{9... | collective-permute-start | bytes 2457608 | tf_op jit(solution)/shard_map/ppermute | solution.py:33
  25.2 6.9 %copy-start.1 = (s32[16,16]{1,0:T(8,128)S(1)}, s32[16,16]{1,0:T(8,128)}, u32[]{:S(2)}) copy-start(s32[16,16]{1,0:T(8,128)} %param.12) | copy-start | bytes 3076
  26.3 23.4 %collective-permute-start.5 = (bf16[8,640,128]{2,1,0:T(8,128)(2,1)}, bf16[8,640,128]{2,1,0:T(8,128)(2,1)}, u32[]{:S(2)}, u32[]{:S(2)}) collective-permute-start(bf16[8,640,128]{2,1,0:T(8,128)(2,1)} %stack.3.kv), channel_id=1, source_target_pairs={{0,32},{1,9},{2,34},{3,11},{4,36},{5,13},{6,38},{7,15},{8,40},{9,1... | collective-permute-start | bytes 3932168 | tf_op jit(solution)/shard_map/ppermute | solution.py:37
  27.9 32.8 %collective-permute-start.3 = (bf16[8,640,128]{2,1,0:T(8,128)(2,1)}, bf16[8,640,128]{2,1,0:T(8,128)(2,1)}, u32[]{:S(2)}, u32[]{:S(2)}) collective-permute-start(bf16[8,640,128]{2,1,0:T(8,128)(2,1)} %stack.3.kv), channel_id=1, source_target_pairs={{0,64},{1,17},{2,66},{3,19},{4,68},{5,21},{6,70},{7,23},{8,72},{9,... | collective-permute-start | bytes 3932168 | tf_op jit(solution)/shard_map/ppermute | solution.py:37
  30.6 30.0 %collective-permute-start.4 = (bf16[8,640,128]{2,1,0:T(8,128)(2,1)}, bf16[8,640,128]{2,1,0:T(8,128)(2,1)}, u32[]{:S(2)}, u32[]{:S(2)}) collective-permute-start(bf16[8,640,128]{2,1,0:T(8,128)(2,1)} %stack.3.kv), channel_id=1, source_target_pairs={{0,96},{1,25},{2,98},{3,27},{4,100},{5,29},{6,102},{7,31},{8,104},... | collective-permute-start | bytes 3932168 | tf_op jit(solution)/shard_map/ppermute | solution.py:37
  32.3 1.4 %copy-start = (s32[16]{0:T(128)S(1)}, s32[16]{0:T(128)}, u32[]{:S(2)}) copy-start(s32[16]{0:T(128)} %bw.9) | copy-start | bytes 196
  48.3 26.4 %collective-permute-start.10 = (bf16[4,2,256,128]{3,2,1,0:T(8,128)(2,1)}, bf16[4,2,256,128]{3,2,1,0:T(8,128)(2,1)S(1)}, u32[]{:S(2)}, u32[]{:S(2)}) collective-permute-start(bf16[4,2,256,128]{3,2,1,0:T(8,128)(2,1)} %get-tuple-element.39), channel_id=1, source_target_pairs={{0,32},{1,9},{2,34},{3,11},{4,36},{5,13},{6,38},{7,15},{8,40},{9,1... | collective-permute-start | bytes 1572872 | tf_op jit(solution)/shard_map/ppermute | solution.py:37
  48.9 27.3 %collective-permute-start.11 = (bf16[4,2,256,128]{3,2,1,0:T(8,128)(2,1)}, bf16[4,2,256,128]{3,2,1,0:T(8,128)(2,1)S(1)}, u32[]{:S(2)}, u32[]{:S(2)}) collective-permute-start(bf16[4,2,256,128]{3,2,1,0:T(8,128)(2,1)} %get-tuple-element.40), channel_id=1, source_target_pairs={{0,64},{1,17},{2,66},{3,19},{4,68},{5,21},{6,70},{7,23},{8,72},{9,... | collective-permute-start | bytes 1572872 | tf_op jit(solution)/shard_map/ppermute | solution.py:37
  49.8 26.4 %collective-permute-start.12 = (bf16[4,2,256,128]{3,2,1,0:T(8,128)(2,1)}, bf16[4,2,256,128]{3,2,1,0:T(8,128)(2,1)S(1)}, u32[]{:S(2)}, u32[]{:S(2)}) collective-permute-start(bf16[4,2,256,128]{3,2,1,0:T(8,128)(2,1)} %get-tuple-element.41), channel_id=1, source_target_pairs={{0,96},{1,25},{2,98},{3,27},{4,100},{5,29},{6,102},{7,31},{8,104},... | collective-permute-start | bytes 1572872 | tf_op jit(solution)/shard_map/ppermute | solution.py:37
  71.6 9.1 %collective-permute-start.7 = (bf16[640,128]{1,0:T(8,128)(2,1)S(1)}, bf16[640,128]{1,0:T(8,128)(2,1)S(1)}, u32[]{:S(2)}, u32[]{:S(2)}) collective-permute-start(bf16[640,128]{1,0:T(8,128)(2,1)S(1)} %get-tuple-element.57), channel_id=1, source_target_pairs={{0,16},{1,65},{2,18},{3,67},{4,20},{5,69},{6,22},{7,71},{8,24},{9,... | collective-permute-start | bytes 491528 | tf_op jit(solution)/shard_map/ppermute | solution.py:33
  74.1 6.6 %collective-permute-start.8 = (bf16[640,128]{1,0:T(8,128)(2,1)S(1)}, bf16[640,128]{1,0:T(8,128)(2,1)S(1)}, u32[]{:S(2)}, u32[]{:S(2)}) collective-permute-start(bf16[640,128]{1,0:T(8,128)(2,1)S(1)} %get-tuple-element.56), channel_id=1, source_target_pairs={{0,24},{1,97},{2,26},{3,99},{4,28},{5,101},{6,30},{7,103},{8,0},{9... | collective-permute-start | bytes 491528 | tf_op jit(solution)/shard_map/ppermute | solution.py:33
  74.7 6.0 %collective-permute-start.9 = (bf16[640,128]{1,0:T(8,128)(2,1)S(1)}, bf16[640,128]{1,0:T(8,128)(2,1)S(1)}, u32[]{:S(2)}, u32[]{:S(2)}) collective-permute-start(bf16[640,128]{1,0:T(8,128)(2,1)S(1)} %get-tuple-element.55), channel_id=1, source_target_pairs={{0,8},{1,33},{2,10},{3,35},{4,12},{5,37},{6,14},{7,39},{8,16},{9,4... | collective-permute-start | bytes 491528 | tf_op jit(solution)/shard_map/ppermute | solution.py:33
  80.9 6.5 %collective-permute-start.13 = (bf16[640,640]{1,0:T(8,128)(2,1)S(1)}, bf16[640,640]{1,0:T(8,128)(2,1)S(1)}, u32[]{:S(2)}, u32[]{:S(2)}) collective-permute-start(bf16[640,640]{1,0:T(8,128)(2,1)S(1)} %assemble.1.att), channel_id=1, source_target_pairs={{0,1},{1,0},{2,3},{3,2},{4,5},{5,4},{6,7},{7,6},{8,9},{9,8},{10,11... | collective-permute-start | bytes 2457608 | tf_op jit(solution)/shard_map/ppermute | solution.py:45
  88.3 3.4 %copy-start.2 = (s32[2]{0:T(128)S(1)}, s32[2]{0:T(128)}, u32[]{:S(2)}) copy-start(s32[2]{0:T(128)} %constant.177.clone) | copy-start | bytes 28
  88.4 13.3 %collective-permute-start.14 = (bf16[320,640]{1,0:T(8,128)(2,1)S(1)}, bf16[320,640]{1,0:T(8,128)(2,1)S(1)}, u32[]{:S(2)}, u32[]{:S(2)}) collective-permute-start(bf16[320,640]{1,0:T(8,128)(2,1)S(1)} %get-tuple-element.54), channel_id=1, source_target_pairs={{0,2},{1,3},{2,4},{3,5},{4,6},{5,7},{6,0},{7,1},{8,10},{9,11},{10,... | collective-permute-start | bytes 1228808 | tf_op jit(solution)/shard_map/ppermute | solution.py:41
  90.0 12.4 %collective-permute-start.15 = (bf16[320,640]{1,0:T(8,128)(2,1)S(1)}, bf16[320,640]{1,0:T(8,128)(2,1)S(1)}, u32[]{:S(2)}, u32[]{:S(2)}) collective-permute-start(bf16[320,640]{1,0:T(8,128)(2,1)S(1)} %get-tuple-element.53), channel_id=1, source_target_pairs={{0,6},{1,7},{2,0},{3,1},{4,2},{5,3},{6,4},{7,5},{8,14},{9,15},{10,... | collective-permute-start | bytes 1228808 | tf_op jit(solution)/shard_map/ppermute | solution.py:41
  97.0 13.7 %collective-permute-start.17 = (bf16[320,640]{1,0:T(8,128)(2,1)S(1)}, bf16[320,640]{1,0:T(8,128)(2,1)S(1)}, u32[]{:S(2)}, u32[]{:S(2)}) collective-permute-start(bf16[320,640]{1,0:T(8,128)(2,1)S(1)} %get-tuple-element.52), channel_id=1, source_target_pairs={{0,2},{1,3},{2,4},{3,5},{4,6},{5,7},{6,0},{7,1},{8,10},{9,11},{10,... | collective-permute-start | bytes 1228808 | tf_op jit(solution)/shard_map/ppermute | solution.py:41
  97.5 13.7 %collective-permute-start.19 = (bf16[320,640]{1,0:T(8,128)(2,1)S(1)}, bf16[320,640]{1,0:T(8,128)(2,1)S(1)}, u32[]{:S(2)}, u32[]{:S(2)}) collective-permute-start(bf16[320,640]{1,0:T(8,128)(2,1)S(1)} %get-tuple-element.51), channel_id=1, source_target_pairs={{0,6},{1,7},{2,0},{3,1},{4,2},{5,3},{6,4},{7,5},{8,14},{9,15},{10,... | collective-permute-start | bytes 1228808 | tf_op jit(solution)/shard_map/ppermute | solution.py:41
  102.6 16.1 %collective-permute-start.16 = (bf16[320,640]{1,0:T(8,128)(2,1)S(1)}, bf16[320,640]{1,0:T(8,128)(2,1)S(1)}, u32[]{:S(2)}, u32[]{:S(2)}) collective-permute-start(bf16[320,640]{1,0:T(8,128)(2,1)S(1)} %get-tuple-element.47), channel_id=1, source_target_pairs={{0,2},{1,3},{2,4},{3,5},{4,6},{5,7},{6,0},{7,1},{8,10},{9,11},{10,... | collective-permute-start | bytes 1228808 | tf_op jit(solution)/shard_map/ppermute | solution.py:41
  104.2 14.5 %collective-permute-start.18 = (bf16[320,640]{1,0:T(8,128)(2,1)S(1)}, bf16[320,640]{1,0:T(8,128)(2,1)S(1)}, u32[]{:S(2)}, u32[]{:S(2)}) collective-permute-start(bf16[320,640]{1,0:T(8,128)(2,1)S(1)} %get-tuple-element.48), channel_id=1, source_target_pairs={{0,6},{1,7},{2,0},{3,1},{4,2},{5,3},{6,4},{7,5},{8,14},{9,15},{10,... | collective-permute-start | bytes 1228808 | tf_op jit(solution)/shard_map/ppermute | solution.py:41
